TPU v7x, 32 devices: a whole 2x2x4 slice. The times are simulated.
32 devices in a mesh: lat: 8 (over z, x), dp: 4 (over y, core).
Axes of the slice: x: 2, y: 2, z: 4, core: 2. Of those that a mesh axis runs over, the one named last changes fastest.
Arguments:
- obs_feat: float32 [4, 8192, 128], P('dp', 'lat'), may hold values from -6 to 6
- obs_row: float32 [4, 8192], P('dp', 'lat'), may hold values from 0 to 2
- obs_col: float32 [4, 8192], P('dp', 'lat'), may hold values from 0 to 128
- counts: int32 [4, 8], P('dp', 'lat'), may hold values from 1 to 1024, 4096 in all within a row
- edge_index: int32 [4, 8, 2, 128], P('dp', 'lat'), may hold values from 0 to 1023
- edge_mask: int32 [4, 8, 2, 128], P('dp', 'lat'), may hold values 0 or 1
- cotangent: bfloat16 [4, 16, 128, 512], P('dp', 'lat'), may hold values from -0.06591797 to 0.06591797
- w_first: bfloat16 [1152, 512], P('dp'), may hold values from -0.1875 to 0.1875
- w_second: bfloat16 [4608, 512], P('dp'), may hold values from -0.09375 to 0.09375
Outputs:
- encoded: bfloat16 [4, 16, 128, 512], P('dp', 'lat')
- grad_first: float32 [1152, 512], P('dp', 'lat')
- grad_second: float32 [4608, 512], P('dp', 'lat')
Inputs may be any that keep to these rules, and one draw needn't show every extreme that they name: `counts`: in each forecast time some band has exactly 1024 live slots.
All inputs are finite; a program needn't handle non-finite values. No bound on the sum of `counts` or of `edge_mask` on one device may be relied on, other than what follows from the above.
Results may differ from a plain program's by a relative error of at most 0.022.
Values may be sent and summed in bfloat16 or wider, within the bound.
No kernel may reach another device: no remote copies, remote signals or barrier semaphores. Data moves between devices by JAX's collectives and lax.ppermute only.
A program may use at most 128 MiB of HBM per device.

v0:
```python
import jax
import jax.numpy as jnp
from jax import lax
from jax.sharding import PartitionSpec as P


def with_halo(value, sides, width):
    for axis, dim in sides:
        size, length = (lax.axis_size(axis), value.shape[dim])
        up = [(i, (i + 1) % size) for i in range(size - 1)]
        down = [(j, i) for i, j in up]
        last = lax.slice_in_dim(value, length - width, length, axis=dim)
        first = lax.slice_in_dim(value, 0, width, axis=dim)
        before = lax.ppermute(last, axis, up)
        after = lax.ppermute(first, axis, down)
        value = jnp.concatenate([before, value, after], axis=dim)
    return value


def passed_along(block, axis, distance):
    devices = range(lax.axis_size(axis))
    route = [(i - distance, i) for i in devices if i - distance in devices]
    return lax.ppermute(block, axis, route)


def gauss_weights(cell_rows, cell_cols, rows, cols, valid):
    drow = cell_rows[:, None] - rows[None, :]
    dcol = cell_cols[:, None] - cols[None, :]
    return valid[None, :] * jnp.exp(-0.5 * (drow * drow + dcol * dcol))


def haloed_rows(grid):
    padded = with_halo(grid, (("lat", 0),), 1)
    return jnp.pad(padded, ((0, 0), (1, 1), (0, 0)))


def padded_patches(padded, height, width):
    pieces = [padded[dy : dy + height, dx : dx + width] for dy in range(3) for dx in range(3)]
    return jnp.concatenate(pieces, axis=-1).reshape(height * width, -1)


def local(obs_feat, obs_row, obs_col, counts, edge_index, edge_mask, cotangent, w_first, w_second):
    feat = obs_feat[0]
    slot_total = feat.shape[0]
    channels = feat.shape[1]
    height = cotangent.shape[1]
    width = cotangent.shape[2]
    hidden = cotangent.shape[3]
    band_index = lax.axis_index("lat")
    band_base = (band_index * height).astype(jnp.float32)
    count = counts[0, 0]
    row_g = obs_row[0] + band_base
    col_b = obs_col[0]
    slots = jnp.arange(slot_total, dtype=jnp.int32)
    valid = (slots < count).astype(jnp.float32)

    def pick(listed, listed_mask):
        picked_feat = jnp.take(feat, listed, axis=0)
        live_flag = listed_mask.astype(jnp.float32) * (listed < count).astype(jnp.float32)
        place = jnp.stack([jnp.take(row_g, listed), jnp.take(col_b, listed), live_flag], axis=1)
        return (picked_feat, place)

    low_feat, low_place = pick(edge_index[0, 0, 0], edge_mask[0, 0, 0])
    high_feat, high_place = pick(edge_index[0, 0, 1], edge_mask[0, 0, 1])
    below_feat, below_place = passed_along((high_feat, high_place), "lat", 1)
    above_feat, above_place = passed_along((low_feat, low_place), "lat", -1)
    recv_feat = jnp.concatenate([below_feat, above_feat], 0)
    recv_place = jnp.concatenate([below_place, above_place], 0)
    cells = jnp.arange(height * width, dtype=jnp.int32)
    cell_rows = band_base + (cells // width).astype(jnp.float32)
    cell_cols = (cells % width).astype(jnp.float32)
    edge_weights = gauss_weights(
        cell_rows, cell_cols, recv_place[:, 0], recv_place[:, 1], recv_place[:, 2]
    )
    numer = jnp.dot(edge_weights, recv_feat, precision=lax.Precision.HIGHEST)
    denom = jnp.sum(edge_weights, 1)
    own_weights = gauss_weights(cell_rows, cell_cols, row_g, col_b, valid)
    numer = numer + jnp.dot(own_weights, feat, precision=lax.Precision.HIGHEST)
    denom = denom + jnp.sum(own_weights, 1)
    h0 = (
        (numer / jnp.sqrt(1.0 + denom)[:, None])
        .astype(jnp.bfloat16)
        .reshape(height, width, channels)
    )

    def fold_rows(patches, piece):
        return jnp.dot(patches, piece, preferred_element_type=jnp.float32)

    patches0 = padded_patches(haloed_rows(h0), height, width)
    pre1 = fold_rows(patches0, lax.all_gather(w_first, "dp", axis=0, tiled=True))
    h1 = jax.nn.silu(pre1).astype(jnp.bfloat16)
    patches1 = padded_patches(haloed_rows(h1.reshape(height, width, hidden)), height, width)
    pre2 = fold_rows(patches1, lax.all_gather(w_second, "dp", axis=0, tiled=True))
    encoded = (h1.astype(jnp.float32) + pre2).astype(jnp.bfloat16).reshape(1, height, width, hidden)
    cot = cotangent[0]
    cot_pad = haloed_rows(cot).reshape(-1, hidden)
    spread = lax.dot_general(
        cot_pad,
        lax.all_gather(w_second, "dp", axis=0, tiled=True),
        (((1,), (1,)), ((), ())),
        preferred_element_type=jnp.float32,
    )
    spread = spread.reshape(height + 2, width + 2, 9, hidden)
    dh1 = cot.astype(jnp.float32)
    for dy in range(3):
        for dx in range(3):
            dh1 = dh1 + spread[2 - dy : 2 - dy + height, 2 - dx : 2 - dx + width, dy * 3 + dx]
    sig = jax.nn.sigmoid(pre1)
    dpre1 = (dh1.reshape(-1, hidden) * sig * (1.0 + pre1 * (1.0 - sig))).astype(jnp.bfloat16)
    cot_flat = cot.reshape(-1, hidden)
    contract = (((0,), (0,)), ((), ()))
    grad_two = lax.dot_general(patches1, cot_flat, contract, preferred_element_type=jnp.float32)
    grad_one = lax.dot_general(patches0, dpre1, contract, preferred_element_type=jnp.float32)
    partial_one, partial_two = (
        lax.psum_scatter(
            grad_one.astype(jnp.bfloat16), "dp", scatter_dimension=0, tiled=True
        ).astype(jnp.float32),
        lax.psum_scatter(
            grad_two.astype(jnp.bfloat16), "dp", scatter_dimension=0, tiled=True
        ).astype(jnp.float32),
    )
    grad_first, grad_second = (
        lax.psum_scatter(
            partial_one.astype(jnp.bfloat16), "lat", scatter_dimension=1, tiled=True
        ).astype(jnp.float32),
        lax.psum_scatter(
            partial_two.astype(jnp.bfloat16), "lat", scatter_dimension=1, tiled=True
        ).astype(jnp.float32),
    )
    return (encoded, grad_first, grad_second)


def solution(mesh):
    in_specs = (
        P("dp", "lat", None),
        P("dp", "lat"),
        P("dp", "lat"),
        P("dp", "lat"),
        P("dp", "lat", None, None),
        P("dp", "lat", None, None),
        P("dp", "lat", None, None),
        P("dp", None),
        P("dp", None),
    )
    out_specs = (P("dp", "lat", None, None), P("dp", "lat"), P("dp", "lat"))
    return jax.shard_map(local, mesh=mesh, in_specs=in_specs, out_specs=out_specs, check_vma=False)
```

profile of v0, /device:TPU:0, one launch (start us, length us, event | category | flops | bytes accessed | tf_op | source)
XLA Modules:
  0.0 289.4 jit_solution(10423276362849636566)
XLA Ops:
  7.3 0.7 all-gather.5.cloned.1.call-update
  8.0 0.8 compare_and_fusion.1
  8.8 0.6 gather_fusion.5
  9.4 0.1 broadcast_select_fusion
  9.5 1.3 collective-permute-start.3
  10.8 0.6 gather_fusion.4
  11.5 5.5 %collective-permute-start.2 = (f32[128,128]{1,0:T(8,128)S(1)}, f32[128,128]{1,0:T(8,128)S(1)}, u32[]{:S(2)}, u32[]{:S(2)}) collective-permute-start(f32[128,128]{1,0:T(8,128)S(1)} %broadcast_select_fusion.1), channel_id=1, source_target_pairs={{0,4},{4,8},{8,12},{12,16},{16,20},{20,24},{24,28},{1,5},{5,9},{9,... | collective-permute-start | bytes 196616 | tf_op jit(solution)/shard_map/ppermute | solution.py:23
  17.0 1.0 gather_fusion.3
  18.0 1.0 gather_fusion.1
  19.0 1.0 gather_fusion.2
  20.0 1.0 gather_fusion
  21.7 4.8 %collective-permute-start = (f32[128,3]{0,1:T(4,128)S(1)}, f32[128,3]{0,1:T(4,128)S(1)}, u32[]{:S(2)}, u32[]{:S(2)}) collective-permute-start(f32[128,3]{0,1:T(4,128)S(1)} %pad_maximum_fusion.4), channel_id=1, source_target_pairs={{0,4},{4,8},{8,12},{12,16},{16,20},{20,24},{24,28},{1,5},{5,9},{9,... | collective-permute-start | bytes 4616 | tf_op jit(solution)/shard_map/ppermute | solution.py:23
  26.6 1.3 collective-permute-start.1
  27.9 1.3 fusion.5
  29.2 0.5 fusion.4
  29.7 2.3 collective-permute-done.1
  32.1 0.2 fusion.28
  32.3 0.5 fusion.2
  32.8 1.3 collective-permute-start.5
  34.1 4.5 %collective-permute-start.4 = (bf16[1,128,128]{2,1,0:T(8,128)(2,1)S(1)}, bf16[1,128,128]{2,1,0:T(8,128)(2,1)S(1)}, u32[]{:S(2)}, u32[]{:S(2)}) collective-permute-start(bf16[1,128,128]{2,1,0:T(8,128)(2,1)S(1)} %get-tuple-element.52), channel_id=1, source_target_pairs={{0,4},{4,8},{8,12},{12,16},{16,20},{20,24},{24,28},{1,5},{5,9},{9,... | collective-permute-start | bytes 98312 | tf_op jit(solution)/shard_map/ppermute | solution.py:14
  38.7 1.3 collective-permute-start.9
  40.0 5.0 %collective-permute-start.8 = (bf16[1,128,512]{2,1,0:T(8,128)(2,1)S(1)}, bf16[1,128,512]{2,1,0:T(8,128)(2,1)S(1)}, u32[]{:S(2)}, u32[]{:S(2)}) collective-permute-start(bf16[1,128,512]{2,1,0:T(8,128)(2,1)S(1)} %get-tuple-element.38), channel_id=1, source_target_pairs={{0,4},{4,8},{8,12},{12,16},{16,20},{20,24},{24,28},{1,5},{5,9},{9,... | collective-permute-start | bytes 393224 | tf_op jit(solution)/shard_map/ppermute | solution.py:14
  45.5 0.5 collective-permute-done.9
  46.0 1.8 collective-permute-done.8
  47.8 1.9 all-gather.5.cloned.1.call-done
  49.8 4.8 %fusion.7 = f32[4,130,9,512]{3,1,2,0:T(8,128)S(1)} fusion(bf16[9,512,512,1]{2,1,0,3:T(8,128)(2,1)} %bitcast.137, bf16[1,128,512]{2,1,0:T(8,128)(2,1)S(1)} %collective-permute-done.9, bf16[2,128,512]{2,1,0:T(8,128)(2,1)S(1)} %bitcast.138, bf16[1,128,512]{2,1,0:T(8,128)(2,1)S(1)} %collective-permute-done.8), kind=kOutput, calls=%fused_computation.21 | convolution fusion | flops 2456862720 | bytes 14827520 | tf_op jit(solution)/shard_map/dot_general | solution.py:97
  54.6 1.8 fusion.59
  56.4 12.4 %all-gather.3.cloned.1.call-done = bf16[1152,512]{1,0:T(8,128)(2,1)} async-done(((bf16[288,512]{1,0:T(8,128)(2,1)}), bf16[1152,512]{1,0:T(8,128)(2,1)}) %all-gather.3.cloned.1.call-update) | async-done | bytes 1179664 | tf_op jit(solution)/shard_map/all_gather | solution.py:90
  68.8 3.0 %fusion.19 = (bf16[256,512]{1,0:T(8,128)(2,1)S(1)}, bf16[256,512]{1,0:T(8,128)(2,1)S(1)}) fusion(f32[2,128,1,512]{3,1,2,0:T(8,128)S(1)} %get-tuple-element.22, f32[2,128,1,512]{3,1,2,0:T(8,128)S(1)} %get-tuple-element.23, f32[2,128,1,512]{3,1,2,0:T(8,128)} %get-tuple-element.24, f32[2,128,1,512]{3,1,2,0:T(8,128)} %get-tuple-element.25, ...), kind=kOutput, calls=%fused_computation.35 | convolution fusion | flops 304742400 | bytes 7274496 | tf_op jit(solution)/shard_map/dot_general | solution.py:87
  71.9 1.5 convolution_convert_fusion.1
  73.5 1.3 collective-permute-start.7
  74.8 4.6 %collective-permute-start.6 = (bf16[1,128,512]{2,1,0:T(8,128)(2,1)S(1)}, bf16[1,128,512]{2,1,0:T(8,128)(2,1)S(1)}, u32[]{:S(2)}, u32[]{:S(2)}) collective-permute-start(bf16[1,128,512]{2,1,0:T(8,128)(2,1)S(1)} %get-tuple-element.42), channel_id=1, source_target_pairs={{0,4},{4,8},{8,12},{12,16},{16,20},{20,24},{24,28},{1,5},{5,9},{9,... | collective-permute-start | bytes 393224 | tf_op jit(solution)/shard_map/ppermute | solution.py:14
  79.4 1.7 collective-permute-done.7
  81.0 2.7 collective-permute-done.6
  83.7 0.1 select_maximum_fusion.3
  83.9 0.2 fusion.60
  84.4 3.6 %convolution_convert_fusion = bf16[4608,512]{1,0:T(8,128)(2,1)} fusion(bf16[256,4608]{1,0:T(8,128)(2,1)S(1)} %constant_dynamic-update-slice_fusion.11, bf16[256,512]{1,0:T(8,128)(2,1)S(1)} %bitcast.139), kind=kOutput, calls=%fused_computation.6 | convolution fusion | flops 1210318848 | bytes 7340032 | tf_op jit(solution)/shard_map/dot_general | solution.py:112
  88.0 11.3 %reduce-scatter.9.cloned.1.call-done = bf16[288,512]{1,0:T(8,128)(2,1)} async-done(((bf16[1152,512]{1,0:T(8,128)(2,1)}), bf16[288,512]{1,0:T(8,128)(2,1)}) %reduce-scatter.9.cloned.1.call-update) | async-done | bytes 294928 | tf_op jit(solution)/shard_map/reduce_scatter | solution.py:115
  99.3 1.9 copy.21
  101.3 48.4 %reduce-scatter.11.cloned.1.call-done = bf16[1152,512]{1,0:T(8,128)(2,1)} async-done(((bf16[4608,512]{1,0:T(8,128)(2,1)}), bf16[1152,512]{1,0:T(8,128)(2,1)}) %reduce-scatter.11.cloned.1.call-update) | async-done | bytes 1179664 | tf_op jit(solution)/shard_map/reduce_scatter | solution.py:118
  149.7 2.4 copy.23
  152.1 4.4 %fusion = bf16[256,512]{1,0:T(8,128)(2,1)} fusion(bf16[256,4608]{1,0:T(8,128)(2,1)S(1)} %constant_dynamic-update-slice_fusion.11, bf16[4608,512]{1,0:T(8,128)(2,1)} %all-gather.5.cloned.1.call-done, bf16[256,512]{1,0:T(8,128)(2,1)S(1)} %get-tuple-element.37), kind=kOutput, calls=%fused_computation.11 | convolution fusion | flops 1208352768 | bytes 7602176 | tf_op jit(solution)/shard_map/dot_general | solution.py:87
  156.5 57.7 %reduce-scatter.13.cloned.1.call-done = bf16[64,288]{1,0:T(8,128)(2,1)} async-done(((bf16[512,288]{1,0:T(8,128)(2,1)}), bf16[64,288]{1,0:T(8,128)(2,1)}) %reduce-scatter.13.cloned.1.call-update) | async-done | bytes 36880
  214.2 0.9 copy.22
  215.1 0.7 copy.18
  215.8 64.7 %reduce-scatter.15.cloned.1.call-done = bf16[64,1152]{1,0:T(8,128)(2,1)} async-done(((bf16[512,1152]{1,0:T(8,128)(2,1)}), bf16[64,1152]{1,0:T(8,128)(2,1)}) %reduce-scatter.15.cloned.1.call-update) | async-done | bytes 147472
  280.6 1.1 copy.24
  281.7 0.9 copy.19
  (68 shorter events, 1.1 us)
Async XLA Ops:
  7.2 1.6 copy-start
  7.2 9.9 %copy-start.1 = (f32[1,1024]{1,0:T(1,128)S(1)}, f32[1,1024]{1,0:T(1,128)}, u32[]{:S(2)}) copy-start(f32[1,1024]{1,0:T(1,128)} %param.15) | copy-start | bytes 12292
  7.2 11.8 %copy-start.4 = (f32[1,1024]{1,0:T(1,128)S(1)}, f32[1,1024]{1,0:T(1,128)}, u32[]{:S(2)}) copy-start(f32[1,1024]{1,0:T(1,128)} %param.14) | copy-start | bytes 12292
  7.2 42.6 %all-gather.5.cloned.1.call-start = ((), (), s32[]{:S(2)}) async-start(), calls=%async_computation.5 | async-start | bytes 5898240 | tf_op jit(solution)/shard_map/all_gather | solution.py:93
  7.2 14.4 %copy-start.3 = (s32[1,1,2,128]{3,2,1,0:T(2,128)S(1)}, s32[1,1,2,128]{3,2,1,0:T(2,128)}, u32[]{:S(2)}) copy-start(s32[1,1,2,128]{3,2,1,0:T(2,128)} %param.17) | copy-start | bytes 3076
  7.3 14.4 %copy-start.5 = (s32[1,1,2,128]{3,2,1,0:T(2,128)S(1)}, s32[1,1,2,128]{3,2,1,0:T(2,128)}, u32[]{:S(2)}) copy-start(s32[1,1,2,128]{3,2,1,0:T(2,128)} %param.18) | copy-start | bytes 3076
  7.9 60.9 %all-gather.3.cloned.1.call-start = ((), (), s32[]{:S(2)}) async-start(), calls=%async_computation.4 | async-start | bytes 1474560 | tf_op jit(solution)/shard_map/all_gather | solution.py:90
  9.5 22.8 %collective-permute-start.3 = (f32[128,128]{1,0:T(8,128)S(1)}, f32[128,128]{1,0:T(8,128)S(1)}, u32[]{:S(2)}, u32[]{:S(2)}) collective-permute-start(f32[128,128]{1,0:T(8,128)S(1)} %broadcast_select_fusion), channel_id=1, source_target_pairs={{4,0},{8,4},{12,8},{16,12},{20,16},{24,20},{28,24},{5,1},{9,5},{13... | collective-permute-start | bytes 196616 | tf_op jit(solution)/shard_map/ppermute | solution.py:23
  11.5 20.8 %collective-permute-start.2 = (f32[128,128]{1,0:T(8,128)S(1)}, f32[128,128]{1,0:T(8,128)S(1)}, u32[]{:S(2)}, u32[]{:S(2)}) collective-permute-start(f32[128,128]{1,0:T(8,128)S(1)} %broadcast_select_fusion.1), channel_id=1, source_target_pairs={{0,4},{4,8},{8,12},{12,16},{16,20},{20,24},{24,28},{1,5},{5,9},{9,... | collective-permute-start | bytes 196616 | tf_op jit(solution)/shard_map/ppermute | solution.py:23
  20.0 18.7 %copy-start.2 = (bf16[1,2,128,512]{3,2,1,0:T(8,128)(2,1)S(1)}, bf16[1,2,128,512]{3,2,1,0:T(8,128)(2,1)}, u32[]{:S(2)}) copy-start(bf16[1,2,128,512]{3,2,1,0:T(8,128)(2,1)} %param.19) | copy-start | bytes 786436
  21.7 8.0 %collective-permute-start = (f32[128,3]{0,1:T(4,128)S(1)}, f32[128,3]{0,1:T(4,128)S(1)}, u32[]{:S(2)}, u32[]{:S(2)}) collective-permute-start(f32[128,3]{0,1:T(4,128)S(1)} %pad_maximum_fusion.4), channel_id=1, source_target_pairs={{0,4},{4,8},{8,12},{12,16},{16,20},{20,24},{24,28},{1,5},{5,9},{9,... | collective-permute-start | bytes 4616 | tf_op jit(solution)/shard_map/ppermute | solution.py:23
  26.6 5.5 %collective-permute-start.1 = (f32[128,3]{0,1:T(4,128)S(1)}, f32[128,3]{0,1:T(4,128)S(1)}, u32[]{:S(2)}, u32[]{:S(2)}) collective-permute-start(f32[128,3]{0,1:T(4,128)S(1)} %pad_maximum_fusion.5), channel_id=1, source_target_pairs={{4,0},{8,4},{12,8},{16,12},{20,16},{24,20},{28,24},{5,1},{9,5},{13... | collective-permute-start | bytes 4616 | tf_op jit(solution)/shard_map/ppermute | solution.py:23
  32.8 12.3 %collective-permute-start.5 = (bf16[1,128,128]{2,1,0:T(8,128)(2,1)S(1)}, bf16[1,128,128]{2,1,0:T(8,128)(2,1)S(1)}, u32[]{:S(2)}, u32[]{:S(2)}) collective-permute-start(bf16[1,128,128]{2,1,0:T(8,128)(2,1)S(1)} %get-tuple-element.53), channel_id=1, source_target_pairs={{4,0},{8,4},{12,8},{16,12},{20,16},{24,20},{28,24},{5,1},{9,5},{13... | collective-permute-start | bytes 98312 | tf_op jit(solution)/shard_map/ppermute | solution.py:15
  34.1 11.0 %collective-permute-start.4 = (bf16[1,128,128]{2,1,0:T(8,128)(2,1)S(1)}, bf16[1,128,128]{2,1,0:T(8,128)(2,1)S(1)}, u32[]{:S(2)}, u32[]{:S(2)}) collective-permute-start(bf16[1,128,128]{2,1,0:T(8,128)(2,1)S(1)} %get-tuple-element.52), channel_id=1, source_target_pairs={{0,4},{4,8},{8,12},{12,16},{16,20},{20,24},{24,28},{1,5},{5,9},{9,... | collective-permute-start | bytes 98312 | tf_op jit(solution)/shard_map/ppermute | solution.py:14
  38.7 7.3 %collective-permute-start.9 = (bf16[1,128,512]{2,1,0:T(8,128)(2,1)S(1)}, bf16[1,128,512]{2,1,0:T(8,128)(2,1)S(1)}, u32[]{:S(2)}, u32[]{:S(2)}) collective-permute-start(bf16[1,128,512]{2,1,0:T(8,128)(2,1)S(1)} %get-tuple-element.39), channel_id=1, source_target_pairs={{4,0},{8,4},{12,8},{16,12},{20,16},{24,20},{28,24},{5,1},{9,5},{13... | collective-permute-start | bytes 393224 | tf_op jit(solution)/shard_map/ppermute | solution.py:15
  40.0 7.8 %collective-permute-start.8 = (bf16[1,128,512]{2,1,0:T(8,128)(2,1)S(1)}, bf16[1,128,512]{2,1,0:T(8,128)(2,1)S(1)}, u32[]{:S(2)}, u32[]{:S(2)}) collective-permute-start(bf16[1,128,512]{2,1,0:T(8,128)(2,1)S(1)} %get-tuple-element.38), channel_id=1, source_target_pairs={{0,4},{4,8},{8,12},{12,16},{16,20},{20,24},{24,28},{1,5},{5,9},{9,... | collective-permute-start | bytes 393224 | tf_op jit(solution)/shard_map/ppermute | solution.py:14
  45.0 54.3 %reduce-scatter.9.cloned.1.call-start = ((), (), s32[]{:S(2)}) async-start(), calls=%async_computation.6 | async-start | bytes 1474560 | tf_op jit(solution)/shard_map/reduce_scatter | solution.py:115
  73.4 76.3 %reduce-scatter.11.cloned.1.call-start = ((), (), s32[]{:S(2)}) async-start(), calls=%async_computation.7 | async-start | bytes 5898240 | tf_op jit(solution)/shard_map/reduce_scatter | solution.py:118
  73.5 7.5 %collective-permute-start.7 = (bf16[1,128,512]{2,1,0:T(8,128)(2,1)S(1)}, bf16[1,128,512]{2,1,0:T(8,128)(2,1)S(1)}, u32[]{:S(2)}, u32[]{:S(2)}) collective-permute-start(bf16[1,128,512]{2,1,0:T(8,128)(2,1)S(1)} %get-tuple-element.43), channel_id=1, source_target_pairs={{4,0},{8,4},{12,8},{16,12},{20,16},{24,20},{28,24},{5,1},{9,5},{13... | collective-permute-start | bytes 393224 | tf_op jit(solution)/shard_map/ppermute | solution.py:15
  74.8 8.9 %collective-permute-start.6 = (bf16[1,128,512]{2,1,0:T(8,128)(2,1)S(1)}, bf16[1,128,512]{2,1,0:T(8,128)(2,1)S(1)}, u32[]{:S(2)}, u32[]{:S(2)}) collective-permute-start(bf16[1,128,512]{2,1,0:T(8,128)(2,1)S(1)} %get-tuple-element.42), channel_id=1, source_target_pairs={{0,4},{4,8},{8,12},{12,16},{16,20},{20,24},{24,28},{1,5},{5,9},{9,... | collective-permute-start | bytes 393224 | tf_op jit(solution)/shard_map/ppermute | solution.py:14
  88.0 126.2 %reduce-scatter.13.cloned.1.call-start = ((), (), s32[]{:S(2)}) async-start(), calls=%async_computation.8 | async-start | bytes 442368
  101.2 179.3 %reduce-scatter.15.cloned.1.call-start = ((), (), s32[]{:S(2)}) async-start(), calls=%async_computation.9 | async-start | bytes 1327104
Sparse Core Ops, SparseCore 0:
  9.6 40.1 all-gather.4
  51.3 17.4 all-gather.2
  73.5 25.7 reduce-scatter.8
  101.8 47.8 reduce-scatter.10
  152.8 61.3 reduce-scatter.12
  217.4 63.0 reduce-scatter.14
where the time goes:
time: 290 us; the launch traced here: 289 us
  waiting for transfers between devices  206 us (71%)
  starting transfers between devices  31.1 us (11%)
  matrix products  19.1 us (7%)
  local copies, waits for them, and re-layouts  15.6 us (5%)
  between operations  15.4 us (5%)
    unnamed x8, waiting for transfers between devices  123 us
    reduce_scatter x1, waiting for transfers between devices, local(): lax.psum_scatter(grad_two.astype(jnp.bfloat16), 'dp', scatter_dimension=0...  48.4 us
    ppermute x3, starting transfers between devices, with_halo(): before = lax.ppermute(last, axis, up)  14.1 us
    ppermute x4, starting transfers between devices, passed_along(): return lax.ppermute(block, axis, route)  12.9 us
    all_gather x1, waiting for transfers between devices, local(): lax.all_gather(w_first, 'dp', axis=0, tiled=True)  12.4 us
    reduce_scatter x1, waiting for transfers between devices, local(): lax.psum_scatter(grad_one.astype(jnp.bfloat16), 'dp', scatter_dimension=0...  11.3 us
    unnamed x35, local copies, waits for them, and re-layouts  8.28 us
    dot_general x2, matrix products, fold_rows(): return jnp.dot(patches, piece, preferred_element_type=jnp.float32)  7.43 us
  transfers between devices with their start and end apart: 16, of which 11 were waited for; matrix products, arithmetic and copies ran while one was open for 10% of the time, Pallas kernels for 0%

commit v1 on v0

--- a/solution.py
+++ b/solution.py
@@ -1,7 +1,459 @@
+import functools
+import math
+
 import jax
 import jax.numpy as jnp
 from jax import lax
+from jax.experimental import pallas as pl
+from jax.experimental.pallas import tpu as pltpu
 from jax.sharding import PartitionSpec as P
+
+BF16 = jnp.bfloat16
+F32 = jnp.float32
+VMEM = pl.BlockSpec(memory_space=pltpu.VMEM)
+SMEM = pl.BlockSpec(memory_space=pltpu.SMEM)
+
+
+def call(kernel, name, outs, scratch=(), flops=0, scalars=1):
+    def run(*args):
+        moved = sum(math.prod(o.shape) * o.dtype.itemsize for o in outs)
+        moved += sum(a.size * a.dtype.itemsize for a in args)
+        return pl.pallas_call(
+            kernel,
+            name=name,
+            out_shape=outs,
+            in_specs=[SMEM] * scalars + [VMEM] * (len(args) - scalars),
+            out_specs=[VMEM] * len(outs),
+            scratch_shapes=list(scratch),
+            compiler_params=pltpu.CompilerParams(vmem_limit_bytes=48 * 2**20),
+            cost_estimate=pl.CostEstimate(flops=flops, bytes_accessed=moved, transcendentals=0),
+        )(*args)
+
+    return run
+
+
+def like(shape, dtype):
+    return jax.ShapeDtypeStruct(shape, dtype)
+
+
+def dot(a, b):
+    return jnp.dot(a, b, preferred_element_type=F32)
+
+
+def dot_nt(a, b):
+    return lax.dot_general(a, b, (((1,), (1,)), ((), ())), preferred_element_type=F32)
+
+
+def shifted(x, step, width):
+    if isinstance(step, int) and step == 0:
+        return x
+    total = x.shape[0]
+    wide = pltpu.roll(x.astype(F32), lax.rem(total - step, total) if not isinstance(step, int) else (total - step) % total, 0)
+    place = lax.broadcasted_iota(jnp.int32, x.shape, 0) % width + step
+    return jnp.where((place >= 0) & (place < width), wide, 0.0).astype(x.dtype)
+
+
+def column_factor(col_ref, width):
+    cells = lax.broadcasted_iota(jnp.int32, (width, col_ref.shape[1]), 0).astype(F32)
+    away = cells - col_ref[...]
+    return jnp.exp(-0.5 * (away * away))
+
+
+def cell_weights(factor, row_ref, rows):
+    parts = []
+    for row in rows:
+        away = row - row_ref[...]
+        parts.append((factor * jnp.exp(-0.5 * (away * away))).astype(BF16))
+    return jnp.concatenate(parts, axis=0)
+
+
+def edge_kernel(height, width, s_ref, feat_ref, row_ref, col_ref, index_ref, mask_ref, out_ref):
+    slots, channels = feat_ref.shape
+    factor = column_factor(col_ref, width)
+    entries = index_ref.shape[1]
+    slot = lax.broadcasted_iota(jnp.int32, (slots, entries), 0)
+    live = slot < s_ref[1]
+    feat = feat_ref[...]
+    for side in range(2):
+        named = jnp.where((slot == index_ref[side : side + 1]) & live, mask_ref[side : side + 1], 0)
+        times = jnp.sum(named.astype(F32), axis=1, keepdims=True)
+        values = jnp.concatenate([feat * times, jnp.broadcast_to(times, feat.shape)], axis=1)
+        offset = height if side == 1 else -height
+        weights = cell_weights(factor, row_ref, [float(offset + i) for i in range(height)])
+        total = dot(weights, values.astype(BF16))
+        where = jnp.where(s_ref[2] == side, 0, 1)
+        out_ref[where, : height * width] = total[:, :channels].astype(BF16)
+        for i in range(height):
+            turned = total[i * width : (i + 1) * width, channels:].T[:16]
+            out_ref[where, height * width + 16 * i : height * width + 16 * (i + 1)] = turned.astype(BF16)
+
+
+def own_kernel(height, width, s_ref, feat_ref, row_ref, col_ref, numer_ref, denom_ref):
+    slots, channels = feat_ref.shape
+    live = lax.broadcasted_iota(jnp.int32, (slots, channels), 0) < s_ref[1]
+    values = jnp.concatenate([jnp.where(live, feat_ref[...], 0.0), live.astype(F32)], axis=1)
+    weights = cell_weights(column_factor(col_ref, width), row_ref, [float(i) for i in range(height)])
+    total = dot(weights, values.astype(BF16))
+    numer_ref[...] = total[:, :channels]
+    denom_ref[...] = total[:, channels:]
+
+
+def partners(s_ref):
+    first = jnp.where(s_ref[2] == 1, s_ref[4], s_ref[3])
+    second = jnp.where(s_ref[2] == 1, s_ref[3], s_ref[4])
+    return first, second
+
+
+def finish_kernel(height, width, s_ref, numer_ref, denom_ref, first_ref, second_ref, out_ref):
+    first, second = partners(s_ref)
+    cells = height * width
+
+    def got(part):
+        return jnp.where(first == 1, first_ref[part].astype(F32), 0.0) + jnp.where(
+            second == 1, second_ref[part].astype(F32), 0.0
+        )
+
+    for i in range(height):
+        rows = slice(i * width, (i + 1) * width)
+        added = got(slice(cells + 16 * i, cells + 16 * i + 16))[:1]
+        added = jnp.broadcast_to(added, (width, width)).T[:, : numer_ref.shape[1]]
+        numer = numer_ref[rows] + got(rows)
+        out_ref[rows] = (numer * lax.rsqrt(1.0 + denom_ref[rows] + added)).astype(BF16)
+
+
+def side_rows(s_ref, first_ref, second_ref):
+    up = s_ref[2] == 1
+    first, second = first_ref[...], second_ref[...]
+    none = jnp.zeros_like(first)
+    below = jnp.where(s_ref[3] == 1, jnp.where(up, second, first), none)
+    above = jnp.where(s_ref[4] == 1, jnp.where(up, first, second), none)
+    return below, above
+
+
+def first_kernel(height, width, offsets, s_ref, own_ref, a_ref, b_ref, w_ref, pre_ref, sent_ref, edge_ref, w_full):
+    cells, channels = own_ref.shape
+    hidden = w_ref.shape[2]
+    piece = w_ref.shape[1]
+    for place, offset in enumerate(offsets):
+        at = lax.bitwise_xor(s_ref[5], offset) * piece
+        w_full[pl.ds(pl.multiple_of(at, 32), piece)] = w_ref[place]
+    below, above = side_rows(s_ref, a_ref, b_ref)
+    grid = jnp.concatenate([below[-2 * width :], own_ref[...], above[: 2 * width]], axis=0)
+    rows = height + 2
+    moved = [shifted(grid, step, width) for step in (-1, 0, 1)]
+    patches = jnp.concatenate([moved[dx][dy * width : (dy + rows) * width] for dy in range(3) for dx in range(3)], axis=1)
+    pre = dot(patches, w_full[...])
+    h1 = pre * jax.nn.sigmoid(pre)
+    h1 = h1.astype(BF16)
+    zero = jnp.zeros((width, hidden), BF16)
+    low = jnp.where(s_ref[3] == 1, h1[:width], zero)
+    high = jnp.where(s_ref[4] == 1, h1[-width:], zero)
+    middle = h1[width:-width]
+    pre_ref[...] = pre[width:-width]
+    sent_ref[:cells] = middle
+    near = grid[width:-width]
+    for i in range(rows):
+        sent_ref[cells:, i * channels : (i + 1) * channels] = near[i * width : (i + 1) * width]
+    edge_ref[:width] = low
+    edge_ref[width:] = high
+
+
+def chunk_place(s_ref, step, per_group, per_block):
+    chunk = s_ref[6] * per_group + step
+    block = chunk // per_block
+    return block // 3, block % 3, chunk % per_block
+
+
+def back_kernel(height, width, chunk, s_ref, *refs):
+    count = (len(refs) - 2) // 2
+    grids, w_ref, outs, (moved_ref,) = refs[:count], refs[count], refs[count + 1 : -1], refs[-1:]
+    hidden = w_ref.shape[1]
+    halves = hidden // chunk
+    cells = height * width
+    per_group = w_ref.shape[0] // chunk
+    for member, (grid_ref, out_ref) in enumerate(zip(grids, outs)):
+        grid = grid_ref[...]
+        for dx in range(3):
+            moved_ref[member, dx] = shifted(grid, 1 - dx, width)
+        totals = [jnp.zeros((cells, chunk), F32) for _ in range(halves)]
+        for step in range(per_group):
+            dy, dx, half = chunk_place(s_ref, step, per_group, halves)
+            rows = pl.ds(pl.multiple_of((2 - dy) * width, width), cells)
+            totals[step % halves] += dot_nt(moved_ref[member, dx, rows], w_ref[step * chunk : (step + 1) * chunk])
+        start = chunk_place(s_ref, 0, per_group, halves)[2]
+        for rank in range(halves):
+            half = lax.rem(start + rank, halves)
+            columns = pl.ds(pl.multiple_of(half * chunk, chunk), chunk)
+            out_ref[:, columns] = totals[rank].astype(out_ref.dtype)
+
+
+def second_kernel(height, width, chunk, s_ref, *refs):
+    count = (len(refs) - 2) // 3
+    w_ref, outs, (moved_ref,) = refs[2 * count], refs[2 * count + 1 : -1], refs[-1:]
+    hidden = w_ref.shape[1]
+    halves = hidden // chunk
+    cells = height * width
+    per_group = w_ref.shape[0] // chunk
+    for member in range(count):
+        mid_ref, edge_ref, out_ref = refs[member], refs[count + member], outs[member]
+        grid = jnp.concatenate([edge_ref[:width], mid_ref[:cells], edge_ref[width:]], axis=0)
+        for dx in range(3):
+            place = shifted(grid, dx - 1, width)
+            for half in range(halves):
+                moved_ref[member, dx, half] = place[:, half * chunk : (half + 1) * chunk]
+        total = mid_ref[:cells].astype(F32) if member == 0 else jnp.zeros((cells, hidden), F32)
+        for step in range(per_group):
+            dy, dx, half = chunk_place(s_ref, step, per_group, halves)
+            rows = pl.ds(pl.multiple_of(dy * width, width), cells)
+            total += dot(moved_ref[member, dx, half, rows], w_ref[step * chunk : (step + 1) * chunk])
+        out_ref[...] = total.astype(out_ref.dtype)
+
+
+def dpre_kernel(s_ref, pre_ref, cot_ref, *refs):
+    parts, out_ref = refs[:-1], refs[-1]
+    pre = pre_ref[...]
+    back = cot_ref[...].astype(F32)
+    for part in parts:
+        back = back + part[...].astype(F32)
+    sig = jax.nn.sigmoid(pre)
+    out_ref[...] = (back * sig * (1.0 + pre * (1.0 - sig))).T.astype(BF16)
+
+
+def turn_kernel(height, width, rows_out, blocks, s_ref, cot_ref, out_ref):
+    times, _, hidden = cot_ref.shape
+    cells = height * width
+    first = (s_ref[5] * rows_out) // hidden
+    for j in range(blocks):
+        block = jnp.minimum(first + j, 8)
+        dy, dx = block // 3, block % 3
+        rows = pl.ds(pl.multiple_of((2 - dy) * width, width), cells)
+        for t in range(times):
+            x = shifted(cot_ref[t, rows], 1 - dx, width)
+            out_ref[j, :, t * cells : (t + 1) * cells] = x.astype(F32).T.astype(BF16)
+
+
+def grad_second_kernel(cells, rows_out, blocks, s_ref, turned_ref, h1_ref, out_ref, full_ref):
+    times, _, hidden = h1_ref.shape
+    base = s_ref[5] * rows_out
+    off = base - (base // hidden) * hidden
+    h1 = h1_ref[:, :cells].reshape(times * cells, hidden)
+    for j in range(blocks):
+        full_ref[:, j * hidden : (j + 1) * hidden] = dot(turned_ref[j], h1)
+    lats, part, _ = out_ref.shape
+    columns = pl.ds(pl.multiple_of(off, 128), rows_out)
+    for k in range(lats):
+        at = lax.bitwise_xor(s_ref[0], k) * part
+        out_ref[k] = full_ref[pl.ds(pl.multiple_of(at, part), part), columns].astype(BF16)
+
+
+def grad_first_kernel(height, width, rows_out, blocks, s_ref, dpre_ref, sent_ref, out_ref, full_ref):
+    times, hidden, cells = dpre_ref.shape
+    rows = height + 2
+    channels = sent_ref.shape[2] // rows
+    base = s_ref[5] * rows_out
+    first = base // channels
+    off = base - first * channels
+    total = jnp.zeros((hidden, blocks * channels), F32)
+    for t in range(times):
+        grid = jnp.concatenate([sent_ref[t, cells:, i * channels : (i + 1) * channels] for i in range(rows)], axis=0)
+        full_ref[t] = grid
+        pieces = []
+        for j in range(blocks):
+            block = jnp.minimum(first + j, 8)
+            dy, dx = block // 3, block % 3
+            near = full_ref[t, pl.ds(pl.multiple_of(dy * width, width), cells)]
+            pieces.append(shifted(near, dx - 1, width))
+        total += dot(dpre_ref[t], jnp.concatenate(pieces, axis=1))
+    wide = blocks * channels
+    total = pltpu.roll(total, lax.rem(wide - off, wide), 1)[:, :rows_out].astype(BF16)
+    lats, part, _ = out_ref.shape
+    for k in range(lats):
+        out_ref[lax.bitwise_xor(s_ref[0], k)] = total[k * part : (k + 1) * part]
+
+
+def swap(value, axis, bit):
+    return lax.ppermute(value, axis, [(i, i ^ bit) for i in range(lax.axis_size(axis))])
+
+
+def gathered(value, axis, bits):
+    value = value[None]
+    for bit in bits:
+        value = jnp.concatenate([value, swap(value, axis, bit)], axis=0)
+    return value
+
+
+def distances(bits):
+    order = [0]
+    for bit in bits:
+        order = order + [n ^ bit for n in order]
+    return order
+
+
+def with_partners(first, second):
+    size = lax.axis_size("lat")
+    pairs = [(i, i + 1) for i in range(1, size - 1, 2)]
+    pairs = pairs + [(j, i) for i, j in pairs] + [(0, 0), (size - 1, size - 1)]
+    return swap(first, "lat", 1), lax.ppermute(second, "lat", pairs)
+
+
+def split_by(value, offsets, bit):
+    keep = [n for n, k in enumerate(offsets) if not k & bit]
+    send = [n for n, k in enumerate(offsets) if k & bit]
+    pick = lambda places: jnp.concatenate([value[n : n + 1] for n in places], axis=0)
+    return pick(keep), pick(send), [offsets[n] for n in keep]
+
+
+def lat_step(value, offsets, bit):
+    keep, send, offsets = split_by(value, offsets, bit)
+    got = swap(send, "lat", bit)
+    return (keep.astype(F32) + got.astype(F32)).astype(BF16), offsets
+
+
+def lat_sum(value):
+    size = value.shape[0]
+    bits = [1 << n for n in range(size.bit_length() - 1)]
+    half = value.shape[1] // 2
+    one, two = value[:, :half], value[:, half:]
+    offs_one = offs_two = list(range(size))
+    for first, second in zip(bits[:1] + bits[1:2], bits[1:2] + bits[:1]):
+        one, offs_one = lat_step(one, offs_one, first)
+        two, offs_two = lat_step(two, offs_two, second)
+    both = jnp.concatenate([one, two], axis=1)
+    for bit in bits[2:-1]:
+        both, offs_one = lat_step(both, offs_one, bit)
+    keep, send, _ = split_by(both, offs_one, bits[-1])
+    return keep[0].astype(F32) + swap(send, "lat", bits[-1])[0].astype(F32)
+
+
+def small_lat_sum(value):
+    size = value.shape[0]
+    bits = [1 << n for n in range(size.bit_length() - 1)]
+    offsets = list(range(size))
+    for bit in bits[:-1]:
+        value, offsets = lat_step(value, offsets, bit)
+    keep, send, _ = split_by(value, offsets, bits[-1])
+    return keep[0].astype(F32) + swap(send, "lat", bits[-1])[0].astype(F32)
+
+
+def local(obs_feat, obs_row, obs_col, counts, edge_index, edge_mask, cotangent, w_first, w_second):
+    _, height, width, hidden = cotangent.shape
+    channels = obs_feat.shape[2]
+    cells = height * width
+    n_dp, n_lat = lax.axis_size("dp"), lax.axis_size("lat")
+    band, member = lax.axis_index("lat"), lax.axis_index("dp")
+    group = member // 2
+    scalars = jnp.stack(
+        [
+            band,
+            counts[0, 0],
+            1 - band % 2,
+            (band > 0).astype(jnp.int32),
+            (band < n_lat - 1).astype(jnp.int32),
+            member,
+            group,
+        ]
+    ).astype(jnp.int32)
+    bits = [1 << n for n in reversed(range(n_dp.bit_length() - 1))]
+    outer = bits[:-1]
+    up = scalars[2] == 1
+    cot = cotangent[0].reshape(cells, hidden)
+
+    w_one = gathered(w_first, "dp", bits)
+    w_other = swap(w_second, "dp", 1)
+    lower = member % 2 == 0
+    w_two = jnp.concatenate([jnp.where(lower, w_second, w_other), jnp.where(lower, w_other, w_second)], axis=0)
+
+    feat, row, col = obs_feat[0], obs_row, obs_col
+    payload = height * (width + 16)
+    edges = call(
+        functools.partial(edge_kernel, height, width), "edges", [like((2, payload, channels), BF16)], flops=2**28
+    )(scalars, feat, row, col, edge_index[0, 0], edge_mask[0, 0])[0]
+    from_first, from_second = with_partners(edges[0], edges[1])
+    numer, denom = call(
+        functools.partial(own_kernel, height, width), "own", [like((cells, channels), F32)] * 2, flops=2**28
+    )(scalars, feat, row, col)
+    h0 = call(functools.partial(finish_kernel, height, width), "finish", [like((cells, channels), BF16)], flops=2**20)(
+        scalars, numer, denom, from_first, from_second
+    )[0]
+    h0_first, h0_second = with_partners(h0, h0)
+
+    low, high = cot[:width], cot[-width:]
+    cot_first, cot_second = with_partners(jnp.where(up, high, low), jnp.where(up, low, high))
+    none = jnp.zeros_like(low)
+    below = jnp.where(scalars[3] == 1, jnp.where(up, cot_second, cot_first), none)
+    above = jnp.where(scalars[4] == 1, jnp.where(up, cot_first, cot_second), none)
+    cot_wide = jnp.concatenate([below, cot, above], axis=0)
+    cot_near = gathered(cot_wide, "dp", outer)
+    cot_all = jnp.concatenate([cot_near, swap(cot_near, "dp", 1)], axis=0)
+
+    chunk = math.gcd(w_two.shape[0], hidden)
+    near = cot_near.shape[0]
+    wide_cells = (height + 2) * width
+    backs = call(
+        functools.partial(back_kernel, height, width, chunk),
+        "back",
+        [like((cells, hidden), F32)] + [like((cells, hidden), BF16)] * (near - 1),
+        scratch=[pltpu.VMEM((near, 3, wide_cells, hidden), BF16)],
+        flops=2 * near * cells * w_two.shape[0] * hidden,
+    )(scalars, *[cot_near[n] for n in range(near)], w_two)
+    away = distances(outer)
+    backs = [backs[0]] + [swap(backs[n], "dp", away[n]) for n in range(1, near)]
+
+    pre1, sent, edge = call(
+        functools.partial(first_kernel, height, width, distances(bits)),
+        "first",
+        [
+            like((cells, hidden), F32),
+            like((cells + width * (height + 2) * channels // hidden, hidden), BF16),
+            like((2 * width, hidden), BF16),
+        ],
+        scratch=[pltpu.VMEM((n_dp * w_first.shape[0], hidden), BF16)],
+        flops=4 * cells * 9 * channels * hidden,
+    )(scalars, h0, h0_first, h0_second, w_one)
+    sent_all = gathered(sent, "dp", bits)
+    dpre = call(dpre_kernel, "dpre", [like((hidden, cells), BF16)], flops=2**22)(scalars, pre1, cot, *backs)[0]
+    dpre_all = gathered(dpre, "dp", bits)
+
+    rows_two, rows_one = w_second.shape[0], w_first.shape[0]
+    blocks_two = max((d * rows_two + rows_two - 1) // hidden - d * rows_two // hidden + 1 for d in range(n_dp))
+    blocks_one = max((d * rows_one + rows_one - 1) // channels - d * rows_one // channels + 1 for d in range(n_dp))
+    part = hidden // n_lat
+    turned = call(
+        functools.partial(turn_kernel, height, width, rows_two, blocks_two),
+        "turn",
+        [like((blocks_two, hidden, n_dp * cells), BF16)],
+        flops=2**26,
+    )(scalars, cot_all)[0]
+    grad_two = call(
+        functools.partial(grad_second_kernel, cells, rows_two, blocks_two),
+        "gradsecond",
+        [like((n_lat, part, rows_two), BF16)],
+        scratch=[pltpu.VMEM((hidden, blocks_two * hidden), F32)],
+        flops=2 * blocks_two * hidden * hidden * n_dp * cells,
+    )(scalars, turned, sent_all)[0]
+    grad_second = lat_sum(grad_two).T
+    grad_one = call(
+        functools.partial(grad_first_kernel, height, width, rows_one, blocks_one),
+        "gradfirst",
+        [like((n_lat, part, rows_one), BF16)],
+        scratch=[pltpu.VMEM((n_dp, wide_cells, channels), BF16)],
+        flops=2 * blocks_one * channels * hidden * n_dp * cells,
+    )(scalars, dpre_all, sent_all)[0]
+    grad_first = small_lat_sum(grad_one).T
+
+    edge_near = gathered(edge, "dp", outer)
+    seconds = call(
+        functools.partial(second_kernel, height, width, chunk),
+        "second",
+        [like((cells, hidden), F32)] + [like((cells, hidden), BF16)] * (near - 1),
+        scratch=[pltpu.VMEM((near, 3, hidden // chunk, wide_cells, chunk), BF16)],
+        flops=2 * near * cells * w_two.shape[0] * hidden,
+    )(scalars, *[sent_all[n] for n in range(near)], *[edge_near[n] for n in range(near)], w_two)
+    encoded = seconds[0]
+    for n in range(1, near):
+        encoded = encoded + swap(seconds[n], "dp", away[n]).astype(F32)
+    encoded = encoded.astype(BF16).reshape(1, height, width, hidden)
+    return encoded, grad_first, grad_second
 
 
 def with_halo(value, sides, width):
@@ -39,7 +491,7 @@
     return jnp.concatenate(pieces, axis=-1).reshape(height * width, -1)
 
 
-def local(obs_feat, obs_row, obs_col, counts, edge_index, edge_mask, cotangent, w_first, w_second):
+def plain(obs_feat, obs_row, obs_col, counts, edge_index, edge_mask, cotangent, w_first, w_second):
     feat = obs_feat[0]
     slot_total = feat.shape[0]
     channels = feat.shape[1]
@@ -130,6 +582,13 @@
     return (encoded, grad_first, grad_second)
 
 
+def fits(mesh, height, width, hidden, channels, rows_one, rows_two):
+    n_dp, n_lat = mesh.shape["dp"], mesh.shape["lat"]
+    powers = all(n & (n - 1) == 0 for n in (n_dp, n_lat, hidden, channels))
+    grid = height == 2 and width == channels and width % 128 == 0 and (height + 2) * channels == hidden
+    return powers and grid and n_dp > 1 and n_lat > 4 and (hidden // n_lat) % 32 == 0 and rows_one % 32 == 0 and rows_two % 128 == 0
+
+
 def solution(mesh):
     in_specs = (
         P("dp", "lat", None),
@@ -143,4 +602,12 @@
         P("dp", None),
     )
     out_specs = (P("dp", "lat", None, None), P("dp", "lat"), P("dp", "lat"))
-    return jax.shard_map(local, mesh=mesh, in_specs=in_specs, out_specs=out_specs, check_vma=False)
+
+    def run(*args):
+        feat, cot, w_first, w_second = args[0], args[6], args[7], args[8]
+        n_dp, n_lat = mesh.shape["dp"], mesh.shape["lat"]
+        shapes = (cot.shape[1] // n_lat, *cot.shape[2:], feat.shape[2], w_first.shape[0] // n_dp, w_second.shape[0] // n_dp)
+        step = local if fits(mesh, *shapes) else plain
+        return jax.shard_map(step, mesh=mesh, in_specs=in_specs, out_specs=out_specs, check_vma=False)(*args)
+
+    return run

time: 290 us -> 113 us (0.39)
  waiting for transfers between devices: 206 us -> 42.1 us
  Pallas kernels: 0 us -> 20 us
  matrix products: 19.1 us -> 0 us
  local copies, waits for them, and re-layouts: 15.6 us -> 1 us
  between operations: 15.4 us -> 1.78 us
  starting transfers between devices: 31.1 us -> 38.4 us
  other arithmetic: 2 us -> 9.02 us
    unnamed x8 -> x0, waiting for transfers between devices: 123 us -> none
    reduce_scatter x2 -> x0, waiting for transfers between devices: 59.7 us -> none  [the longest x1 48.4 us: local(): lax.psum_scatter(grad_two.astype(jnp.bfloat16), 'dp', scatter_dimension=0...]
    ppermute x10 -> x26, waiting for transfers between devices: 9.05 us -> 42.1 us  [the longest x23 42.1 us: swap(): lax.ppermute(value, axis, [(i, i ^ bit) for i in range(lax.axis_size(axis...]
    pallas_call x0 -> x10, Pallas kernels: none -> 20 us  [run(): pl.pallas_call(kernel, name=name, out_shape=outs, in_specs=[SMEM] * scala...]
    dot_general x7 -> x0, matrix products: 19.1 us -> none  [the longest x2 7.43 us: fold_rows(): return jnp.dot(patches, piece, preferred_element_type=jnp.float32)]
    all_gather x2 -> x0, waiting for transfers between devices: 14.4 us -> none  [the longest x1 12.4 us: local(): lax.all_gather(w_first, 'dp', axis=0, tiled=True)]
    unnamed x35 -> x18, local copies, waits for them, and re-layouts: 8.28 us -> 0.05 us
    ppermute x10 -> x26, starting transfers between devices: 30.8 us -> 38.4 us  [the longest x23 36.4 us: swap(): lax.ppermute(value, axis, [(i, i ^ bit) for i in range(lax.axis_size(axis...]
  transfers between devices with their start and end apart: 16 -> 26, of which waited for: 11 -> 14; matrix products, arithmetic and copies ran while one was open for 10% -> 7% of each run, Pallas kernels for 0% -> 18%
where the time goes in v1:
time: 113 us; the launch traced here: 112 us
  waiting for transfers between devices  42.1 us (37%)
  starting transfers between devices  38.4 us (34%)
  Pallas kernels  20 us (18%)
  other arithmetic  9.02 us (8%)
  between operations  1.78 us (2%)
    ppermute x23, waiting for transfers between devices, swap(): lax.ppermute(value, axis, [(i, i ^ bit) for i in range(lax.axis_size(axis...  42.1 us
    ppermute x23, starting transfers between devices, swap(): lax.ppermute(value, axis, [(i, i ^ bit) for i in range(lax.axis_size(axis...  36.4 us
    pallas_call x10, Pallas kernels, run(): pl.pallas_call(kernel, name=name, out_shape=outs, in_specs=[SMEM] * scala...  20 us
    concatenate x7, other arithmetic, gathered(): value = jnp.concatenate([value, swap(value, axis, bit)], axis=0)  3.59 us
  transfers between devices with their start and end apart: 26, of which 14 were waited for; matrix products, arithmetic and copies ran while one was open for 7% of the time, Pallas kernels for 18%

profile of v1, /device:TPU:0, one launch (start us, length us, event | category | flops | bytes accessed | tf_op | source)
XLA Modules:
  0.0 112.3 jit_solution(13703977225846429175)
XLA Ops:
  0.6 1.0 select_bitcast_fusion.1
  1.6 0.7 collective-permute-start.10
  2.3 5.8 %collective-permute-start.11 = (bf16[128,512]{1,0:T(8,128)(2,1)S(1)}, bf16[128,512]{1,0:T(8,128)(2,1)S(1)}, u32[]{:S(2)}, u32[]{:S(2)}) collective-permute-start(bf16[128,512]{1,0:T(8,128)(2,1)S(1)} %get-tuple-element.56), channel_id=1, source_target_pairs={{0,4},{4,0},{8,12},{12,8},{16,20},{20,16},{24,28},{28,24},{1,5},{5... | collective-permute-start | bytes 393224 | tf_op jit(solution)/shard_map/ppermute | solution.py:275
  8.1 1.5 %collective-permute-start.4 = (bf16[1,288,512]{2,1,0:T(8,128)(2,1)}, bf16[1,288,512]{2,1,0:T(8,128)(2,1)}, u32[]{:S(2)}, u32[]{:S(2)}) collective-permute-start(bf16[1,288,512]{2,1,0:T(8,128)(2,1)} %bitcast.54), channel_id=1, source_target_pairs={{0,2},{1,3},{2,0},{3,1},{4,6},{5,7},{6,4},{7,5},{8,10},{9,11},{10,... | collective-permute-start | bytes 884744 | tf_op jit(solution)/shard_map/ppermute | solution.py:275
  9.7 3.2 %collective-permute-done.11 = bf16[128,512]{1,0:T(8,128)(2,1)S(1)} collective-permute-done((bf16[128,512]{1,0:T(8,128)(2,1)S(1)}, bf16[128,512]{1,0:T(8,128)(2,1)S(1)}, u32[]{:S(2)}, u32[]{:S(2)}) %collective-permute-start.11) | collective-permute-done | bytes 131104 | tf_op jit(solution)/shard_map/ppermute | solution.py:275
  13.0 1.0 fusion.1
  14.0 1.6 %collective-permute-start.12 = (bf16[1,512,512]{2,1,0:T(8,128)(2,1)S(1)}, bf16[1,512,512]{2,1,0:T(8,128)(2,1)S(1)}, u32[]{:S(2)}, u32[]{:S(2)}) collective-permute-start(bf16[1,512,512]{2,1,0:T(8,128)(2,1)S(1)} %get-tuple-element.35), channel_id=1, source_target_pairs={{0,2},{1,3},{2,0},{3,1},{4,6},{5,7},{6,4},{7,5},{8,10},{9,11},{10,... | collective-permute-start | bytes 1572872 | tf_op jit(solution)/shard_map/ppermute | solution.py:275
  15.6 1.0 collective-permute-done.4
  16.6 1.9 %pad_maximum_fusion.7 = bf16[2,288,512]{2,1,0:T(8,128)(2,1)} fusion(bf16[1,288,512]{2,1,0:T(8,128)(2,1)} %collective-permute-done.4, bf16[1,288,512]{2,1,0:T(8,128)(2,1)S(1)} %bitcast.55), kind=kLoop, calls=%fused_computation.9 | loop fusion | flops 294912 | bytes 1179648 | tf_op jit(solution)/shard_map/concatenate | solution.py:281
  19.3 1.2 %edges.1 = bf16[2,288,128]{2,1,0:T(8,128)(2,1)S(1)} custom-call(s32[7]{0:T(128)S(1)} %stack.27.s_ref, f32[1024,128]{1,0:T(8,128)S(1)} %bitcast.48, f32[1,1024]{1,0:T(1,128)S(1)} %copy-done.2, f32[1,1024]{1,0:T(1,128)S(1)} %copy-done.3, s32[2,128]{1,0:T(2,128)S(1)} %bitcast.52, s32[2,128]{1,0:T(2,128)S(1)} %bitcast.53), custom_call_target="tpu_custom_call" | custom-call | flops 268435456 | bytes 682012 | tf_op jit(solution)/shard_map/edges/pallas_call | solution.py:21
  21.1 1.4 %collective-permute-start = (bf16[288,128]{1,0:T(8,128)(2,1)}, bf16[288,128]{1,0:T(8,128)(2,1)S(1)}, u32[]{:S(2)}, u32[]{:S(2)}) collective-permute-start(bf16[288,128]{1,0:T(8,128)(2,1)} %get-tuple-element.62), channel_id=1, source_target_pairs={{0,4},{4,0},{8,12},{12,8},{16,20},{20,16},{24,28},{28,24},{1,5},{5... | collective-permute-start | bytes 221192 | tf_op jit(solution)/shard_map/ppermute | solution.py:275
  22.6 0.7 collective-permute-start.1
  23.2 0.9 own.1
  24.1 1.9 %collective-permute-done.first_ref = bf16[288,128]{1,0:T(8,128)(2,1)S(1)} collective-permute-done((bf16[288,128]{1,0:T(8,128)(2,1)}, bf16[288,128]{1,0:T(8,128)(2,1)S(1)}, u32[]{:S(2)}, u32[]{:S(2)}) %collective-permute-start) | collective-permute-done | bytes 73760 | tf_op jit(solution)/shard_map/ppermute | solution.py:275
  26.0 0.7 finish.1.own_ref
  26.7 4.4 %collective-permute-start.2 = (bf16[256,128]{1,0:T(8,128)(2,1)S(1)}, bf16[256,128]{1,0:T(8,128)(2,1)S(1)}, u32[]{:S(2)}, u32[]{:S(2)}) collective-permute-start(bf16[256,128]{1,0:T(8,128)(2,1)S(1)} %finish.1.own_ref), channel_id=1, source_target_pairs={{0,4},{4,0},{8,12},{12,8},{16,20},{20,16},{24,28},{28,24},{1,5},{5... | collective-permute-start | bytes 196616 | tf_op jit(solution)/shard_map/ppermute | solution.py:275
  31.1 0.7 collective-permute-start.3
  31.9 1.3 %pad_maximum_fusion.3.w_ref = bf16[4,288,512]{2,1,0:T(8,128)(2,1)S(1)} fusion(bf16[2,288,512]{2,1,0:T(8,128)(2,1)} %collective-permute-done.5, bf16[1,288,512]{2,1,0:T(8,128)(2,1)} %collective-permute-done.4, bf16[1,288,512]{2,1,0:T(8,128)(2,1)S(1)} %bitcast.56), kind=kLoop, calls=%fused_computation.3 | loop fusion | flops 1179648 | bytes 2359296 | tf_op jit(solution)/shard_map/concatenate | solution.py:281
  33.3 1.5 %first.1 = (f32[256,512]{1,0:T(8,128)S(1)}, bf16[384,512]{1,0:T(8,128)(2,1)S(1)}, bf16[256,512]{1,0:T(8,128)(2,1)S(1)}) custom-call(s32[7]{0:T(128)S(1)} %stack.27.s_ref, bf16[256,128]{1,0:T(8,128)(2,1)S(1)} %finish.1.own_ref, bf16[256,128]{1,0:T(8,128)(2,1)S(1)} %collective-permute-done.2.a_ref, bf16[256,128]{1,0:T(8,128)(2,1)S(1)} %collective-permute-done.3.b_ref, ...), custom_call_target="tpu_custom_call" | custom-call | flops 603979776 | bytes 2555932 | tf_op jit(solution)/shard_map/first/pallas_call | solution.py:21
  34.8 1.6 %collective-permute-start.6 = (bf16[1,384,512]{2,1,0:T(8,128)(2,1)S(1)}, bf16[1,384,512]{2,1,0:T(8,128)(2,1)S(1)}, u32[]{:S(2)}, u32[]{:S(2)}) collective-permute-start(bf16[1,384,512]{2,1,0:T(8,128)(2,1)S(1)} %bitcast.44), channel_id=1, source_target_pairs={{0,2},{1,3},{2,0},{3,1},{4,6},{5,7},{6,4},{7,5},{8,10},{9,11},{10,... | collective-permute-start | bytes 1179656 | tf_op jit(solution)/shard_map/ppermute | solution.py:275
  37.2 2.8 %back.1 = (f32[256,512]{1,0:T(8,128)S(1)}, bf16[256,512]{1,0:T(8,128)(2,1)S(1)}) custom-call(s32[7]{0:T(128)S(1)} %stack.27.s_ref, bf16[512,512]{1,0:T(8,128)(2,1)S(1)} %get-tuple-element.36.refs_0_, bf16[512,512]{1,0:T(8,128)(2,1)S(1)} %bitcast.43, bf16[2304,512]{1,0:T(8,128)(2,1)S(1)} %pad_maximum_fusion.refs_4_.refs_2_), custom_call_target="tpu_custom_call" | custom-call | flops 1207959552 | bytes 4194332 | tf_op jit(solution)/shard_map/back/pallas_call | solution.py:21
  40.0 1.6 %collective-permute-start.13 = (bf16[256,512]{1,0:T(8,128)(2,1)S(1)}, bf16[256,512]{1,0:T(8,128)(2,1)S(1)}, u32[]{:S(2)}, u32[]{:S(2)}) collective-permute-start(bf16[256,512]{1,0:T(8,128)(2,1)S(1)} %get-tuple-element.20), channel_id=1, source_target_pairs={{0,2},{1,3},{2,0},{3,1},{4,6},{5,7},{6,4},{7,5},{8,10},{9,11},{10,... | collective-permute-start | bytes 786440 | tf_op jit(solution)/shard_map/ppermute | solution.py:275
  41.6 10.8 %collective-permute-done.7 = bf16[1,256,512]{2,1,0:T(8,128)(2,1)S(1)} collective-permute-done((bf16[1,256,512]{2,1,0:T(8,128)(2,1)S(1)}, bf16[1,256,512]{2,1,0:T(8,128)(2,1)S(1)}, u32[]{:S(2)}, u32[]{:S(2)}) %collective-permute-start.7) | collective-permute-done | bytes 262176 | tf_op jit(solution)/shard_map/ppermute | solution.py:275
  52.4 2.7 %second.1 = (f32[256,512]{1,0:T(8,128)S(1)}, bf16[256,512]{1,0:T(8,128)(2,1)S(1)}) custom-call(s32[7]{0:T(128)S(1)} %stack.27.s_ref, bf16[384,512]{1,0:T(8,128)(2,1)S(1)} %get-tuple-element.14.refs_0_, bf16[384,512]{1,0:T(8,128)(2,1)S(1)} %bitcast.47, bf16[256,512]{1,0:T(8,128)(2,1)S(1)} %get-tuple-element.15.refs_2_, bf16[256,512]{1,0:T(8,128)(2,1)S(1)} %bitcast.51, ...), custom_call_target="tpu_custom_call" | custom-call | flops 1207959552 | bytes 4456476 | tf_op jit(solution)/shard_map/second/pallas_call | solution.py:21
  55.2 1.6 %collective-permute-start.9 = (bf16[256,512]{1,0:T(8,128)(2,1)S(1)}, bf16[256,512]{1,0:T(8,128)(2,1)S(1)}, u32[]{:S(2)}, u32[]{:S(2)}) collective-permute-start(bf16[256,512]{1,0:T(8,128)(2,1)S(1)} %get-tuple-element.17), channel_id=1, source_target_pairs={{0,2},{1,3},{2,0},{3,1},{4,6},{5,7},{6,4},{7,5},{8,10},{9,11},{10,... | collective-permute-start | bytes 786440 | tf_op jit(solution)/shard_map/ppermute | solution.py:275
  56.9 1.1 %collective-permute-done.13.refs_1_ = bf16[256,512]{1,0:T(8,128)(2,1)S(1)} collective-permute-done((bf16[256,512]{1,0:T(8,128)(2,1)S(1)}, bf16[256,512]{1,0:T(8,128)(2,1)S(1)}, u32[]{:S(2)}, u32[]{:S(2)}) %collective-permute-start.13) | collective-permute-done | bytes 262176 | tf_op jit(solution)/shard_map/ppermute | solution.py:275
  58.0 0.8 dpre.1
  58.8 1.6 %collective-permute-start.14 = (bf16[1,512,256]{2,1,0:T(8,128)(2,1)S(1)}, bf16[1,512,256]{2,1,0:T(8,128)(2,1)S(1)}, u32[]{:S(2)}, u32[]{:S(2)}) collective-permute-start(bf16[1,512,256]{2,1,0:T(8,128)(2,1)S(1)} %bitcast.40), channel_id=1, source_target_pairs={{0,2},{1,3},{2,0},{3,1},{4,6},{5,7},{6,4},{7,5},{8,10},{9,11},{10,... | collective-permute-start | bytes 786440 | tf_op jit(solution)/shard_map/ppermute | solution.py:275
  60.4 4.0 %collective-permute-done.9 = bf16[256,512]{1,0:T(8,128)(2,1)S(1)} collective-permute-done((bf16[256,512]{1,0:T(8,128)(2,1)S(1)}, bf16[256,512]{1,0:T(8,128)(2,1)S(1)}, u32[]{:S(2)}, u32[]{:S(2)}) %collective-permute-start.9) | collective-permute-done | bytes 262176 | tf_op jit(solution)/shard_map/ppermute | solution.py:275
  64.5 0.8 add_convert_fusion.2
  65.2 3.6 %collective-permute-done.14 = bf16[1,512,256]{2,1,0:T(8,128)(2,1)S(1)} collective-permute-done((bf16[1,512,256]{2,1,0:T(8,128)(2,1)S(1)}, bf16[1,512,256]{2,1,0:T(8,128)(2,1)S(1)}, u32[]{:S(2)}, u32[]{:S(2)}) %collective-permute-start.14) | collective-permute-done | bytes 262176 | tf_op jit(solution)/shard_map/ppermute | solution.py:275
  69.2 4.9 %turn.1.turned_ref = bf16[3,512,1024]{2,1,0:T(8,128)(2,1)S(1)} custom-call(s32[7]{0:T(128)S(1)} %stack.27.s_ref, bf16[4,512,512]{2,1,0:T(8,128)(2,1)S(1)} %pad_maximum_fusion.1.cot_ref), custom_call_target="tpu_custom_call" | custom-call | flops 67108864 | bytes 5242908 | tf_op jit(solution)/shard_map/turn/pallas_call | solution.py:21
  74.2 2.4 %gradsecond.1 = bf16[8,64,1152]{2,1,0:T(8,128)(2,1)S(1)} custom-call(s32[7]{0:T(128)S(1)} %stack.27.s_ref, bf16[3,512,1024]{2,1,0:T(8,128)(2,1)S(1)} %turn.1.turned_ref, bf16[4,384,512]{2,1,0:T(8,128)(2,1)S(1)} %pad_maximum_fusion.2.sent_ref.h1_ref), custom_call_target="tpu_custom_call" | custom-call | flops 1610612736 | bytes 5898268 | tf_op jit(solution)/shard_map/gradsecond/pallas_call | solution.py:21
  76.8 5.0 %collective-permute-start.23 = (bf16[4,32,1152]{2,1,0:T(8,128)(2,1)S(1)}, bf16[4,32,1152]{2,1,0:T(8,128)(2,1)S(1)}, u32[]{:S(2)}, u32[]{:S(2)}) collective-permute-start(bf16[4,32,1152]{2,1,0:T(8,128)(2,1)S(1)} %pad_maximum_fusion.11), channel_id=1, source_target_pairs={{0,8},{4,12},{8,0},{12,4},{16,24},{20,28},{24,16},{28,20},{1,9},{5... | collective-permute-start | bytes 884744 | tf_op jit(solution)/shard_map/ppermute | solution.py:275
  82.1 1.5 %collective-permute-start.21 = (bf16[4,32,1152]{2,1,0:T(8,128)(2,1)S(1)}, bf16[4,32,1152]{2,1,0:T(8,128)(2,1)S(1)}, u32[]{:S(2)}, u32[]{:S(2)}) collective-permute-start(bf16[4,32,1152]{2,1,0:T(8,128)(2,1)S(1)} %pad_maximum_fusion.10), channel_id=1, source_target_pairs={{0,4},{4,0},{8,12},{12,8},{16,20},{20,16},{24,28},{28,24},{1,5},{5... | collective-permute-start | bytes 884744 | tf_op jit(solution)/shard_map/ppermute | solution.py:275
  83.7 2.2 %gradfirst.1 = bf16[8,64,288]{2,1,0:T(8,128)(2,1)S(1)} custom-call(s32[7]{0:T(128)S(1)} %stack.27.s_ref, bf16[4,512,256]{2,1,0:T(8,128)(2,1)S(1)} %pad_maximum_fusion.4.dpre_ref, bf16[4,384,512]{2,1,0:T(8,128)(2,1)S(1)} %pad_maximum_fusion.2.sent_ref.h1_ref), custom_call_target="tpu_custom_call" | custom-call | flops 402653184 | bytes 2916380 | tf_op jit(solution)/shard_map/gradfirst/pallas_call | solution.py:21
  86.6 2.8 %collective-permute-done.23 = bf16[4,32,1152]{2,1,0:T(8,128)(2,1)S(1)} collective-permute-done((bf16[4,32,1152]{2,1,0:T(8,128)(2,1)S(1)}, bf16[4,32,1152]{2,1,0:T(8,128)(2,1)S(1)}, u32[]{:S(2)}, u32[]{:S(2)}) %collective-permute-start.23) | collective-permute-done | bytes 294944 | tf_op jit(solution)/shard_map/ppermute | solution.py:275
  89.6 1.5 %collective-permute-start.24 = (bf16[2,32,1152]{2,1,0:T(8,128)(2,1)S(1)}, bf16[2,32,1152]{2,1,0:T(8,128)(2,1)S(1)}, u32[]{:S(2)}, u32[]{:S(2)}) collective-permute-start(bf16[2,32,1152]{2,1,0:T(8,128)(2,1)S(1)} %pad_maximum_fusion.15), channel_id=1, source_target_pairs={{0,4},{4,0},{8,12},{12,8},{16,20},{20,16},{24,28},{28,24},{1,5},{5... | collective-permute-start | bytes 442376 | tf_op jit(solution)/shard_map/ppermute | solution.py:275
  91.1 0.9 collective-permute-done.21
  92.1 4.1 %collective-permute-done.17 = bf16[4,64,288]{2,1,0:T(8,128)(2,1)S(1)} collective-permute-done((bf16[4,64,288]{2,1,0:T(8,128)(2,1)S(1)}, bf16[4,64,288]{2,1,0:T(8,128)(2,1)S(1)}, u32[]{:S(2)}, u32[]{:S(2)}) %collective-permute-start.17) | collective-permute-done | bytes 147488 | tf_op jit(solution)/shard_map/ppermute | solution.py:275
  96.4 2.1 %collective-permute-start.22 = (bf16[2,32,1152]{2,1,0:T(8,128)(2,1)S(1)}, bf16[2,32,1152]{2,1,0:T(8,128)(2,1)S(1)}, u32[]{:S(2)}, u32[]{:S(2)}) collective-permute-start(bf16[2,32,1152]{2,1,0:T(8,128)(2,1)S(1)} %pad_maximum_fusion.14), channel_id=1, source_target_pairs={{0,8},{4,12},{8,0},{12,4},{16,24},{20,28},{24,16},{28,20},{1,9},{5... | collective-permute-start | bytes 442376 | tf_op jit(solution)/shard_map/ppermute | solution.py:275
  98.5 2.8 %collective-permute-done.18 = bf16[2,64,288]{2,1,0:T(8,128)(2,1)S(1)} collective-permute-done((bf16[2,64,288]{2,1,0:T(8,128)(2,1)S(1)}, bf16[2,64,288]{2,1,0:T(8,128)(2,1)S(1)}, u32[]{:S(2)}, u32[]{:S(2)}) %collective-permute-start.18) | collective-permute-done | bytes 73760 | tf_op jit(solution)/shard_map/ppermute | solution.py:275
  101.3 2.2 %collective-permute-start.19 = (bf16[1,64,288]{2,1,0:T(8,128)(2,1)S(1)}, bf16[1,64,288]{2,1,0:T(8,128)(2,1)S(1)}, u32[]{:S(2)}, u32[]{:S(2)}) collective-permute-start(bf16[1,64,288]{2,1,0:T(8,128)(2,1)S(1)} %slice.203), channel_id=1, source_target_pairs={{0,16},{4,20},{8,24},{12,28},{16,0},{20,4},{24,8},{28,12},{1,17},{... | collective-permute-start | bytes 110600 | tf_op jit(solution)/shard_map/ppermute | solution.py:275
  103.7 1.6 %collective-permute-start.25 = (bf16[1,64,1152]{2,1,0:T(8,128)(2,1)S(1)}, bf16[1,64,1152]{2,1,0:T(8,128)(2,1)S(1)}, u32[]{:S(2)}, u32[]{:S(2)}) collective-permute-start(bf16[1,64,1152]{2,1,0:T(8,128)(2,1)S(1)} %pad_maximum_fusion.13), channel_id=1, source_target_pairs={{0,16},{4,20},{8,24},{12,28},{16,0},{20,4},{24,8},{28,12},{1,17},{... | collective-permute-start | bytes 442376 | tf_op jit(solution)/shard_map/ppermute | solution.py:275
  105.3 3.1 %collective-permute-done.19 = bf16[1,64,288]{2,1,0:T(8,128)(2,1)S(1)} collective-permute-done((bf16[1,64,288]{2,1,0:T(8,128)(2,1)S(1)}, bf16[1,64,288]{2,1,0:T(8,128)(2,1)S(1)}, u32[]{:S(2)}, u32[]{:S(2)}) %collective-permute-start.19) | collective-permute-done | bytes 36896 | tf_op jit(solution)/shard_map/ppermute | solution.py:275
  108.4 0.7 add_bitcast_fusion.1
  109.1 2.5 %collective-permute-done.25 = bf16[1,64,1152]{2,1,0:T(8,128)(2,1)S(1)} collective-permute-done((bf16[1,64,1152]{2,1,0:T(8,128)(2,1)S(1)}, bf16[1,64,1152]{2,1,0:T(8,128)(2,1)S(1)}, u32[]{:S(2)}, u32[]{:S(2)}) %collective-permute-start.25) | collective-permute-done | bytes 147488 | tf_op jit(solution)/shard_map/ppermute | solution.py:275
  111.6 0.7 add_bitcast_fusion
  (70 shorter events, 4.3 us)
Async XLA Ops:
  1.6 8.0 %collective-permute-start.10 = (bf16[128,512]{1,0:T(8,128)(2,1)S(1)}, bf16[128,512]{1,0:T(8,128)(2,1)S(1)}, u32[]{:S(2)}, u32[]{:S(2)}) collective-permute-start(bf16[128,512]{1,0:T(8,128)(2,1)S(1)} %get-tuple-element.55), channel_id=1, source_target_pairs={{4,8},{12,16},{20,24},{8,4},{16,12},{24,20},{0,0},{28,28},{5,9},{1... | collective-permute-start | bytes 393224 | tf_op jit(solution)/shard_map/ppermute | solution.py:296
  2.3 10.6 %collective-permute-start.11 = (bf16[128,512]{1,0:T(8,128)(2,1)S(1)}, bf16[128,512]{1,0:T(8,128)(2,1)S(1)}, u32[]{:S(2)}, u32[]{:S(2)}) collective-permute-start(bf16[128,512]{1,0:T(8,128)(2,1)S(1)} %get-tuple-element.56), channel_id=1, source_target_pairs={{0,4},{4,0},{8,12},{12,8},{16,20},{20,16},{24,28},{28,24},{1,5},{5... | collective-permute-start | bytes 393224 | tf_op jit(solution)/shard_map/ppermute | solution.py:275
  8.1 8.5 %collective-permute-start.4 = (bf16[1,288,512]{2,1,0:T(8,128)(2,1)}, bf16[1,288,512]{2,1,0:T(8,128)(2,1)}, u32[]{:S(2)}, u32[]{:S(2)}) collective-permute-start(bf16[1,288,512]{2,1,0:T(8,128)(2,1)} %bitcast.54), channel_id=1, source_target_pairs={{0,2},{1,3},{2,0},{3,1},{4,6},{5,7},{6,4},{7,5},{8,10},{9,11},{10,... | collective-permute-start | bytes 884744 | tf_op jit(solution)/shard_map/ppermute | solution.py:275
  9.6 27.3 %collective-permute-start.8 = (bf16[1152,512]{1,0:T(8,128)(2,1)}, bf16[1152,512]{1,0:T(8,128)(2,1)S(1)}, u32[]{:S(2)}, u32[]{:S(2)}) collective-permute-start(bf16[1152,512]{1,0:T(8,128)(2,1)} %param.17), channel_id=1, source_target_pairs={{0,1},{1,0},{2,3},{3,2},{4,5},{5,4},{6,7},{7,6},{8,9},{9,8},{10,11... | collective-permute-start | bytes 3538952 | tf_op jit(solution)/shard_map/ppermute | solution.py:275
  9.6 7.0 %copy-start.7 = (bf16[288,512]{1,0:T(8,128)(2,1)S(1)}, bf16[288,512]{1,0:T(8,128)(2,1)}, u32[]{:S(2)}) copy-start(bf16[288,512]{1,0:T(8,128)(2,1)} %param.16) | copy-start | bytes 884740
  9.6 9.6 %copy-start.1 = (f32[1,1024,128]{2,1,0:T(8,128)S(1)}, f32[1,1024,128]{2,1,0:T(8,128)}, u32[]{:S(2)}) copy-start(f32[1,1024,128]{2,1,0:T(8,128)} %param.9) | copy-start | bytes 1572868
  9.6 9.6 %copy-start.2 = (f32[1,1024]{1,0:T(1,128)S(1)}, f32[1,1024]{1,0:T(1,128)}, u32[]{:S(2)}) copy-start(f32[1,1024]{1,0:T(1,128)} %row_ref.3) | copy-start | bytes 12292
  9.6 9.6 %copy-start.3 = (f32[1,1024]{1,0:T(1,128)S(1)}, f32[1,1024]{1,0:T(1,128)}, u32[]{:S(2)}) copy-start(f32[1,1024]{1,0:T(1,128)} %col_ref.3) | copy-start | bytes 12292
  9.7 9.6 %copy-start.4 = (s32[1,1,2,128]{3,2,1,0:T(2,128)S(1)}, s32[1,1,2,128]{3,2,1,0:T(2,128)}, u32[]{:S(2)}) copy-start(s32[1,1,2,128]{3,2,1,0:T(2,128)} %param.13) | copy-start | bytes 3076
  9.7 9.6 %copy-start.5 = (s32[1,1,2,128]{3,2,1,0:T(2,128)S(1)}, s32[1,1,2,128]{3,2,1,0:T(2,128)}, u32[]{:S(2)}) copy-start(s32[1,1,2,128]{3,2,1,0:T(2,128)} %param.14) | copy-start | bytes 3076
  14.0 17.7 %collective-permute-start.12 = (bf16[1,512,512]{2,1,0:T(8,128)(2,1)S(1)}, bf16[1,512,512]{2,1,0:T(8,128)(2,1)S(1)}, u32[]{:S(2)}, u32[]{:S(2)}) collective-permute-start(bf16[1,512,512]{2,1,0:T(8,128)(2,1)S(1)} %get-tuple-element.35), channel_id=1, source_target_pairs={{0,2},{1,3},{2,0},{3,1},{4,6},{5,7},{6,4},{7,5},{8,10},{9,11},{10,... | collective-permute-start | bytes 1572872 | tf_op jit(solution)/shard_map/ppermute | solution.py:275
  18.5 13.4 %collective-permute-start.5 = (bf16[2,288,512]{2,1,0:T(8,128)(2,1)}, bf16[2,288,512]{2,1,0:T(8,128)(2,1)}, u32[]{:S(2)}, u32[]{:S(2)}) collective-permute-start(bf16[2,288,512]{2,1,0:T(8,128)(2,1)} %pad_maximum_fusion.7), channel_id=1, source_target_pairs={{0,1},{1,0},{2,3},{3,2},{4,5},{5,4},{6,7},{7,6},{8,9},{9,8},{10,11... | collective-permute-start | bytes 1769480 | tf_op jit(solution)/shard_map/ppermute | solution.py:275
  21.1 4.9 %collective-permute-start = (bf16[288,128]{1,0:T(8,128)(2,1)}, bf16[288,128]{1,0:T(8,128)(2,1)S(1)}, u32[]{:S(2)}, u32[]{:S(2)}) collective-permute-start(bf16[288,128]{1,0:T(8,128)(2,1)} %get-tuple-element.62), channel_id=1, source_target_pairs={{0,4},{4,0},{8,12},{12,8},{16,20},{20,16},{24,28},{28,24},{1,5},{5... | collective-permute-start | bytes 221192 | tf_op jit(solution)/shard_map/ppermute | solution.py:275
  22.6 3.4 %collective-permute-start.1 = (bf16[288,128]{1,0:T(8,128)(2,1)S(1)}, bf16[288,128]{1,0:T(8,128)(2,1)S(1)}, u32[]{:S(2)}, u32[]{:S(2)}) collective-permute-start(bf16[288,128]{1,0:T(8,128)(2,1)S(1)} %get-tuple-element.61), channel_id=1, source_target_pairs={{4,8},{12,16},{20,24},{8,4},{16,12},{24,20},{0,0},{28,28},{5,9},{1... | collective-permute-start | bytes 221192 | tf_op jit(solution)/shard_map/ppermute | solution.py:296
  23.2 8.7 %copy-start.8 = (bf16[288,512]{1,0:T(8,128)(2,1)S(1)}, bf16[288,512]{1,0:T(8,128)(2,1)}, u32[]{:S(2)}) copy-start(bf16[288,512]{1,0:T(8,128)(2,1)} %param.16) | copy-start | bytes 884740
  26.7 6.6 %collective-permute-start.2 = (bf16[256,128]{1,0:T(8,128)(2,1)S(1)}, bf16[256,128]{1,0:T(8,128)(2,1)S(1)}, u32[]{:S(2)}, u32[]{:S(2)}) collective-permute-start(bf16[256,128]{1,0:T(8,128)(2,1)S(1)} %finish.1.own_ref), channel_id=1, source_target_pairs={{0,4},{4,0},{8,12},{12,8},{16,20},{20,16},{24,28},{28,24},{1,5},{5... | collective-permute-start | bytes 196616 | tf_op jit(solution)/shard_map/ppermute | solution.py:275
  31.1 2.2 %collective-permute-start.3 = (bf16[256,128]{1,0:T(8,128)(2,1)S(1)}, bf16[256,128]{1,0:T(8,128)(2,1)S(1)}, u32[]{:S(2)}, u32[]{:S(2)}) collective-permute-start(bf16[256,128]{1,0:T(8,128)(2,1)S(1)} %finish.1.own_ref), channel_id=1, source_target_pairs={{4,8},{12,16},{20,24},{8,4},{16,12},{24,20},{0,0},{28,28},{5,9},{1... | collective-permute-start | bytes 196616 | tf_op jit(solution)/shard_map/ppermute | solution.py:296
  31.8 37.1 %collective-permute-start.20 = (bf16[2,512,512]{2,1,0:T(8,128)(2,1)S(1)}, bf16[2,512,512]{2,1,0:T(8,128)(2,1)S(1)}, u32[]{:S(2)}, u32[]{:S(2)}) collective-permute-start(bf16[2,512,512]{2,1,0:T(8,128)(2,1)S(1)} %pad_maximum_fusion.5), channel_id=1, source_target_pairs={{0,1},{1,0},{2,3},{3,2},{4,5},{5,4},{6,7},{7,6},{8,9},{9,8},{10,11... | collective-permute-start | bytes 3145736 | tf_op jit(solution)/shard_map/ppermute | solution.py:275
  33.2 3.7 %copy-start.6 = (bf16[1152,512]{1,0:T(8,128)(2,1)S(1)}, bf16[1152,512]{1,0:T(8,128)(2,1)}, u32[]{:S(2)}) copy-start(bf16[1152,512]{1,0:T(8,128)(2,1)} %param.17) | copy-start | bytes 3538948
  34.8 17.6 %collective-permute-start.6 = (bf16[1,384,512]{2,1,0:T(8,128)(2,1)S(1)}, bf16[1,384,512]{2,1,0:T(8,128)(2,1)S(1)}, u32[]{:S(2)}, u32[]{:S(2)}) collective-permute-start(bf16[1,384,512]{2,1,0:T(8,128)(2,1)S(1)} %bitcast.44), channel_id=1, source_target_pairs={{0,2},{1,3},{2,0},{3,1},{4,6},{5,7},{6,4},{7,5},{8,10},{9,11},{10,... | collective-permute-start | bytes 1179656 | tf_op jit(solution)/shard_map/ppermute | solution.py:275
  36.4 16.0 %collective-permute-start.7 = (bf16[1,256,512]{2,1,0:T(8,128)(2,1)S(1)}, bf16[1,256,512]{2,1,0:T(8,128)(2,1)S(1)}, u32[]{:S(2)}, u32[]{:S(2)}) collective-permute-start(bf16[1,256,512]{2,1,0:T(8,128)(2,1)S(1)} %bitcast.50), channel_id=1, source_target_pairs={{0,2},{1,3},{2,0},{3,1},{4,6},{5,7},{6,4},{7,5},{8,10},{9,11},{10,... | collective-permute-start | bytes 786440 | tf_op jit(solution)/shard_map/ppermute | solution.py:275
  40.0 18.0 %collective-permute-start.13 = (bf16[256,512]{1,0:T(8,128)(2,1)S(1)}, bf16[256,512]{1,0:T(8,128)(2,1)S(1)}, u32[]{:S(2)}, u32[]{:S(2)}) collective-permute-start(bf16[256,512]{1,0:T(8,128)(2,1)S(1)} %get-tuple-element.20), channel_id=1, source_target_pairs={{0,2},{1,3},{2,0},{3,1},{4,6},{5,7},{6,4},{7,5},{8,10},{9,11},{10,... | collective-permute-start | bytes 786440 | tf_op jit(solution)/shard_map/ppermute | solution.py:275
  55.1 2.9 %copy-start = (bf16[1,2,128,512]{3,2,1,0:T(8,128)(2,1)S(1)}, bf16[1,2,128,512]{3,2,1,0:T(8,128)(2,1)}, u32[]{:S(2)}) copy-start(bf16[1,2,128,512]{3,2,1,0:T(8,128)(2,1)} %param.15) | copy-start | bytes 786436
  55.2 9.3 %collective-permute-start.9 = (bf16[256,512]{1,0:T(8,128)(2,1)S(1)}, bf16[256,512]{1,0:T(8,128)(2,1)S(1)}, u32[]{:S(2)}, u32[]{:S(2)}) collective-permute-start(bf16[256,512]{1,0:T(8,128)(2,1)S(1)} %get-tuple-element.17), channel_id=1, source_target_pairs={{0,2},{1,3},{2,0},{3,1},{4,6},{5,7},{6,4},{7,5},{8,10},{9,11},{10,... | collective-permute-start | bytes 786440 | tf_op jit(solution)/shard_map/ppermute | solution.py:275
  56.8 17.2 %collective-permute-start.16 = (bf16[2,384,512]{2,1,0:T(8,128)(2,1)S(1)}, bf16[2,384,512]{2,1,0:T(8,128)(2,1)S(1)}, u32[]{:S(2)}, u32[]{:S(2)}) collective-permute-start(bf16[2,384,512]{2,1,0:T(8,128)(2,1)S(1)} %pad_maximum_fusion.6), channel_id=1, source_target_pairs={{0,1},{1,0},{2,3},{3,2},{4,5},{5,4},{6,7},{7,6},{8,9},{9,8},{10,11... | collective-permute-start | bytes 2359304 | tf_op jit(solution)/shard_map/ppermute | solution.py:275
  58.8 9.9 %collective-permute-start.14 = (bf16[1,512,256]{2,1,0:T(8,128)(2,1)S(1)}, bf16[1,512,256]{2,1,0:T(8,128)(2,1)S(1)}, u32[]{:S(2)}, u32[]{:S(2)}) collective-permute-start(bf16[1,512,256]{2,1,0:T(8,128)(2,1)S(1)} %bitcast.40), channel_id=1, source_target_pairs={{0,2},{1,3},{2,0},{3,1},{4,6},{5,7},{6,4},{7,5},{8,10},{9,11},{10,... | collective-permute-start | bytes 786440 | tf_op jit(solution)/shard_map/ppermute | solution.py:275
  68.8 14.7 %collective-permute-start.15 = (bf16[2,512,256]{2,1,0:T(8,128)(2,1)S(1)}, bf16[2,512,256]{2,1,0:T(8,128)(2,1)S(1)}, u32[]{:S(2)}, u32[]{:S(2)}) collective-permute-start(bf16[2,512,256]{2,1,0:T(8,128)(2,1)S(1)} %pad_maximum_fusion.9), channel_id=1, source_target_pairs={{0,1},{1,0},{2,3},{3,2},{4,5},{5,4},{6,7},{7,6},{8,9},{9,8},{10,11... | collective-permute-start | bytes 1572872 | tf_op jit(solution)/shard_map/ppermute | solution.py:275
  76.8 12.6 %collective-permute-start.23 = (bf16[4,32,1152]{2,1,0:T(8,128)(2,1)S(1)}, bf16[4,32,1152]{2,1,0:T(8,128)(2,1)S(1)}, u32[]{:S(2)}, u32[]{:S(2)}) collective-permute-start(bf16[4,32,1152]{2,1,0:T(8,128)(2,1)S(1)} %pad_maximum_fusion.11), channel_id=1, source_target_pairs={{0,8},{4,12},{8,0},{12,4},{16,24},{20,28},{24,16},{28,20},{1,9},{5... | collective-permute-start | bytes 884744 | tf_op jit(solution)/shard_map/ppermute | solution.py:275
  82.1 9.9 %collective-permute-start.21 = (bf16[4,32,1152]{2,1,0:T(8,128)(2,1)S(1)}, bf16[4,32,1152]{2,1,0:T(8,128)(2,1)S(1)}, u32[]{:S(2)}, u32[]{:S(2)}) collective-permute-start(bf16[4,32,1152]{2,1,0:T(8,128)(2,1)S(1)} %pad_maximum_fusion.10), channel_id=1, source_target_pairs={{0,4},{4,0},{8,12},{12,8},{16,20},{20,16},{24,28},{28,24},{1,5},{5... | collective-permute-start | bytes 884744 | tf_op jit(solution)/shard_map/ppermute | solution.py:275
  85.9 10.2 %collective-permute-start.17 = (bf16[4,64,288]{2,1,0:T(8,128)(2,1)S(1)}, bf16[4,64,288]{2,1,0:T(8,128)(2,1)S(1)}, u32[]{:S(2)}, u32[]{:S(2)}) collective-permute-start(bf16[4,64,288]{2,1,0:T(8,128)(2,1)S(1)} %pad_maximum_fusion.12), channel_id=1, source_target_pairs={{0,4},{4,0},{8,12},{12,8},{16,20},{20,16},{24,28},{28,24},{1,5},{5... | collective-permute-start | bytes 442376 | tf_op jit(solution)/shard_map/ppermute | solution.py:275
  89.6 14.0 %collective-permute-start.24 = (bf16[2,32,1152]{2,1,0:T(8,128)(2,1)S(1)}, bf16[2,32,1152]{2,1,0:T(8,128)(2,1)S(1)}, u32[]{:S(2)}, u32[]{:S(2)}) collective-permute-start(bf16[2,32,1152]{2,1,0:T(8,128)(2,1)S(1)} %pad_maximum_fusion.15), channel_id=1, source_target_pairs={{0,4},{4,0},{8,12},{12,8},{16,20},{20,16},{24,28},{28,24},{1,5},{5... | collective-permute-start | bytes 442376 | tf_op jit(solution)/shard_map/ppermute | solution.py:275
  96.3 5.0 %collective-permute-start.18 = (bf16[2,64,288]{2,1,0:T(8,128)(2,1)S(1)}, bf16[2,64,288]{2,1,0:T(8,128)(2,1)S(1)}, u32[]{:S(2)}, u32[]{:S(2)}) collective-permute-start(bf16[2,64,288]{2,1,0:T(8,128)(2,1)S(1)} %pad_maximum_fusion.16), channel_id=1, source_target_pairs={{0,8},{4,12},{8,0},{12,4},{16,24},{20,28},{24,16},{28,20},{1,9},{5... | collective-permute-start | bytes 221192 | tf_op jit(solution)/shard_map/ppermute | solution.py:275
  96.4 7.2 %collective-permute-start.22 = (bf16[2,32,1152]{2,1,0:T(8,128)(2,1)S(1)}, bf16[2,32,1152]{2,1,0:T(8,128)(2,1)S(1)}, u32[]{:S(2)}, u32[]{:S(2)}) collective-permute-start(bf16[2,32,1152]{2,1,0:T(8,128)(2,1)S(1)} %pad_maximum_fusion.14), channel_id=1, source_target_pairs={{0,8},{4,12},{8,0},{12,4},{16,24},{20,28},{24,16},{28,20},{1,9},{5... | collective-permute-start | bytes 442376 | tf_op jit(solution)/shard_map/ppermute | solution.py:275
  101.3 7.1 %collective-permute-start.19 = (bf16[1,64,288]{2,1,0:T(8,128)(2,1)S(1)}, bf16[1,64,288]{2,1,0:T(8,128)(2,1)S(1)}, u32[]{:S(2)}, u32[]{:S(2)}) collective-permute-start(bf16[1,64,288]{2,1,0:T(8,128)(2,1)S(1)} %slice.203), channel_id=1, source_target_pairs={{0,16},{4,20},{8,24},{12,28},{16,0},{20,4},{24,8},{28,12},{1,17},{... | collective-permute-start | bytes 110600 | tf_op jit(solution)/shard_map/ppermute | solution.py:275
  103.7 7.9 %collective-permute-start.25 = (bf16[1,64,1152]{2,1,0:T(8,128)(2,1)S(1)}, bf16[1,64,1152]{2,1,0:T(8,128)(2,1)S(1)}, u32[]{:S(2)}, u32[]{:S(2)}) collective-permute-start(bf16[1,64,1152]{2,1,0:T(8,128)(2,1)S(1)} %pad_maximum_fusion.13), channel_id=1, source_target_pairs={{0,16},{4,20},{8,24},{12,28},{16,0},{20,4},{24,8},{28,12},{1,17},{... | collective-permute-start | bytes 442376 | tf_op jit(solution)/shard_map/ppermute | solution.py:275

commit v2 on v1

v2 whole, which is shorter than its diff:
```python
import functools
import math

import jax
import jax.numpy as jnp
from jax import lax
from jax.experimental import pallas as pl
from jax.experimental.pallas import tpu as pltpu
from jax.sharding import PartitionSpec as P

BF16 = jnp.bfloat16
F32 = jnp.float32
VMEM = pl.BlockSpec(memory_space=pltpu.VMEM)
SMEM = pl.BlockSpec(memory_space=pltpu.SMEM)
FAR = pl.BlockSpec(memory_space=pltpu.HBM)


def call(kernel, name, outs, scratch=(), scalars=1, far=0, grant=48):
    def run(*args):
        return pl.pallas_call(
            kernel,
            name=name,
            out_shape=outs,
            in_specs=[SMEM] * scalars + [VMEM] * (len(args) - scalars - far) + [FAR] * far,
            out_specs=[VMEM] * len(outs),
            scratch_shapes=list(scratch),
            compiler_params=pltpu.CompilerParams(vmem_limit_bytes=grant * 2**20),
        )(*args)

    return run


def like(shape, dtype):
    return jax.ShapeDtypeStruct(shape, dtype)


def dot(a, b):
    return jnp.dot(a, b, preferred_element_type=F32)


def dot_nt(a, b):
    return lax.dot_general(a, b, (((1,), (1,)), ((), ())), preferred_element_type=F32)


def shifted(x, step, width):
    if isinstance(step, int) and step == 0:
        return x
    total = x.shape[0]
    wide = pltpu.roll(x.astype(F32), lax.rem(total - step, total) if not isinstance(step, int) else (total - step) % total, 0)
    place = lax.broadcasted_iota(jnp.int32, x.shape, 0) % width + step
    return jnp.where((place >= 0) & (place < width), wide, 0.0).astype(x.dtype)


def column_factor(col_ref, width):
    cells = lax.broadcasted_iota(jnp.int32, (width, col_ref.shape[1]), 0).astype(F32)
    away = cells - col_ref[...]
    return jnp.exp(-0.5 * (away * away))


def cell_weights(factor, row_ref, rows):
    parts = []
    for row in rows:
        away = row - row_ref[...]
        parts.append((factor * jnp.exp(-0.5 * (away * away))).astype(BF16))
    return jnp.concatenate(parts, axis=0)


def edge_kernel(height, width, s_ref, *refs):
    far, (first_ref, second_ref), near, sems = refs[:5], refs[5:7], refs[7:12], refs[12]
    copies = [pltpu.make_async_copy(a, b, sems.at[n]) for n, (a, b) in enumerate(zip(far, near))]
    for copy in copies:
        copy.start()
    for copy in copies:
        copy.wait()
    feat_ref, row_ref, col_ref, index_ref, mask_ref = near
    slots, channels = feat_ref.shape
    factor = column_factor(col_ref, width)
    entries = index_ref.shape[1]
    slot = lax.broadcasted_iota(jnp.int32, (slots, entries), 0)
    live = slot < s_ref[1]
    feat = feat_ref[...]
    totals = []
    for side in range(2):
        named = jnp.where((slot == index_ref[side : side + 1]) & live, mask_ref[side : side + 1], 0)
        times = jnp.sum(named.astype(F32), axis=1, keepdims=True)
        values = jnp.concatenate([feat * times, jnp.broadcast_to(times, feat.shape)], axis=1)
        offset = height if side == 1 else -height
        weights = cell_weights(factor, row_ref, [float(offset + i) for i in range(height)])
        totals.append(dot(weights, values.astype(BF16)))
    for out_ref, one, other in ((first_ref, 1, 0), (second_ref, 0, 1)):
        total = jnp.where(s_ref[2] == 1, totals[one], totals[other])
        out_ref[: height * width] = total[:, :channels].astype(BF16)
        for i in range(height):
            turned = total[i * width : (i + 1) * width, channels:].T[:16]
            out_ref[height * width + 16 * i : height * width + 16 * (i + 1)] = turned.astype(BF16)


def own_kernel(height, width, s_ref, feat_ref, row_ref, col_ref, numer_ref, denom_ref):
    slots, channels = feat_ref.shape
    live = lax.broadcasted_iota(jnp.int32, (slots, channels), 0) < s_ref[1]
    values = jnp.concatenate([jnp.where(live, feat_ref[...], 0.0), live.astype(F32)], axis=1)
    weights = cell_weights(column_factor(col_ref, width), row_ref, [float(i) for i in range(height)])
    total = dot(weights, values.astype(BF16))
    numer_ref[...] = total[:, :channels]
    denom_ref[...] = total[:, channels:]


def partners(s_ref):
    first = jnp.where(s_ref[2] == 1, s_ref[4], s_ref[3])
    second = jnp.where(s_ref[2] == 1, s_ref[3], s_ref[4])
    return first, second


def finish_kernel(height, width, s_ref, numer_ref, denom_ref, first_ref, second_ref, out_ref):
    first, second = partners(s_ref)
    cells = height * width

    def got(part):
        return jnp.where(first == 1, first_ref[part].astype(F32), 0.0) + jnp.where(
            second == 1, second_ref[part].astype(F32), 0.0
        )

    for i in range(height):
        rows = slice(i * width, (i + 1) * width)
        added = got(slice(cells + 16 * i, cells + 16 * i + 16))[:1]
        added = jnp.broadcast_to(added, (width, width)).T[:, : numer_ref.shape[1]]
        numer = numer_ref[rows] + got(rows)
        out_ref[rows] = (numer * lax.rsqrt(1.0 + denom_ref[rows] + added)).astype(BF16)


def side_rows(s_ref, first, second):
    up = s_ref[2] == 1
    none = jnp.zeros_like(first)
    below = jnp.where(s_ref[3] == 1, jnp.where(up, second, first), none)
    above = jnp.where(s_ref[4] == 1, jnp.where(up, first, second), none)
    return below, above


def first_kernel(height, width, offsets, s_ref, own_ref, a_ref, b_ref, w_near, w_far, cot_ref, other_ref, *refs):
    pre_ref, h1_ref, edge_ref, near_ref, pair_ref, side_a, side_b, w_full = refs
    channels = own_ref.shape[1]
    count, piece, hidden = w_near.shape
    for place, offset in enumerate(offsets):
        at = lax.bitwise_xor(s_ref[5], offset) * piece
        w_full[pl.ds(pl.multiple_of(at, 32), piece)] = (w_near, w_far)[place // count][place % count]
    below, above = side_rows(s_ref, a_ref[...], b_ref[...])
    grid = jnp.concatenate([below[-2 * width :], own_ref[...], above[: 2 * width]], axis=0)
    rows = height + 2
    moved = [shifted(grid, step, width) for step in (-1, 0, 1)]
    patches = jnp.concatenate([moved[dx][dy * width : (dy + rows) * width] for dy in range(3) for dx in range(3)], axis=1)
    pre = dot(patches, w_full[...])
    h1 = (pre * jax.nn.sigmoid(pre)).astype(BF16)
    zero = jnp.zeros((width, hidden), BF16)
    pre_ref[...] = pre[width:-width]
    h1_ref[...] = h1[width:-width]
    edge_ref[:width] = jnp.where(s_ref[3] == 1, h1[:width], zero)
    edge_ref[width:] = jnp.where(s_ref[4] == 1, h1[-width:], zero)
    near = grid[width:-width]
    for i in range(rows):
        near_ref[:, i * channels : (i + 1) * channels] = near[i * width : (i + 1) * width]
    for n, ref in enumerate((cot_ref, other_ref)):
        pair_ref[n] = ref[...]
        low, high = ref[:width], ref[(height - 1) * width :]
        side_a[n * width : (n + 1) * width] = jnp.where(s_ref[2] == 1, high, low)
        side_b[n * width : (n + 1) * width] = jnp.where(s_ref[2] == 1, low, high)


def wide_rows(s_ref, width, pair_ref, a_ref, b_ref, n):
    rows = slice(n * width, (n + 1) * width)
    below, above = side_rows(s_ref, a_ref[rows], b_ref[rows])
    return jnp.concatenate([below, pair_ref[n], above], axis=0)


def chunk_place(s_ref, step, per_group, per_block):
    chunk = s_ref[6] * per_group + step
    block = chunk // per_block
    return block // 3, block % 3, chunk % per_block


def back_kernel(height, width, chunk, s_ref, pair_ref, a_ref, b_ref, w_ref, own_ref, other_ref, moved_ref):
    hidden = w_ref.shape[1]
    halves = hidden // chunk
    cells = height * width
    per_group = w_ref.shape[0] // chunk
    for member, out_ref in enumerate((own_ref, other_ref)):
        grid = wide_rows(s_ref, width, pair_ref, a_ref, b_ref, member)
        for dx in range(3):
            moved_ref[member, dx] = shifted(grid, 1 - dx, width)
        totals = [jnp.zeros((cells, chunk), F32) for _ in range(halves)]
        for step in range(per_group):
            dy, dx, _ = chunk_place(s_ref, step, per_group, halves)
            rows = pl.ds(pl.multiple_of((2 - dy) * width, width), cells)
            totals[step % halves] += dot_nt(moved_ref[member, dx, rows], w_ref[step * chunk : (step + 1) * chunk])
        start = chunk_place(s_ref, 0, per_group, halves)[2]
        for rank in range(halves):
            half = lax.rem(start + rank, halves)
            columns = pl.ds(pl.multiple_of(half * chunk, chunk), chunk)
            out_ref[:, columns] = totals[rank].astype(out_ref.dtype)


def second_kernel(height, width, chunk, s_ref, mid_one, mid_two, edge_one, edge_two, w_ref, own_ref, other_ref, moved_ref):
    hidden = w_ref.shape[1]
    halves = hidden // chunk
    cells = height * width
    per_group = w_ref.shape[0] // chunk
    for member, (mid_ref, edge_ref, out_ref) in enumerate(((mid_one, edge_one, own_ref), (mid_two, edge_two, other_ref))):
        grid = jnp.concatenate([edge_ref[:width], mid_ref[...], edge_ref[width:]], axis=0)
        for dx in range(3):
            place = shifted(grid, dx - 1, width)
            for half in range(halves):
                moved_ref[member, dx, half] = place[:, half * chunk : (half + 1) * chunk]
        total = mid_ref[...].astype(F32) if member == 0 else jnp.zeros((cells, hidden), F32)
        for step in range(per_group):
            dy, dx, half = chunk_place(s_ref, step, per_group, halves)
            rows = pl.ds(pl.multiple_of(dy * width, width), cells)
            total += dot(moved_ref[member, dx, half, rows], w_ref[step * chunk : (step + 1) * chunk])
        out_ref[...] = total.astype(out_ref.dtype)


def dpre_kernel(s_ref, pre_ref, cot_ref, near_ref, own_ref, got_ref, out_ref):
    pre = pre_ref[...]
    back = cot_ref[...].astype(F32) + own_ref[...] + got_ref[...].astype(F32)
    sig = jax.nn.sigmoid(pre)
    hidden, cells = pre.shape[1], pre.shape[0]
    out_ref[:hidden] = (back * sig * (1.0 + pre * (1.0 - sig))).T.astype(BF16)
    width = near_ref.shape[0]
    for half in range(near_ref.shape[1] // cells):
        out_ref[hidden + half * width : hidden + (half + 1) * width] = near_ref[:, half * cells : (half + 1) * cells]


def turn_kernel(height, width, rows_out, s_ref, near_pair, near_a, near_b, far_pair, far_a, far_b, out_ref, wide_ref):
    count, cells, hidden = near_pair.shape
    first = (s_ref[5] * rows_out) // hidden
    for t in range(2 * count):
        refs = (near_pair, near_a, near_b) if t < count else (far_pair, far_a, far_b)
        wide_ref[t] = wide_rows(s_ref, width, *refs, t % count)
    for dx in range(3):
        j = lax.rem(dx + 3 - lax.rem(first, 3), 3)
        dy = jnp.minimum(first + j, 8) // 3
        rows = pl.ds(pl.multiple_of((2 - dy) * width, width), cells)
        for t in range(2 * count):
            x = shifted(wide_ref[t, rows], 1 - dx, width)
            out_ref[j, :, t * cells : (t + 1) * cells] = x.astype(F32).T.astype(BF16)


def grad_second_kernel(rows_out, blocks, lats, s_ref, turned_ref, *refs):
    h1_refs, (keep_one, send_one, keep_two, send_two, full_ref) = refs[:-5], refs[-5:]
    hidden = h1_refs[0].shape[1]
    base = s_ref[5] * rows_out
    off = base - (base // hidden) * hidden
    h1 = jnp.concatenate([h1_ref[...] for h1_ref in h1_refs], axis=0)
    for j in range(blocks):
        full_ref[:, j * hidden : (j + 1) * hidden] = dot(turned_ref[j], h1)
    part = hidden // lats
    half = part // 2
    columns = pl.ds(pl.multiple_of(off, 128), rows_out)
    slots = [0] * 4
    for k in range(lats):
        at = lax.bitwise_xor(s_ref[0], k) * part
        for number, (keep_ref, send_ref, bit) in enumerate(((keep_one, send_one, 1), (keep_two, send_two, 2))):
            sent = 1 if k & bit else 0
            place = 2 * number + sent
            rows = pl.ds(pl.multiple_of(at + number * half, half), half)
            (keep_ref, send_ref)[sent][slots[place]] = full_ref[rows, columns].astype(BF16)
            slots[place] += 1


def grad_first_kernel(height, width, rows_out, lats, distance, s_ref, *refs):
    sent_refs, (keep_ref, send_ref, full_ref) = refs[:-3], refs[-3:]
    cells = sent_refs[0].shape[1]
    channels = full_ref.shape[2]
    rows = height + 2
    hidden = rows * channels
    wide = 3 * channels
    part = hidden // lats
    for t, sent_ref in enumerate(sent_refs):
        for i in range(rows):
            half, side = i // height, i % height
            full_ref[t, i * width : (i + 1) * width] = sent_ref[
                hidden + half * width : hidden + (half + 1) * width, side * channels : (side + 1) * channels
            ]
    for out_ref, away in ((send_ref, distance), (keep_ref, 0)):
        base = lax.bitwise_xor(s_ref[5], away) * rows_out
        first = base // channels
        off = base - first * channels
        turn = lax.rem(first, 3)
        total = jnp.zeros((hidden, wide), F32)
        for t, sent_ref in enumerate(sent_refs):
            pieces = []
            for dx in range(3):
                dy = jnp.minimum(first + lax.rem(dx + 3 - turn, 3), 8) // 3
                near = full_ref[t, pl.ds(pl.multiple_of(dy * width, width), cells)]
                pieces.append(shifted(near, dx - 1, width))
            total += dot(sent_ref[:hidden], jnp.concatenate(pieces, axis=1))
        total = pltpu.roll(total, lax.rem(2 * wide - off - turn * channels, wide), 1)[:, :rows_out].astype(BF16)
        for k in range(lats):
            out_ref[lax.bitwise_xor(s_ref[0], k)] = total[k * part : (k + 1) * part]


def add_kernel(places, *refs):
    count = len(places)
    for n, (stay, go) in enumerate(places):
        keep_ref, got_ref = refs[2 * n : 2 * n + 2]
        stay_ref, go_ref = refs[2 * (count + n) : 2 * (count + n) + 2]
        for out_ref, picked in ((stay_ref, stay), (go_ref, go)):
            for slot, place in enumerate(picked):
                out_ref[slot] = (keep_ref[place].astype(F32) + got_ref[place].astype(F32)).astype(BF16)


def meet_kernel(one_ref, got_one, two_ref, got_two, stay_ref, go_ref):
    half = one_ref.shape[1]
    for rows, keep_ref, got_ref in ((slice(0, half), one_ref, got_one), (slice(half, 2 * half), two_ref, got_two)):
        for place in range(keep_ref.shape[0]):
            out_ref = (stay_ref, go_ref)[place % 2]
            out_ref[place // 2, rows] = (keep_ref[place].astype(F32) + got_ref[place].astype(F32)).astype(BF16)


def last_kernel(keep_ref, got_ref, out_ref):
    out_ref[...] = keep_ref[0].astype(F32) + got_ref[0].astype(F32)


def swap(value, axis, bit):
    return lax.ppermute(value, axis, [(i, i ^ bit) for i in range(lax.axis_size(axis))])


def after(value, other):
    return lax.optimization_barrier((value, other))[0]


def distances(bits):
    order = [0]
    for bit in bits:
        order = order + [n ^ bit for n in order]
    return order


def with_partners(first, second):
    size = lax.axis_size("lat")
    pairs = [(i, i + 1) for i in range(1, size - 1, 2)]
    pairs = pairs + [(j, i) for i, j in pairs] + [(0, 0), (size - 1, size - 1)]
    return swap(first, "lat", 1), lax.ppermute(second, "lat", pairs)


def parted(offsets, bit):
    stay = [n for n, k in enumerate(offsets) if not k & bit]
    go = [n for n, k in enumerate(offsets) if k & bit]
    return (stay, go), [offsets[n] for n in stay]


def add_step(streams, offsets, bits):
    places, left = zip(*[parted(o, b) for o, b in zip(offsets, bits)])
    outs = [like((len(side), *keep.shape[1:]), BF16) for (keep, _), place in zip(streams, places) for side in place]
    flat = call(functools.partial(add_kernel, places), "add", outs, scalars=0)(*[v for pair in streams for v in pair])
    return [flat[n : n + 2] for n in range(0, len(flat), 2)], list(left)


def finished(stay, got, offsets, bits):
    for bit in bits:
        ((stay, go),), (offsets,) = add_step([(stay, got)], [offsets], [bit])
        got = swap(go, "lat", bit)
    return call(last_kernel, "last", [like(stay.shape[1:], F32)], scalars=0)(stay, got)[0].T


def local(obs_feat, obs_row, obs_col, counts, edge_index, edge_mask, cotangent, w_first, w_second):
    _, height, width, hidden = cotangent.shape
    channels = obs_feat.shape[2]
    cells = height * width
    n_dp, n_lat = lax.axis_size("dp"), lax.axis_size("lat")
    band, member = lax.axis_index("lat"), lax.axis_index("dp")
    scalars = jnp.stack(
        [
            band,
            counts[0, 0],
            1 - band % 2,
            (band > 0).astype(jnp.int32),
            (band < n_lat - 1).astype(jnp.int32),
            member,
            member // 2,
        ]
    ).astype(jnp.int32)
    lat_bits = [1 << n for n in range(n_lat.bit_length() - 1)]
    outer = n_dp // 2
    cot = cotangent[0].reshape(cells, hidden)

    feat, row, col = obs_feat[0], obs_row, obs_col
    payload = like((height * (width + 16), channels), BF16)
    observed = [feat, row, col, edge_index[0, 0], edge_mask[0, 0]]
    edges = call(
        functools.partial(edge_kernel, height, width),
        "edges",
        [payload, payload],
        scratch=[pltpu.VMEM(v.shape, v.dtype) for v in observed] + [pltpu.SemaphoreType.DMA((len(observed),))],
        far=len(observed),
        grant=60,
    )(scalars, *observed)
    w_got, cot_got = swap(w_first, "dp", outer), swap(cot, "dp", outer)
    from_first, from_second = with_partners(*edges)
    numer, denom = call(functools.partial(own_kernel, height, width), "own", [like((cells, channels), F32)] * 2)(
        after(scalars, edges[0]), feat, row, col
    )
    h0 = call(functools.partial(finish_kernel, height, width), "finish", [like((cells, channels), BF16)])(
        after(scalars, w_got), numer, denom, from_first, from_second
    )[0]
    h0_first, h0_second = with_partners(h0, h0)

    w_near = jnp.stack([w_first, w_got])
    w_far = swap(w_near, "dp", 1)
    w_other = swap(after(w_second, h0), "dp", 1)
    side = like((2 * width, hidden), BF16)
    pre1, h1, edge, h0_near, cot_pair, side_a, side_b = call(
        functools.partial(first_kernel, height, width, distances([outer, 1])),
        "first",
        [
            like((cells, hidden), F32),
            like((cells, hidden), BF16),
            side,
            like((width, (height + 2) * channels), BF16),
            like((2, cells, hidden), BF16),
            side,
            side,
        ],
        scratch=[pltpu.VMEM((n_dp * w_first.shape[0], hidden), BF16)],
    )(after(scalars, w_other), h0, h0_first, h0_second, w_near, w_far, cot, cot_got)

    lower = member % 2 == 0
    w_other = after(w_other, h1)
    w_two = jnp.concatenate([jnp.where(lower, w_second, w_other), jnp.where(lower, w_other, w_second)], axis=0)
    h1_got = swap(h1, "dp", outer)
    got_a, got_b = with_partners(side_a, side_b)
    pair_far = swap(cot_pair, "dp", 1)
    h1_got, got_a, got_b, pair_far, w_two = lax.optimization_barrier((h1_got, got_a, got_b, pair_far, w_two))
    chunk = math.gcd(w_two.shape[0], hidden)
    wide_cells = (height + 2) * width
    partial_outs = [like((cells, hidden), F32), like((cells, hidden), BF16)]
    back, back_other = call(
        functools.partial(back_kernel, height, width, chunk),
        "back",
        partial_outs,
        scratch=[pltpu.VMEM((2, 3, wide_cells, hidden), BF16)],
    )(scalars, cot_pair, got_a, got_b, w_two)
    back_got = swap(back_other, "dp", outer)
    h1_far, h1_far_got, far_a, far_b = [swap(v, "dp", 1) for v in (h1, h1_got, got_a, got_b)]

    rows_two, rows_one = w_second.shape[0], w_first.shape[0]
    part = hidden // n_lat
    turned = call(
        functools.partial(turn_kernel, height, width, rows_two),
        "turn",
        [like((3, hidden, n_dp * cells), BF16)],
        scratch=[pltpu.VMEM((n_dp, wide_cells, hidden), BF16)],
    )(after(scalars, back), cot_pair, got_a, got_b, pair_far, far_a, far_b)[0]
    piece = like((n_lat // 2, part // 2, rows_two), BF16)
    keep_one, send_one, keep_two, send_two = call(
        functools.partial(grad_second_kernel, rows_two, 3, n_lat),
        "gradsecond",
        [piece] * 4,
        scratch=[pltpu.VMEM((hidden, 3 * hidden), F32)],
    )(scalars, turned, h1, h1_got, h1_far, h1_far_got)
    streams = [(keep_one, swap(send_one, "lat", 1)), (keep_two, swap(send_two, "lat", 2))]
    offsets = [[k for k in range(n_lat) if not k & bit] for bit in (1, 2)]
    ((stay_one, go_one), (stay_two, go_two)), _ = add_step(streams, offsets, (2, 1))
    got_one, got_two = swap(go_one, "lat", 2), swap(go_two, "lat", 1)
    stay, go = call(meet_kernel, "meet", [like((n_lat // 8, part, rows_two), BF16)] * 2, scalars=0)(
        stay_one, got_one, stay_two, got_two
    )
    grad_second = finished(stay, swap(go, "lat", 4), list(range(0, n_lat, 8)), lat_bits[3:])

    sent = call(dpre_kernel, "dpre", [like((hidden + (height + 2) // height * width, cells), BF16)])(
        after(scalars, keep_one), pre1, cot, h0_near, back, back_got
    )[0]
    keep, send = call(
        functools.partial(grad_first_kernel, height, width, rows_one, n_lat, outer),
        "gradfirst",
        [like((n_lat, part, rows_one), BF16)] * 2,
        scratch=[pltpu.VMEM((2, wide_cells, channels), BF16)],
    )(scalars, sent, swap(sent, "dp", 1))
    grad_first = finished(keep, swap(send, "dp", outer), list(range(n_lat)), lat_bits)

    edge_got = swap(after(edge, send_one), "dp", outer)
    second, second_other = call(
        functools.partial(second_kernel, height, width, chunk),
        "second",
        partial_outs,
        scratch=[pltpu.VMEM((2, 3, hidden // chunk, wide_cells, chunk), BF16)],
    )(scalars, h1, h1_got, edge, edge_got, w_two)
    encoded = (second + swap(second_other, "dp", outer).astype(F32)).astype(BF16).reshape(1, height, width, hidden)
    return encoded, grad_first, grad_second


def with_halo(value, sides, width):
    for axis, dim in sides:
        size, length = (lax.axis_size(axis), value.shape[dim])
        up = [(i, (i + 1) % size) for i in range(size - 1)]
        down = [(j, i) for i, j in up]
        last = lax.slice_in_dim(value, length - width, length, axis=dim)
        first = lax.slice_in_dim(value, 0, width, axis=dim)
        before = lax.ppermute(last, axis, up)
        after = lax.ppermute(first, axis, down)
        value = jnp.concatenate([before, value, after], axis=dim)
    return value


def passed_along(block, axis, distance):
    devices = range(lax.axis_size(axis))
    route = [(i - distance, i) for i in devices if i - distance in devices]
    return lax.ppermute(block, axis, route)


def gauss_weights(cell_rows, cell_cols, rows, cols, valid):
    drow = cell_rows[:, None] - rows[None, :]
    dcol = cell_cols[:, None] - cols[None, :]
    return valid[None, :] * jnp.exp(-0.5 * (drow * drow + dcol * dcol))


def haloed_rows(grid):
    padded = with_halo(grid, (("lat", 0),), 1)
    return jnp.pad(padded, ((0, 0), (1, 1), (0, 0)))


def padded_patches(padded, height, width):
    pieces = [padded[dy : dy + height, dx : dx + width] for dy in range(3) for dx in range(3)]
    return jnp.concatenate(pieces, axis=-1).reshape(height * width, -1)


def plain(obs_feat, obs_row, obs_col, counts, edge_index, edge_mask, cotangent, w_first, w_second):
    feat = obs_feat[0]
    slot_total = feat.shape[0]
    channels = feat.shape[1]
    height = cotangent.shape[1]
    width = cotangent.shape[2]
    hidden = cotangent.shape[3]
    band_index = lax.axis_index("lat")
    band_base = (band_index * height).astype(jnp.float32)
    count = counts[0, 0]
    row_g = obs_row[0] + band_base
    col_b = obs_col[0]
    slots = jnp.arange(slot_total, dtype=jnp.int32)
    valid = (slots < count).astype(jnp.float32)

    def pick(listed, listed_mask):
        picked_feat = jnp.take(feat, listed, axis=0)
        live_flag = listed_mask.astype(jnp.float32) * (listed < count).astype(jnp.float32)
        place = jnp.stack([jnp.take(row_g, listed), jnp.take(col_b, listed), live_flag], axis=1)
        return (picked_feat, place)

    low_feat, low_place = pick(edge_index[0, 0, 0], edge_mask[0, 0, 0])
    high_feat, high_place = pick(edge_index[0, 0, 1], edge_mask[0, 0, 1])
    below_feat, below_place = passed_along((high_feat, high_place), "lat", 1)
    above_feat, above_place = passed_along((low_feat, low_place), "lat", -1)
    recv_feat = jnp.concatenate([below_feat, above_feat], 0)
    recv_place = jnp.concatenate([below_place, above_place], 0)
    cells = jnp.arange(height * width, dtype=jnp.int32)
    cell_rows = band_base + (cells // width).astype(jnp.float32)
    cell_cols = (cells % width).astype(jnp.float32)
    edge_weights = gauss_weights(
        cell_rows, cell_cols, recv_place[:, 0], recv_place[:, 1], recv_place[:, 2]
    )
    numer = jnp.dot(edge_weights, recv_feat, precision=lax.Precision.HIGHEST)
    denom = jnp.sum(edge_weights, 1)
    own_weights = gauss_weights(cell_rows, cell_cols, row_g, col_b, valid)
    numer = numer + jnp.dot(own_weights, feat, precision=lax.Precision.HIGHEST)
    denom = denom + jnp.sum(own_weights, 1)
    h0 = (
        (numer / jnp.sqrt(1.0 + denom)[:, None])
        .astype(jnp.bfloat16)
        .reshape(height, width, channels)
    )

    def fold_rows(patches, piece):
        return jnp.dot(patches, piece, preferred_element_type=jnp.float32)

    patches0 = padded_patches(haloed_rows(h0), height, width)
    pre1 = fold_rows(patches0, lax.all_gather(w_first, "dp", axis=0, tiled=True))
    h1 = jax.nn.silu(pre1).astype(jnp.bfloat16)
    patches1 = padded_patches(haloed_rows(h1.reshape(height, width, hidden)), height, width)
    pre2 = fold_rows(patches1, lax.all_gather(w_second, "dp", axis=0, tiled=True))
    encoded = (h1.astype(jnp.float32) + pre2).astype(jnp.bfloat16).reshape(1, height, width, hidden)
    cot = cotangent[0]
    cot_pad = haloed_rows(cot).reshape(-1, hidden)
    spread = lax.dot_general(
        cot_pad,
        lax.all_gather(w_second, "dp", axis=0, tiled=True),
        (((1,), (1,)), ((), ())),
        preferred_element_type=jnp.float32,
    )
    spread = spread.reshape(height + 2, width + 2, 9, hidden)
    dh1 = cot.astype(jnp.float32)
    for dy in range(3):
        for dx in range(3):
            dh1 = dh1 + spread[2 - dy : 2 - dy + height, 2 - dx : 2 - dx + width, dy * 3 + dx]
    sig = jax.nn.sigmoid(pre1)
    dpre1 = (dh1.reshape(-1, hidden) * sig * (1.0 + pre1 * (1.0 - sig))).astype(jnp.bfloat16)
    cot_flat = cot.reshape(-1, hidden)
    contract = (((0,), (0,)), ((), ()))
    grad_two = lax.dot_general(patches1, cot_flat, contract, preferred_element_type=jnp.float32)
    grad_one = lax.dot_general(patches0, dpre1, contract, preferred_element_type=jnp.float32)
    partial_one, partial_two = (
        lax.psum_scatter(
            grad_one.astype(jnp.bfloat16), "dp", scatter_dimension=0, tiled=True
        ).astype(jnp.float32),
        lax.psum_scatter(
            grad_two.astype(jnp.bfloat16), "dp", scatter_dimension=0, tiled=True
        ).astype(jnp.float32),
    )
    grad_first, grad_second = (
        lax.psum_scatter(
            partial_one.astype(jnp.bfloat16), "lat", scatter_dimension=1, tiled=True
        ).astype(jnp.float32),
        lax.psum_scatter(
            partial_two.astype(jnp.bfloat16), "lat", scatter_dimension=1, tiled=True
        ).astype(jnp.float32),
    )
    return (encoded, grad_first, grad_second)


def fits(mesh, height, width, hidden, channels, rows_one, rows_two):
    n_dp, n_lat = mesh.shape["dp"], mesh.shape["lat"]
    powers = all(n & (n - 1) == 0 for n in (n_dp, n_lat, hidden, channels))
    grid = height == 2 and width == channels and width % 128 == 0 and (height + 2) * channels == hidden
    blocks = all(
        [(d * rows + rows - 1) // size - d * rows // size for d in range(n_dp)] == [2] * n_dp
        for rows, size in ((rows_one, channels), (rows_two, hidden))
    )
    return powers and grid and n_dp == 2 * 2 and n_lat > 4 and (hidden // n_lat) % 32 == 0 and blocks and rows_one % 32 == 0 and rows_two % 128 == 0


def solution(mesh):
    in_specs = (
        P("dp", "lat", None),
        P("dp", "lat"),
        P("dp", "lat"),
        P("dp", "lat"),
        P("dp", "lat", None, None),
        P("dp", "lat", None, None),
        P("dp", "lat", None, None),
        P("dp", None),
        P("dp", None),
    )
    out_specs = (P("dp", "lat", None, None), P("dp", "lat"), P("dp", "lat"))

    def run(*args):
        feat, cot, w_first, w_second = args[0], args[6], args[7], args[8]
        n_dp, n_lat = mesh.shape["dp"], mesh.shape["lat"]
        shapes = (cot.shape[1] // n_lat, *cot.shape[2:], feat.shape[2], w_first.shape[0] // n_dp, w_second.shape[0] // n_dp)
        step = local if fits(mesh, *shapes) else plain
        return jax.shard_map(step, mesh=mesh, in_specs=in_specs, out_specs=out_specs, check_vma=False)(*args)

    return run
```

time: 113 us -> 93.9 us (0.83)
  waiting for transfers between devices: 42.1 us -> 23.2 us
  other arithmetic: 9.02 us -> 2.42 us
  starting transfers between devices: 38.4 us -> 42.5 us
  local copies, waits for them, and re-layouts: 1 us -> 3.7 us
    ppermute x23 -> x26, waiting for transfers between devices: 42.1 us -> 23.2 us  [swap(): lax.ppermute(value, axis, [(i, i ^ bit) for i in range(lax.axis_size(axis...]
    concatenate x15 -> x0, other arithmetic: 4.19 us -> none  [the longest x7 3.59 us: gathered(): value = jnp.concatenate([value, swap(value, axis, bit)], axis=0)]
    ppermute x23 -> x26, starting transfers between devices: 36.4 us -> 39.5 us  [swap(): lax.ppermute(value, axis, [(i, i ^ bit) for i in range(lax.axis_size(axis...]
    unnamed x18 -> x16, local copies, waits for them, and re-layouts: 0.05 us -> 3.07 us
    transpose x2 -> x0, other arithmetic: 1.4 us -> none  [the longest x1 0.74 us: local(): grad_second = lat_sum(grad_two).T]
    select_n x1, other arithmetic: 0.16 us -> 1.43 us  [local(): jnp.where(lower, w_second, w_other)]
    pallas_call x10 -> x17, Pallas kernels: 20 us -> 20.2 us  [run(): pl.pallas_call(kernel, name=name, out_shape=outs, in_specs=[SMEM] * scala...]
  transfers between devices with their start and end apart: 26 -> 29, of which waited for: 14 -> 10; matrix products, arithmetic and copies ran while one was open for 7% -> 3% of each run, Pallas kernels for 18% -> 18%
where the time goes in v2:
time: 93.9 us; the launch traced here: 93.5 us
  starting transfers between devices  42.5 us (45%)
  waiting for transfers between devices  23.2 us (25%)
  Pallas kernels  20.2 us (22%)
  local copies, waits for them, and re-layouts  3.7 us (4%)
  other arithmetic  2.42 us (3%)
  between operations  1.59 us (2%)
    ppermute x26, starting transfers between devices, swap(): lax.ppermute(value, axis, [(i, i ^ bit) for i in range(lax.axis_size(axis...  39.5 us
    ppermute x26, waiting for transfers between devices, swap(): lax.ppermute(value, axis, [(i, i ^ bit) for i in range(lax.axis_size(axis...  23.2 us
    pallas_call x17, Pallas kernels, run(): pl.pallas_call(kernel, name=name, out_shape=outs, in_specs=[SMEM] * scala...  20.2 us
    unnamed x16, local copies, waits for them, and re-layouts  3.07 us
    ppermute x3, starting transfers between devices, with_partners(): return (swap(first, 'lat', 1), lax.ppermute(second, 'lat', pairs))  3.03 us
  transfers between devices with their start and end apart: 29, of which 10 were waited for; matrix products, arithmetic and copies ran while one was open for 3% of the time, Pallas kernels for 18%

profile of v2, /device:TPU:0, one launch (start us, length us, event | category | flops | bytes accessed | tf_op | source)
XLA Modules:
  0.0 93.5 jit_solution(14266789626239523250)
XLA Ops:
  0.6 3.0 %collective-permute-start = (bf16[288,512]{1,0:T(8,128)(2,1)}, bf16[288,512]{1,0:T(8,128)(2,1)S(1)}, u32[]{:S(2)}, u32[]{:S(2)}) collective-permute-start(bf16[288,512]{1,0:T(8,128)(2,1)} %param.16), channel_id=1, source_target_pairs={{0,2},{1,3},{2,0},{3,1},{4,6},{5,7},{6,4},{7,5},{8,10},{9,11},{10,... | collective-permute-start | bytes 884744 | tf_op jit(solution)/shard_map/ppermute | solution.py:323
  4.3 0.6 stack.44.s_ref
  5.0 3.2 %edges.1 = (bf16[288,128]{1,0:T(8,128)(2,1)}, bf16[288,128]{1,0:T(8,128)(2,1)}) custom-call(s32[7]{0:T(128)} %stack.44.s_ref, f32[1024,128]{1,0:T(8,128)} %bitcast.17, f32[1,1024]{1,0:T(1,128)} %row_ref.1, f32[1,1024]{1,0:T(1,128)} %col_ref.1, s32[2,128]{1,0:T(2,128)} %bitcast.27, s32[2,128]{1,0:T(2,128)} %bitcast.28), custom_call_target="tpu_custom_call" | custom-call | tf_op jit(solution)/shard_map/edges/pallas_call | solution.py:20
  8.2 1.6 %collective-permute-start.1 = (bf16[288,128]{1,0:T(8,128)(2,1)}, bf16[288,128]{1,0:T(8,128)(2,1)S(1)}, u32[]{:S(2)}, u32[]{:S(2)}) collective-permute-start(bf16[288,128]{1,0:T(8,128)(2,1)} %get-tuple-element.50), channel_id=1, source_target_pairs={{0,4},{4,0},{8,12},{12,8},{16,20},{20,16},{24,28},{28,24},{1,5},{5... | collective-permute-start | bytes 221192 | tf_op jit(solution)/shard_map/ppermute | solution.py:323
  9.8 1.5 %collective-permute-start.2 = (bf16[288,128]{1,0:T(8,128)(2,1)}, bf16[288,128]{1,0:T(8,128)(2,1)S(1)}, u32[]{:S(2)}, u32[]{:S(2)}) collective-permute-start(bf16[288,128]{1,0:T(8,128)(2,1)} %get-tuple-element.54), channel_id=1, source_target_pairs={{4,8},{12,16},{20,24},{8,4},{16,12},{24,20},{0,0},{28,28},{5,9},{1... | collective-permute-start | bytes 221192 | tf_op jit(solution)/shard_map/ppermute | solution.py:341
  11.3 1.0 %copy-done = f32[1,1024,128]{2,1,0:T(8,128)S(1)} copy-done((f32[1,1024,128]{2,1,0:T(8,128)S(1)}, f32[1,1024,128]{2,1,0:T(8,128)}, u32[]{:S(2)}) %copy-start) | copy-done | bytes 524312
  12.3 0.6 copy-done.2
  13.0 0.7 copy-done.4
  13.7 0.7 copy-done.5
  14.3 0.9 own.1
  15.3 0.7 finish.1.own_ref
  16.1 0.5 collective-permute-start.6
  17.2 3.4 %collective-permute-start.4 = (bf16[256,128]{1,0:T(8,128)(2,1)S(1)}, bf16[256,128]{1,0:T(8,128)(2,1)S(1)}, u32[]{:S(2)}, u32[]{:S(2)}) collective-permute-start(bf16[256,128]{1,0:T(8,128)(2,1)S(1)} %finish.1.own_ref), channel_id=1, source_target_pairs={{0,4},{4,0},{8,12},{12,8},{16,20},{20,16},{24,28},{28,24},{1,5},{5... | collective-permute-start | bytes 196616 | tf_op jit(solution)/shard_map/ppermute | solution.py:323
  20.6 0.7 collective-permute-start.5
  21.3 3.7 %collective-permute-done.7.other_ref = bf16[256,512]{1,0:T(8,128)(2,1)S(1)} collective-permute-done((bf16[256,512]{1,0:T(8,128)(2,1)S(1)}, bf16[256,512]{1,0:T(8,128)(2,1)S(1)}, u32[]{:S(2)}, u32[]{:S(2)}) %collective-permute-start.7) | collective-permute-done | bytes 262176 | tf_op jit(solution)/shard_map/ppermute | solution.py:323
  25.0 1.6 %first.1 = (f32[256,512]{1,0:T(8,128)S(1)}, bf16[256,512]{1,0:T(8,128)(2,1)S(1)}, bf16[256,512]{1,0:T(8,128)(2,1)S(1)}, bf16[128,512]{1,0:T(8,128)(2,1)S(1)}, bf...) custom-call(s32[7]{0:T(128)S(1)} %copy-done.3, ...), custom_call_target="tpu_custom_call" | custom-call | tf_op jit(solution)/shard_map/first/pallas_call | solution.py:20
  26.5 0.6 collective-permute-start.8
  27.1 3.8 %collective-permute-start.9 = (bf16[256,512]{1,0:T(8,128)(2,1)S(1)}, bf16[256,512]{1,0:T(8,128)(2,1)S(1)}, u32[]{:S(2)}, u32[]{:S(2)}) collective-permute-start(bf16[256,512]{1,0:T(8,128)(2,1)S(1)} %get-tuple-element.58), channel_id=1, source_target_pairs={{0,4},{4,0},{8,12},{12,8},{16,20},{20,16},{24,28},{28,24},{1,5},{5... | collective-permute-start | bytes 786440 | tf_op jit(solution)/shard_map/ppermute | solution.py:323
  30.9 0.8 collective-permute-start.10
  31.9 1.4 %broadcast_select_fusion.1 = (bf16[1152,512]{1,0:T(8,128)(2,1)S(1)}, bf16[1152,512]{1,0:T(8,128)(2,1)S(1)}) fusion(bf16[1152,512]{1,0:T(8,128)(2,1)S(1)} %copy-done.6, bf16[1152,512]{1,0:T(8,128)(2,1)} %collective-permute-done.3, pred[]{:T(512)S(6)} %eq.6), kind=kLoop, calls=%fused_computation.2 | loop fusion | flops 1179648 | bytes 4718593 | tf_op jit(solution)/shard_map/jit(_where)/select_n | solution.py:427
  33.4 0.6 collective-permute-done.8.refs_1_.mid_two
  34.1 6.8 %collective-permute-done.9.a_ref.near_a = bf16[256,512]{1,0:T(8,128)(2,1)S(1)} collective-permute-done((bf16[256,512]{1,0:T(8,128)(2,1)S(1)}, bf16[256,512]{1,0:T(8,128)(2,1)S(1)}, u32[]{:S(2)}, u32[]{:S(2)}) %collective-permute-start.9) | collective-permute-done | bytes 262176 | tf_op jit(solution)/shard_map/ppermute | solution.py:323
  41.9 2.8 %back.1 = (f32[256,512]{1,0:T(8,128)S(1)}, bf16[256,512]{1,0:T(8,128)(2,1)S(1)}) custom-call(s32[7]{0:T(128)S(1)} %copy-done.3, bf16[2,256,512]{2,1,0:T(8,128)(2,1)S(1)} %get-tuple-element.60.pair_ref.near_pair, bf16[256,512]{1,0:T(8,128)(2,1)S(1)} %collective-permute-done.9.a_ref.near_a, bf16[256,512]{1,0:T(8,128)(2,1)S(1)} %collective-permute-done.10.b_ref.near_b, ...), custom_call_target="tpu_custom_call" | custom-call | tf_op jit(solution)/shard_map/back/pallas_call | solution.py:20
  44.7 1.6 %collective-permute-start.18 = (bf16[256,512]{1,0:T(8,128)(2,1)S(1)}, bf16[256,512]{1,0:T(8,128)(2,1)S(1)}, u32[]{:S(2)}, u32[]{:S(2)}) collective-permute-start(bf16[256,512]{1,0:T(8,128)(2,1)S(1)} %get-tuple-element.78), channel_id=1, source_target_pairs={{0,2},{1,3},{2,0},{3,1},{4,6},{5,7},{6,4},{7,5},{8,10},{9,11},{10,... | collective-permute-start | bytes 786440 | tf_op jit(solution)/shard_map/ppermute | solution.py:323
  46.3 1.8 %turn.1.turned_ref = bf16[3,512,1024]{2,1,0:T(8,128)(2,1)S(1)} custom-call(s32[7]{0:T(128)S(1)} %copy-done.3, bf16[2,256,512]{2,1,0:T(8,128)(2,1)S(1)} %get-tuple-element.60.pair_ref.near_pair, bf16[256,512]{1,0:T(8,128)(2,1)S(1)} %collective-permute-done.9.a_ref.near_a, bf16[256,512]{1,0:T(8,128)(2,1)S(1)} %collective-permute-done.10.b_ref.near_b, ...), custom_call_target="tpu_custom_call" | custom-call | tf_op jit(solution)/shard_map/turn/pallas_call | solution.py:20
  48.1 2.5 %gradsecond.1 = (bf16[4,32,1152]{2,1,0:T(8,128)(2,1)S(1)}, bf16[4,32,1152]{2,1,0:T(8,128)(2,1)S(1)}, bf16[4,32,1152]{2,1,0:T(8,128)(2,1)S(1)}, bf16[4,32,1152]{2,1,0:T(8,128)(2,1)S(1)}) custom-call(s32[7]{0:T(128)S(1)} %copy-done.3, bf16[3,512,1024]{2,1,0:T(8,128)(2,1)S(1)} %turn.1.turned_ref, bf16[256,512]{1,0:T(8,128)(2,1)S(1)} %get-tuple-element.57.refs_0_.mid_one, ...), custom_call_target="tpu_custom_call" | custom-call | tf_op jit(solution)/shard_map/gradsecond/pallas_call | solution.py:20
  50.6 2.5 %collective-permute-done.18.got_ref = bf16[256,512]{1,0:T(8,128)(2,1)S(1)} collective-permute-done((bf16[256,512]{1,0:T(8,128)(2,1)S(1)}, bf16[256,512]{1,0:T(8,128)(2,1)S(1)}, u32[]{:S(2)}, u32[]{:S(2)}) %collective-permute-start.18) | collective-permute-done | bytes 262176 | tf_op jit(solution)/shard_map/ppermute | solution.py:323
  53.1 0.8 dpre.1.refs_0_
  54.0 1.6 %collective-permute-start.16 = (bf16[256,512]{1,0:T(8,128)(2,1)S(1)}, bf16[256,512]{1,0:T(8,128)(2,1)S(1)}, u32[]{:S(2)}, u32[]{:S(2)}) collective-permute-start(bf16[256,512]{1,0:T(8,128)(2,1)S(1)} %get-tuple-element.71.edge_one), channel_id=1, source_target_pairs={{0,2},{1,3},{2,0},{3,1},{4,6},{5,7},{6,4},{7,5},{8,10},{9,11},{10,... | collective-permute-start | bytes 786440 | tf_op jit(solution)/shard_map/ppermute | solution.py:323
  55.7 1.5 %gradfirst.1 = (bf16[8,64,288]{2,1,0:T(8,128)(2,1)S(1)}, bf16[8,64,288]{2,1,0:T(8,128)(2,1)S(1)}) custom-call(s32[7]{0:T(128)S(1)} %copy-done.3, bf16[768,256]{1,0:T(8,128)(2,1)S(1)} %dpre.1.refs_0_, bf16[768,256]{1,0:T(8,128)(2,1)S(1)} %collective-permute-done.19.refs_1_), custom_call_target="tpu_custom_call" | custom-call | tf_op jit(solution)/shard_map/gradfirst/pallas_call | solution.py:20
  57.1 1.6 %collective-permute-start.20 = (bf16[8,64,288]{2,1,0:T(8,128)(2,1)S(1)}, bf16[8,64,288]{2,1,0:T(8,128)(2,1)S(1)}, u32[]{:S(2)}, u32[]{:S(2)}) collective-permute-start(bf16[8,64,288]{2,1,0:T(8,128)(2,1)S(1)} %get-tuple-element.80), channel_id=1, source_target_pairs={{0,2},{1,3},{2,0},{3,1},{4,6},{5,7},{6,4},{7,5},{8,10},{9,11},{10,... | collective-permute-start | bytes 884744 | tf_op jit(solution)/shard_map/ppermute | solution.py:323
  58.7 2.5 %collective-permute-start.24 = (bf16[4,32,1152]{2,1,0:T(8,128)(2,1)S(1)}, bf16[4,32,1152]{2,1,0:T(8,128)(2,1)S(1)}, u32[]{:S(2)}, u32[]{:S(2)}) collective-permute-start(bf16[4,32,1152]{2,1,0:T(8,128)(2,1)S(1)} %get-tuple-element.70), channel_id=1, source_target_pairs={{0,4},{4,0},{8,12},{12,8},{16,20},{20,16},{24,28},{28,24},{1,5},{5... | collective-permute-start | bytes 884744 | tf_op jit(solution)/shard_map/ppermute | solution.py:323
  61.2 1.6 %collective-permute-start.25 = (bf16[4,32,1152]{2,1,0:T(8,128)(2,1)S(1)}, bf16[4,32,1152]{2,1,0:T(8,128)(2,1)S(1)}, u32[]{:S(2)}, u32[]{:S(2)}) collective-permute-start(bf16[4,32,1152]{2,1,0:T(8,128)(2,1)S(1)} %get-tuple-element.88), channel_id=1, source_target_pairs={{0,8},{4,12},{8,0},{12,4},{16,24},{20,28},{24,16},{28,20},{1,9},{5... | collective-permute-start | bytes 884744 | tf_op jit(solution)/shard_map/ppermute | solution.py:323
  63.1 2.7 %second.1 = (f32[256,512]{1,0:T(8,128)S(1)}, bf16[256,512]{1,0:T(8,128)(2,1)S(1)}) custom-call(s32[7]{0:T(128)S(1)} %copy-done.3, bf16[256,512]{1,0:T(8,128)(2,1)S(1)} %get-tuple-element.57.refs_0_.mid_one, bf16[256,512]{1,0:T(8,128)(2,1)S(1)} %collective-permute-done.8.refs_1_.mid_two, bf16[256,512]{1,0:T(8,128)(2,1)S(1)} %get-tuple-element.71.edge_one, ...), custom_call_target="tpu_custom_call" | custom-call | tf_op jit(solution)/shard_map/second/pallas_call | solution.py:20
  65.9 1.6 %collective-permute-start.17 = (bf16[256,512]{1,0:T(8,128)(2,1)S(1)}, bf16[256,512]{1,0:T(8,128)(2,1)S(1)}, u32[]{:S(2)}, u32[]{:S(2)}) collective-permute-start(bf16[256,512]{1,0:T(8,128)(2,1)S(1)} %get-tuple-element.73), channel_id=1, source_target_pairs={{0,2},{1,3},{2,0},{3,1},{4,6},{5,7},{6,4},{7,5},{8,10},{9,11},{10,... | collective-permute-start | bytes 786440 | tf_op jit(solution)/shard_map/ppermute | solution.py:323
  67.4 4.1 %collective-permute-done.20.refs_1_ = bf16[8,64,288]{2,1,0:T(8,128)(2,1)S(1)} collective-permute-done((bf16[8,64,288]{2,1,0:T(8,128)(2,1)S(1)}, bf16[8,64,288]{2,1,0:T(8,128)(2,1)S(1)}, u32[]{:S(2)}, u32[]{:S(2)}) %collective-permute-start.20) | collective-permute-done | bytes 294944 | tf_op jit(solution)/shard_map/ppermute | solution.py:323
  71.7 2.6 %collective-permute-start.21 = (bf16[4,64,288]{2,1,0:T(8,128)(2,1)S(1)}, bf16[4,64,288]{2,1,0:T(8,128)(2,1)S(1)}, u32[]{:S(2)}, u32[]{:S(2)}) collective-permute-start(bf16[4,64,288]{2,1,0:T(8,128)(2,1)S(1)} %get-tuple-element.82), channel_id=1, source_target_pairs={{0,4},{4,0},{8,12},{12,8},{16,20},{20,16},{24,28},{28,24},{1,5},{5... | collective-permute-start | bytes 442376 | tf_op jit(solution)/shard_map/ppermute | solution.py:323
  74.4 1.7 %collective-permute-start.26 = (bf16[2,32,1152]{2,1,0:T(8,128)(2,1)S(1)}, bf16[2,32,1152]{2,1,0:T(8,128)(2,1)S(1)}, u32[]{:S(2)}, u32[]{:S(2)}) collective-permute-start(bf16[2,32,1152]{2,1,0:T(8,128)(2,1)S(1)} %get-tuple-element.90), channel_id=1, source_target_pairs={{0,8},{4,12},{8,0},{12,4},{16,24},{20,28},{24,16},{28,20},{1,9},{5... | collective-permute-start | bytes 442376 | tf_op jit(solution)/shard_map/ppermute | solution.py:323
  76.0 1.5 %collective-permute-start.27 = (bf16[2,32,1152]{2,1,0:T(8,128)(2,1)S(1)}, bf16[2,32,1152]{2,1,0:T(8,128)(2,1)S(1)}, u32[]{:S(2)}, u32[]{:S(2)}) collective-permute-start(bf16[2,32,1152]{2,1,0:T(8,128)(2,1)S(1)} %get-tuple-element.92), channel_id=1, source_target_pairs={{0,4},{4,0},{8,12},{12,8},{16,20},{20,16},{24,28},{28,24},{1,5},{5... | collective-permute-start | bytes 442376 | tf_op jit(solution)/shard_map/ppermute | solution.py:323
  77.5 2.2 %collective-permute-done.21.refs_1_ = bf16[4,64,288]{2,1,0:T(8,128)(2,1)S(1)} collective-permute-done((bf16[4,64,288]{2,1,0:T(8,128)(2,1)S(1)}, bf16[4,64,288]{2,1,0:T(8,128)(2,1)S(1)}, u32[]{:S(2)}, u32[]{:S(2)}) %collective-permute-start.21) | collective-permute-done | bytes 147488 | tf_op jit(solution)/shard_map/ppermute | solution.py:323
  79.7 3.2 %collective-permute-start.22 = (bf16[2,64,288]{2,1,0:T(8,128)(2,1)S(1)}, bf16[2,64,288]{2,1,0:T(8,128)(2,1)S(1)}, u32[]{:S(2)}, u32[]{:S(2)}) collective-permute-start(bf16[2,64,288]{2,1,0:T(8,128)(2,1)S(1)} %get-tuple-element.84), channel_id=1, source_target_pairs={{0,8},{4,12},{8,0},{12,4},{16,24},{20,28},{24,16},{28,20},{1,9},{5... | collective-permute-start | bytes 221192 | tf_op jit(solution)/shard_map/ppermute | solution.py:323
  83.0 2.5 %collective-permute-start.28 = (bf16[1,64,1152]{2,1,0:T(8,128)(2,1)S(1)}, bf16[1,64,1152]{2,1,0:T(8,128)(2,1)S(1)}, u32[]{:S(2)}, u32[]{:S(2)}) collective-permute-start(bf16[1,64,1152]{2,1,0:T(8,128)(2,1)S(1)} %get-tuple-element.94), channel_id=1, source_target_pairs={{0,16},{4,20},{8,24},{12,28},{16,0},{20,4},{24,8},{28,12},{1,17},{... | collective-permute-start | bytes 442376 | tf_op jit(solution)/shard_map/ppermute | solution.py:323
  85.6 1.1 %collective-permute-done.22.refs_1_ = bf16[2,64,288]{2,1,0:T(8,128)(2,1)S(1)} collective-permute-done((bf16[2,64,288]{2,1,0:T(8,128)(2,1)S(1)}, bf16[2,64,288]{2,1,0:T(8,128)(2,1)S(1)}, u32[]{:S(2)}, u32[]{:S(2)}) %collective-permute-start.22) | collective-permute-done | bytes 73760 | tf_op jit(solution)/shard_map/ppermute | solution.py:323
  86.7 2.9 %collective-permute-start.23 = (bf16[1,64,288]{2,1,0:T(8,128)(2,1)S(1)}, bf16[1,64,288]{2,1,0:T(8,128)(2,1)S(1)}, u32[]{:S(2)}, u32[]{:S(2)}) collective-permute-start(bf16[1,64,288]{2,1,0:T(8,128)(2,1)S(1)} %get-tuple-element.86), channel_id=1, source_target_pairs={{0,16},{4,20},{8,24},{12,28},{16,0},{20,4},{24,8},{28,12},{1,17},{... | collective-permute-start | bytes 110600 | tf_op jit(solution)/shard_map/ppermute | solution.py:323
  89.6 0.8 add_convert_fusion
  90.4 1.7 %collective-permute-done.28.got_ref = bf16[1,64,1152]{2,1,0:T(8,128)(2,1)S(1)} collective-permute-done((bf16[1,64,1152]{2,1,0:T(8,128)(2,1)S(1)}, bf16[1,64,1152]{2,1,0:T(8,128)(2,1)S(1)}, u32[]{:S(2)}, u32[]{:S(2)}) %collective-permute-start.28) | collective-permute-done | bytes 147488 | tf_op jit(solution)/shard_map/ppermute | solution.py:323
  92.1 0.7 last.3
  92.9 0.7 last.2
  (48 shorter events, 2.9 us)
Async XLA Ops:
  0.6 15.4 %copy-start.7 = (bf16[288,512]{1,0:T(8,128)(2,1)S(1)}, bf16[288,512]{1,0:T(8,128)(2,1)}, u32[]{:S(2)}) copy-start(bf16[288,512]{1,0:T(8,128)(2,1)} %param.16) | copy-start | bytes 884740
  0.6 14.6 %collective-permute-start = (bf16[288,512]{1,0:T(8,128)(2,1)}, bf16[288,512]{1,0:T(8,128)(2,1)S(1)}, u32[]{:S(2)}, u32[]{:S(2)}) collective-permute-start(bf16[288,512]{1,0:T(8,128)(2,1)} %param.16), channel_id=1, source_target_pairs={{0,2},{1,3},{2,0},{3,1},{4,6},{5,7},{6,4},{7,5},{8,10},{9,11},{10,... | collective-permute-start | bytes 884744 | tf_op jit(solution)/shard_map/ppermute | solution.py:323
  5.0 11.7 %copy-start.1 = (bf16[1,2,128,512]{3,2,1,0:T(8,128)(2,1)S(1)}, bf16[1,2,128,512]{3,2,1,0:T(8,128)(2,1)}, u32[]{:S(2)}) copy-start(bf16[1,2,128,512]{3,2,1,0:T(8,128)(2,1)} %param.15) | copy-start | bytes 786436
  8.2 16.8 %copy-start.3 = (s32[7]{0:T(128)S(1)}, s32[7]{0:T(128)}, u32[]{:S(2)}) copy-start(s32[7]{0:T(128)} %stack.44.s_ref) | copy-start | bytes 88
  8.2 7.0 %collective-permute-start.1 = (bf16[288,128]{1,0:T(8,128)(2,1)}, bf16[288,128]{1,0:T(8,128)(2,1)S(1)}, u32[]{:S(2)}, u32[]{:S(2)}) collective-permute-start(bf16[288,128]{1,0:T(8,128)(2,1)} %get-tuple-element.50), channel_id=1, source_target_pairs={{0,4},{4,0},{8,12},{12,8},{16,20},{20,16},{24,28},{28,24},{1,5},{5... | collective-permute-start | bytes 221192 | tf_op jit(solution)/shard_map/ppermute | solution.py:323
  9.8 5.5 %collective-permute-start.2 = (bf16[288,128]{1,0:T(8,128)(2,1)}, bf16[288,128]{1,0:T(8,128)(2,1)S(1)}, u32[]{:S(2)}, u32[]{:S(2)}) collective-permute-start(bf16[288,128]{1,0:T(8,128)(2,1)} %get-tuple-element.54), channel_id=1, source_target_pairs={{4,8},{12,16},{20,24},{8,4},{16,12},{24,20},{0,0},{28,28},{5,9},{1... | collective-permute-start | bytes 221192 | tf_op jit(solution)/shard_map/ppermute | solution.py:341
  11.3 1.0 %copy-start = (f32[1,1024,128]{2,1,0:T(8,128)S(1)}, f32[1,1024,128]{2,1,0:T(8,128)}, u32[]{:S(2)}) copy-start(f32[1,1024,128]{2,1,0:T(8,128)} %param.9) | copy-start | bytes 1572868
  12.3 0.6 copy-start.2
  13.0 0.7 copy-start.4
  13.7 0.7 copy-start.5
  15.9 5.3 %collective-permute-start.3 = (bf16[1152,512]{1,0:T(8,128)(2,1)}, bf16[1152,512]{1,0:T(8,128)(2,1)}, u32[]{:S(2)}, u32[]{:S(2)}) collective-permute-start(bf16[1152,512]{1,0:T(8,128)(2,1)} %param.17), channel_id=1, source_target_pairs={{0,1},{1,0},{2,3},{3,2},{4,5},{5,4},{6,7},{7,6},{8,9},{9,8},{10,11... | collective-permute-start | bytes 3538952 | tf_op jit(solution)/shard_map/ppermute | solution.py:323
  16.1 15.7 %copy-start.6 = (bf16[1152,512]{1,0:T(8,128)(2,1)S(1)}, bf16[1152,512]{1,0:T(8,128)(2,1)}, u32[]{:S(2)}) copy-start(bf16[1152,512]{1,0:T(8,128)(2,1)} %param.17) | copy-start | bytes 3538948
  16.1 8.9 %collective-permute-start.6 = (bf16[2,288,512]{2,1,0:T(8,128)(2,1)S(1)}, bf16[2,288,512]{2,1,0:T(8,128)(2,1)S(1)}, u32[]{:S(2)}, u32[]{:S(2)}) collective-permute-start(bf16[2,288,512]{2,1,0:T(8,128)(2,1)S(1)} %pad_maximum_fusion.1.w_near), channel_id=1, source_target_pairs={{0,1},{1,0},{2,3},{3,2},{4,5},{5,4},{6,7},{7,6},{8,9},{9,8},{10,11... | collective-permute-start | bytes 1769480 | tf_op jit(solution)/shard_map/ppermute | solution.py:323
  16.7 8.3 %collective-permute-start.7 = (bf16[256,512]{1,0:T(8,128)(2,1)S(1)}, bf16[256,512]{1,0:T(8,128)(2,1)S(1)}, u32[]{:S(2)}, u32[]{:S(2)}) collective-permute-start(bf16[256,512]{1,0:T(8,128)(2,1)S(1)} %bitcast.19), channel_id=1, source_target_pairs={{0,2},{1,3},{2,0},{3,1},{4,6},{5,7},{6,4},{7,5},{8,10},{9,11},{10,... | collective-permute-start | bytes 786440 | tf_op jit(solution)/shard_map/ppermute | solution.py:323
  17.2 7.8 %collective-permute-start.4 = (bf16[256,128]{1,0:T(8,128)(2,1)S(1)}, bf16[256,128]{1,0:T(8,128)(2,1)S(1)}, u32[]{:S(2)}, u32[]{:S(2)}) collective-permute-start(bf16[256,128]{1,0:T(8,128)(2,1)S(1)} %finish.1.own_ref), channel_id=1, source_target_pairs={{0,4},{4,0},{8,12},{12,8},{16,20},{20,16},{24,28},{28,24},{1,5},{5... | collective-permute-start | bytes 196616 | tf_op jit(solution)/shard_map/ppermute | solution.py:323
  20.6 4.4 %collective-permute-start.5 = (bf16[256,128]{1,0:T(8,128)(2,1)S(1)}, bf16[256,128]{1,0:T(8,128)(2,1)S(1)}, u32[]{:S(2)}, u32[]{:S(2)}) collective-permute-start(bf16[256,128]{1,0:T(8,128)(2,1)S(1)} %finish.1.own_ref), channel_id=1, source_target_pairs={{4,8},{12,16},{20,24},{8,4},{16,12},{24,20},{0,0},{28,28},{5,9},{1... | collective-permute-start | bytes 196616 | tf_op jit(solution)/shard_map/ppermute | solution.py:341
  26.5 7.5 %collective-permute-start.8 = (bf16[256,512]{1,0:T(8,128)(2,1)S(1)}, bf16[256,512]{1,0:T(8,128)(2,1)S(1)}, u32[]{:S(2)}, u32[]{:S(2)}) collective-permute-start(bf16[256,512]{1,0:T(8,128)(2,1)S(1)} %get-tuple-element.57.refs_0_.mid_one), channel_id=1, source_target_pairs={{0,2},{1,3},{2,0},{3,1},{4,6},{5,7},{6,4},{7,5},{8,10},{9,11},{10,... | collective-permute-start | bytes 786440 | tf_op jit(solution)/shard_map/ppermute | solution.py:323
  27.1 13.7 %collective-permute-start.9 = (bf16[256,512]{1,0:T(8,128)(2,1)S(1)}, bf16[256,512]{1,0:T(8,128)(2,1)S(1)}, u32[]{:S(2)}, u32[]{:S(2)}) collective-permute-start(bf16[256,512]{1,0:T(8,128)(2,1)S(1)} %get-tuple-element.58), channel_id=1, source_target_pairs={{0,4},{4,0},{8,12},{12,8},{16,20},{20,16},{24,28},{28,24},{1,5},{5... | collective-permute-start | bytes 786440 | tf_op jit(solution)/shard_map/ppermute | solution.py:323
  30.9 9.9 %collective-permute-start.10 = (bf16[256,512]{1,0:T(8,128)(2,1)S(1)}, bf16[256,512]{1,0:T(8,128)(2,1)S(1)}, u32[]{:S(2)}, u32[]{:S(2)}) collective-permute-start(bf16[256,512]{1,0:T(8,128)(2,1)S(1)} %get-tuple-element.59), channel_id=1, source_target_pairs={{4,8},{12,16},{20,24},{8,4},{16,12},{24,20},{0,0},{28,28},{5,9},{1... | collective-permute-start | bytes 786440 | tf_op jit(solution)/shard_map/ppermute | solution.py:341
  31.8 9.1 %collective-permute-start.11 = (bf16[2,256,512]{2,1,0:T(8,128)(2,1)S(1)}, bf16[2,256,512]{2,1,0:T(8,128)(2,1)S(1)}, u32[]{:S(2)}, u32[]{:S(2)}) collective-permute-start(bf16[2,256,512]{2,1,0:T(8,128)(2,1)S(1)} %get-tuple-element.60.pair_ref.near_pair), channel_id=1, source_target_pairs={{0,1},{1,0},{2,3},{3,2},{4,5},{5,4},{6,7},{7,6},{8,9},{9,8},{10,11... | collective-permute-start | bytes 1572872 | tf_op jit(solution)/shard_map/ppermute | solution.py:323
  40.8 5.5 %collective-permute-start.12 = (bf16[256,512]{1,0:T(8,128)(2,1)S(1)}, bf16[256,512]{1,0:T(8,128)(2,1)S(1)}, u32[]{:S(2)}, u32[]{:S(2)}) collective-permute-start(bf16[256,512]{1,0:T(8,128)(2,1)S(1)} %collective-permute-done.9.a_ref.near_a), channel_id=1, source_target_pairs={{0,1},{1,0},{2,3},{3,2},{4,5},{5,4},{6,7},{7,6},{8,9},{9,8},{10,11... | collective-permute-start | bytes 786440 | tf_op jit(solution)/shard_map/ppermute | solution.py:323
  40.8 5.5 %collective-permute-start.13 = (bf16[256,512]{1,0:T(8,128)(2,1)S(1)}, bf16[256,512]{1,0:T(8,128)(2,1)S(1)}, u32[]{:S(2)}, u32[]{:S(2)}) collective-permute-start(bf16[256,512]{1,0:T(8,128)(2,1)S(1)} %collective-permute-done.10.b_ref.near_b), channel_id=1, source_target_pairs={{0,1},{1,0},{2,3},{3,2},{4,5},{5,4},{6,7},{7,6},{8,9},{9,8},{10,11... | collective-permute-start | bytes 786440 | tf_op jit(solution)/shard_map/ppermute | solution.py:323
  41.4 6.7 %collective-permute-start.14 = (bf16[256,512]{1,0:T(8,128)(2,1)S(1)}, bf16[256,512]{1,0:T(8,128)(2,1)S(1)}, u32[]{:S(2)}, u32[]{:S(2)}) collective-permute-start(bf16[256,512]{1,0:T(8,128)(2,1)S(1)} %get-tuple-element.57.refs_0_.mid_one), channel_id=1, source_target_pairs={{0,1},{1,0},{2,3},{3,2},{4,5},{5,4},{6,7},{7,6},{8,9},{9,8},{10,11... | collective-permute-start | bytes 786440 | tf_op jit(solution)/shard_map/ppermute | solution.py:323
  41.4 6.7 %collective-permute-start.15 = (bf16[256,512]{1,0:T(8,128)(2,1)S(1)}, bf16[256,512]{1,0:T(8,128)(2,1)S(1)}, u32[]{:S(2)}, u32[]{:S(2)}) collective-permute-start(bf16[256,512]{1,0:T(8,128)(2,1)S(1)} %collective-permute-done.8.refs_1_.mid_two), channel_id=1, source_target_pairs={{0,1},{1,0},{2,3},{3,2},{4,5},{5,4},{6,7},{7,6},{8,9},{9,8},{10,11... | collective-permute-start | bytes 786440 | tf_op jit(solution)/shard_map/ppermute | solution.py:323
  44.7 8.3 %collective-permute-start.18 = (bf16[256,512]{1,0:T(8,128)(2,1)S(1)}, bf16[256,512]{1,0:T(8,128)(2,1)S(1)}, u32[]{:S(2)}, u32[]{:S(2)}) collective-permute-start(bf16[256,512]{1,0:T(8,128)(2,1)S(1)} %get-tuple-element.78), channel_id=1, source_target_pairs={{0,2},{1,3},{2,0},{3,1},{4,6},{5,7},{6,4},{7,5},{8,10},{9,11},{10,... | collective-permute-start | bytes 786440 | tf_op jit(solution)/shard_map/ppermute | solution.py:323
  53.9 1.8 %collective-permute-start.19 = (bf16[768,256]{1,0:T(8,128)(2,1)S(1)}, bf16[768,256]{1,0:T(8,128)(2,1)S(1)}, u32[]{:S(2)}, u32[]{:S(2)}) collective-permute-start(bf16[768,256]{1,0:T(8,128)(2,1)S(1)} %dpre.1.refs_0_), channel_id=1, source_target_pairs={{0,1},{1,0},{2,3},{3,2},{4,5},{5,4},{6,7},{7,6},{8,9},{9,8},{10,11... | collective-permute-start | bytes 1179656 | tf_op jit(solution)/shard_map/ppermute | solution.py:323
  54.0 9.2 %collective-permute-start.16 = (bf16[256,512]{1,0:T(8,128)(2,1)S(1)}, bf16[256,512]{1,0:T(8,128)(2,1)S(1)}, u32[]{:S(2)}, u32[]{:S(2)}) collective-permute-start(bf16[256,512]{1,0:T(8,128)(2,1)S(1)} %get-tuple-element.71.edge_one), channel_id=1, source_target_pairs={{0,2},{1,3},{2,0},{3,1},{4,6},{5,7},{6,4},{7,5},{8,10},{9,11},{10,... | collective-permute-start | bytes 786440 | tf_op jit(solution)/shard_map/ppermute | solution.py:323
  57.1 14.4 %collective-permute-start.20 = (bf16[8,64,288]{2,1,0:T(8,128)(2,1)S(1)}, bf16[8,64,288]{2,1,0:T(8,128)(2,1)S(1)}, u32[]{:S(2)}, u32[]{:S(2)}) collective-permute-start(bf16[8,64,288]{2,1,0:T(8,128)(2,1)S(1)} %get-tuple-element.80), channel_id=1, source_target_pairs={{0,2},{1,3},{2,0},{3,1},{4,6},{5,7},{6,4},{7,5},{8,10},{9,11},{10,... | collective-permute-start | bytes 884744 | tf_op jit(solution)/shard_map/ppermute | solution.py:323
  58.7 15.5 %collective-permute-start.24 = (bf16[4,32,1152]{2,1,0:T(8,128)(2,1)S(1)}, bf16[4,32,1152]{2,1,0:T(8,128)(2,1)S(1)}, u32[]{:S(2)}, u32[]{:S(2)}) collective-permute-start(bf16[4,32,1152]{2,1,0:T(8,128)(2,1)S(1)} %get-tuple-element.70), channel_id=1, source_target_pairs={{0,4},{4,0},{8,12},{12,8},{16,20},{20,16},{24,28},{28,24},{1,5},{5... | collective-permute-start | bytes 884744 | tf_op jit(solution)/shard_map/ppermute | solution.py:323
  61.2 13.0 %collective-permute-start.25 = (bf16[4,32,1152]{2,1,0:T(8,128)(2,1)S(1)}, bf16[4,32,1152]{2,1,0:T(8,128)(2,1)S(1)}, u32[]{:S(2)}, u32[]{:S(2)}) collective-permute-start(bf16[4,32,1152]{2,1,0:T(8,128)(2,1)S(1)} %get-tuple-element.88), channel_id=1, source_target_pairs={{0,8},{4,12},{8,0},{12,4},{16,24},{20,28},{24,16},{28,20},{1,9},{5... | collective-permute-start | bytes 884744 | tf_op jit(solution)/shard_map/ppermute | solution.py:323
  65.9 23.8 %collective-permute-start.17 = (bf16[256,512]{1,0:T(8,128)(2,1)S(1)}, bf16[256,512]{1,0:T(8,128)(2,1)S(1)}, u32[]{:S(2)}, u32[]{:S(2)}) collective-permute-start(bf16[256,512]{1,0:T(8,128)(2,1)S(1)} %get-tuple-element.73), channel_id=1, source_target_pairs={{0,2},{1,3},{2,0},{3,1},{4,6},{5,7},{6,4},{7,5},{8,10},{9,11},{10,... | collective-permute-start | bytes 786440 | tf_op jit(solution)/shard_map/ppermute | solution.py:323
  71.7 8.0 %collective-permute-start.21 = (bf16[4,64,288]{2,1,0:T(8,128)(2,1)S(1)}, bf16[4,64,288]{2,1,0:T(8,128)(2,1)S(1)}, u32[]{:S(2)}, u32[]{:S(2)}) collective-permute-start(bf16[4,64,288]{2,1,0:T(8,128)(2,1)S(1)} %get-tuple-element.82), channel_id=1, source_target_pairs={{0,4},{4,0},{8,12},{12,8},{16,20},{20,16},{24,28},{28,24},{1,5},{5... | collective-permute-start | bytes 442376 | tf_op jit(solution)/shard_map/ppermute | solution.py:323
  74.4 8.6 %collective-permute-start.26 = (bf16[2,32,1152]{2,1,0:T(8,128)(2,1)S(1)}, bf16[2,32,1152]{2,1,0:T(8,128)(2,1)S(1)}, u32[]{:S(2)}, u32[]{:S(2)}) collective-permute-start(bf16[2,32,1152]{2,1,0:T(8,128)(2,1)S(1)} %get-tuple-element.90), channel_id=1, source_target_pairs={{0,8},{4,12},{8,0},{12,4},{16,24},{20,28},{24,16},{28,20},{1,9},{5... | collective-permute-start | bytes 442376 | tf_op jit(solution)/shard_map/ppermute | solution.py:323
  76.0 6.9 %collective-permute-start.27 = (bf16[2,32,1152]{2,1,0:T(8,128)(2,1)S(1)}, bf16[2,32,1152]{2,1,0:T(8,128)(2,1)S(1)}, u32[]{:S(2)}, u32[]{:S(2)}) collective-permute-start(bf16[2,32,1152]{2,1,0:T(8,128)(2,1)S(1)} %get-tuple-element.92), channel_id=1, source_target_pairs={{0,4},{4,0},{8,12},{12,8},{16,20},{20,16},{24,28},{28,24},{1,5},{5... | collective-permute-start | bytes 442376 | tf_op jit(solution)/shard_map/ppermute | solution.py:323
  79.7 7.0 %collective-permute-start.22 = (bf16[2,64,288]{2,1,0:T(8,128)(2,1)S(1)}, bf16[2,64,288]{2,1,0:T(8,128)(2,1)S(1)}, u32[]{:S(2)}, u32[]{:S(2)}) collective-permute-start(bf16[2,64,288]{2,1,0:T(8,128)(2,1)S(1)} %get-tuple-element.84), channel_id=1, source_target_pairs={{0,8},{4,12},{8,0},{12,4},{16,24},{20,28},{24,16},{28,20},{1,9},{5... | collective-permute-start | bytes 221192 | tf_op jit(solution)/shard_map/ppermute | solution.py:323
  83.0 9.1 %collective-permute-start.28 = (bf16[1,64,1152]{2,1,0:T(8,128)(2,1)S(1)}, bf16[1,64,1152]{2,1,0:T(8,128)(2,1)S(1)}, u32[]{:S(2)}, u32[]{:S(2)}) collective-permute-start(bf16[1,64,1152]{2,1,0:T(8,128)(2,1)S(1)} %get-tuple-element.94), channel_id=1, source_target_pairs={{0,16},{4,20},{8,24},{12,28},{16,0},{20,4},{24,8},{28,12},{1,17},{... | collective-permute-start | bytes 442376 | tf_op jit(solution)/shard_map/ppermute | solution.py:323
  86.7 6.2 %collective-permute-start.23 = (bf16[1,64,288]{2,1,0:T(8,128)(2,1)S(1)}, bf16[1,64,288]{2,1,0:T(8,128)(2,1)S(1)}, u32[]{:S(2)}, u32[]{:S(2)}) collective-permute-start(bf16[1,64,288]{2,1,0:T(8,128)(2,1)S(1)} %get-tuple-element.86), channel_id=1, source_target_pairs={{0,16},{4,20},{8,24},{12,28},{16,0},{20,4},{24,8},{28,12},{1,17},{... | collective-permute-start | bytes 110600 | tf_op jit(solution)/shard_map/ppermute | solution.py:323

commit v3 on v2

--- a/solution.py
+++ b/solution.py
@@ -24,10 +24,14 @@
             in_specs=[SMEM] * scalars + [VMEM] * (len(args) - scalars - far) + [FAR] * far,
             out_specs=[VMEM] * len(outs),
             scratch_shapes=list(scratch),
+            cost_estimate=pl.CostEstimate(flops=COST[name], bytes_accessed=0, transcendentals=0),
             compiler_params=pltpu.CompilerParams(vmem_limit_bytes=grant * 2**20),
         )(*args)
 
     return run
+
+
+COST = {"edges": 4107269028, "own": 657163044, "finish": 1150035328, "back": 4600141312, "first": 24202651983, "turn": 2957233700, "gradsecond": 4107269028, "dpre": 1314326089, "gradfirst": 2464361417, "second": 4435850551, "add": 1150035328, "meet": 1150035328, "last": 1150035328}
 
 
 def like(shape, dtype):
@@ -66,18 +70,22 @@
 
 
 def edge_kernel(height, width, s_ref, *refs):
-    far, (first_ref, second_ref), near, sems = refs[:5], refs[5:7], refs[7:12], refs[12]
+    far, (first_ref, second_ref, side_a, side_b), near, sems = refs[:6], refs[6:10], refs[10:16], refs[16]
     copies = [pltpu.make_async_copy(a, b, sems.at[n]) for n, (a, b) in enumerate(zip(far, near))]
     for copy in copies:
         copy.start()
     for copy in copies:
         copy.wait()
-    feat_ref, row_ref, col_ref, index_ref, mask_ref = near
+    feat_ref, row_ref, col_ref, index_ref, mask_ref, cot_ref = near
+    up = lax.rem(lax.axis_index("lat"), 2) == 0
+    low, high = cot_ref[:width], cot_ref[(height - 1) * width :]
+    side_a[...] = jnp.where(up, high, low)
+    side_b[...] = jnp.where(up, low, high)
     slots, channels = feat_ref.shape
     factor = column_factor(col_ref, width)
     entries = index_ref.shape[1]
     slot = lax.broadcasted_iota(jnp.int32, (slots, entries), 0)
-    live = slot < s_ref[1]
+    live = slot < s_ref[0, 0]
     feat = feat_ref[...]
     totals = []
     for side in range(2):
@@ -88,7 +96,7 @@
         weights = cell_weights(factor, row_ref, [float(offset + i) for i in range(height)])
         totals.append(dot(weights, values.astype(BF16)))
     for out_ref, one, other in ((first_ref, 1, 0), (second_ref, 0, 1)):
-        total = jnp.where(s_ref[2] == 1, totals[one], totals[other])
+        total = jnp.where(up, totals[one], totals[other])
         out_ref[: height * width] = total[:, :channels].astype(BF16)
         for i in range(height):
             turned = total[i * width : (i + 1) * width, channels:].T[:16]
@@ -97,7 +105,7 @@
 
 def own_kernel(height, width, s_ref, feat_ref, row_ref, col_ref, numer_ref, denom_ref):
     slots, channels = feat_ref.shape
-    live = lax.broadcasted_iota(jnp.int32, (slots, channels), 0) < s_ref[1]
+    live = lax.broadcasted_iota(jnp.int32, (slots, channels), 0) < s_ref[0, 0]
     values = jnp.concatenate([jnp.where(live, feat_ref[...], 0.0), live.astype(F32)], axis=1)
     weights = cell_weights(column_factor(col_ref, width), row_ref, [float(i) for i in range(height)])
     total = dot(weights, values.astype(BF16))
@@ -136,8 +144,8 @@
     return below, above
 
 
-def first_kernel(height, width, offsets, s_ref, own_ref, a_ref, b_ref, w_near, w_far, cot_ref, other_ref, *refs):
-    pre_ref, h1_ref, edge_ref, near_ref, pair_ref, side_a, side_b, w_full = refs
+def first_kernel(height, width, offsets, s_ref, own_ref, a_ref, b_ref, w_near, w_far, *refs):
+    pre_ref, h1_ref, edge_ref, near_ref, w_full = refs
     channels = own_ref.shape[1]
     count, piece, hidden = w_near.shape
     for place, offset in enumerate(offsets):
@@ -158,17 +166,11 @@
     near = grid[width:-width]
     for i in range(rows):
         near_ref[:, i * channels : (i + 1) * channels] = near[i * width : (i + 1) * width]
-    for n, ref in enumerate((cot_ref, other_ref)):
-        pair_ref[n] = ref[...]
-        low, high = ref[:width], ref[(height - 1) * width :]
-        side_a[n * width : (n + 1) * width] = jnp.where(s_ref[2] == 1, high, low)
-        side_b[n * width : (n + 1) * width] = jnp.where(s_ref[2] == 1, low, high)
-
-
-def wide_rows(s_ref, width, pair_ref, a_ref, b_ref, n):
-    rows = slice(n * width, (n + 1) * width)
-    below, above = side_rows(s_ref, a_ref[rows], b_ref[rows])
-    return jnp.concatenate([below, pair_ref[n], above], axis=0)
+
+
+def wide_rows(s_ref, width, cot_ref, side_ref):
+    below, above = side_rows(s_ref, side_ref[:width], side_ref[width:])
+    return jnp.concatenate([below, cot_ref[...], above], axis=0)
 
 
 def chunk_place(s_ref, step, per_group, per_block):
@@ -177,13 +179,15 @@
     return block // 3, block % 3, chunk % per_block
 
 
-def back_kernel(height, width, chunk, s_ref, pair_ref, a_ref, b_ref, w_ref, own_ref, other_ref, moved_ref):
+def back_kernel(height, width, chunk, s_ref, cot_ref, cot_got, side_ref, side_got, w_ref, own_ref, other_ref, stack_ref, moved_ref):
     hidden = w_ref.shape[1]
     halves = hidden // chunk
     cells = height * width
     per_group = w_ref.shape[0] // chunk
+    for place, ref in enumerate((cot_ref, cot_got, side_ref, side_got)):
+        stack_ref[place] = ref[...]
     for member, out_ref in enumerate((own_ref, other_ref)):
-        grid = wide_rows(s_ref, width, pair_ref, a_ref, b_ref, member)
+        grid = wide_rows(s_ref, width, (cot_ref, cot_got)[member], (side_ref, side_got)[member])
         for dx in range(3):
             moved_ref[member, dx] = shifted(grid, 1 - dx, width)
         totals = [jnp.zeros((cells, chunk), F32) for _ in range(halves)]
@@ -228,17 +232,19 @@
         out_ref[hidden + half * width : hidden + (half + 1) * width] = near_ref[:, half * cells : (half + 1) * cells]
 
 
-def turn_kernel(height, width, rows_out, s_ref, near_pair, near_a, near_b, far_pair, far_a, far_b, out_ref, wide_ref):
-    count, cells, hidden = near_pair.shape
+def turn_kernel(height, width, rows_out, s_ref, *refs):
+    near_ref, far_ref, out_ref, wide_ref = refs
+    times, count = wide_ref.shape[0], wide_ref.shape[0] // 2
+    _, cells, hidden = near_ref.shape
     first = (s_ref[5] * rows_out) // hidden
-    for t in range(2 * count):
-        refs = (near_pair, near_a, near_b) if t < count else (far_pair, far_a, far_b)
-        wide_ref[t] = wide_rows(s_ref, width, *refs, t % count)
+    for t in range(times):
+        ref = (near_ref, far_ref)[t // count]
+        wide_ref[t] = wide_rows(s_ref, width, ref.at[t % count], ref.at[count + t % count])
     for dx in range(3):
         j = lax.rem(dx + 3 - lax.rem(first, 3), 3)
         dy = jnp.minimum(first + j, 8) // 3
         rows = pl.ds(pl.multiple_of((2 - dy) * width, width), cells)
-        for t in range(2 * count):
+        for t in range(times):
             x = shifted(wide_ref[t, rows], 1 - dx, width)
             out_ref[j, :, t * cells : (t + 1) * cells] = x.astype(F32).T.astype(BF16)
 
@@ -384,30 +390,44 @@
 
     feat, row, col = obs_feat[0], obs_row, obs_col
     payload = like((height * (width + 16), channels), BF16)
-    observed = [feat, row, col, edge_index[0, 0], edge_mask[0, 0]]
-    edges = call(
+    observed = [feat, row, col, edge_index[0, 0], edge_mask[0, 0], cot]
+    side = like((width, hidden), BF16)
+    *edges, side_a, side_b = call(
         functools.partial(edge_kernel, height, width),
         "edges",
-        [payload, payload],
+        [payload, payload, side, side],
         scratch=[pltpu.VMEM(v.shape, v.dtype) for v in observed] + [pltpu.SemaphoreType.DMA((len(observed),))],
         far=len(observed),
         grant=60,
-    )(scalars, *observed)
-    w_got, cot_got = swap(w_first, "dp", outer), swap(cot, "dp", outer)
+    )(counts, *observed)
+    cot_got, w_got, w_other = swap(cot, "dp", outer), swap(w_first, "dp", outer), swap(w_second, "dp", 1)
+    side = jnp.concatenate(with_partners(side_a, side_b), axis=0)
     from_first, from_second = with_partners(*edges)
     numer, denom = call(functools.partial(own_kernel, height, width), "own", [like((cells, channels), F32)] * 2)(
-        after(scalars, edges[0]), feat, row, col
+        after(counts, (side, w_other)), feat, row, col
     )
     h0 = call(functools.partial(finish_kernel, height, width), "finish", [like((cells, channels), BF16)])(
-        after(scalars, w_got), numer, denom, from_first, from_second
+        scalars, numer, denom, from_first, from_second
     )[0]
     h0_first, h0_second = with_partners(h0, h0)
-
-    w_near = jnp.stack([w_first, w_got])
+    side_got = swap(side, "dp", outer)
+    lower = member % 2 == 0
+    w_two = jnp.concatenate([jnp.where(lower, w_second, w_other), jnp.where(lower, w_other, w_second)], axis=0)
+    w_two = after(w_two, h0)
+    chunk = math.gcd(w_two.shape[0], hidden)
+    wide_cells = (height + 2) * width
+    partial_outs = [like((cells, hidden), F32), like((cells, hidden), BF16)]
+    back, back_other, stack = call(
+        functools.partial(back_kernel, height, width, chunk),
+        "back",
+        partial_outs + [like((4, cells, hidden), BF16)],
+        scratch=[pltpu.VMEM((2, 3, wide_cells, hidden), BF16)],
+    )(after(scalars, h0), cot, cot_got, side, side_got, w_two)
+    back_got = swap(back_other, "dp", outer)
+
+    w_near = jnp.stack([w_first, after(w_got, h0)])
     w_far = swap(w_near, "dp", 1)
-    w_other = swap(after(w_second, h0), "dp", 1)
-    side = like((2 * width, hidden), BF16)
-    pre1, h1, edge, h0_near, cot_pair, side_a, side_b = call(
+    pre1, h1, edge, h0_near = call(
         functools.partial(first_kernel, height, width, distances([outer, 1])),
         "first",
         [
@@ -415,31 +435,12 @@
             like((cells, hidden), BF16),
             side,
             like((width, (height + 2) * channels), BF16),
-            like((2, cells, hidden), BF16),
-            side,
-            side,
         ],
         scratch=[pltpu.VMEM((n_dp * w_first.shape[0], hidden), BF16)],
-    )(after(scalars, w_other), h0, h0_first, h0_second, w_near, w_far, cot, cot_got)
-
-    lower = member % 2 == 0
-    w_other = after(w_other, h1)
-    w_two = jnp.concatenate([jnp.where(lower, w_second, w_other), jnp.where(lower, w_other, w_second)], axis=0)
+    )(after(scalars, back), h0, h0_first, h0_second, w_near, w_far)
+
     h1_got = swap(h1, "dp", outer)
-    got_a, got_b = with_partners(side_a, side_b)
-    pair_far = swap(cot_pair, "dp", 1)
-    h1_got, got_a, got_b, pair_far, w_two = lax.optimization_barrier((h1_got, got_a, got_b, pair_far, w_two))
-    chunk = math.gcd(w_two.shape[0], hidden)
-    wide_cells = (height + 2) * width
-    partial_outs = [like((cells, hidden), F32), like((cells, hidden), BF16)]
-    back, back_other = call(
-        functools.partial(back_kernel, height, width, chunk),
-        "back",
-        partial_outs,
-        scratch=[pltpu.VMEM((2, 3, wide_cells, hidden), BF16)],
-    )(scalars, cot_pair, got_a, got_b, w_two)
-    back_got = swap(back_other, "dp", outer)
-    h1_far, h1_far_got, far_a, far_b = [swap(v, "dp", 1) for v in (h1, h1_got, got_a, got_b)]
+    h1_far, h1_far_got, stack_far = [swap(v, "dp", 1) for v in (h1, h1_got, stack)]
 
     rows_two, rows_one = w_second.shape[0], w_first.shape[0]
     part = hidden // n_lat
@@ -448,7 +449,7 @@
         "turn",
         [like((3, hidden, n_dp * cells), BF16)],
         scratch=[pltpu.VMEM((n_dp, wide_cells, hidden), BF16)],
-    )(after(scalars, back), cot_pair, got_a, got_b, pair_far, far_a, far_b)[0]
+    )(after(scalars, (h1, back_got)), stack, stack_far)[0]
     piece = like((n_lat // 2, part // 2, rows_two), BF16)
     keep_one, send_one, keep_two, send_two = call(
         functools.partial(grad_second_kernel, rows_two, 3, n_lat),
@@ -456,6 +457,9 @@
         [piece] * 4,
         scratch=[pltpu.VMEM((hidden, 3 * hidden), F32)],
     )(scalars, turned, h1, h1_got, h1_far, h1_far_got)
+    sent = call(dpre_kernel, "dpre", [like((hidden + (height + 2) // height * width, cells), BF16)])(
+        after(scalars, keep_one), pre1, cot, h0_near, back, back_got
+    )[0]
     streams = [(keep_one, swap(send_one, "lat", 1)), (keep_two, swap(send_two, "lat", 2))]
     offsets = [[k for k in range(n_lat) if not k & bit] for bit in (1, 2)]
     ((stay_one, go_one), (stay_two, go_two)), _ = add_step(streams, offsets, (2, 1))
@@ -465,24 +469,22 @@
     )
     grad_second = finished(stay, swap(go, "lat", 4), list(range(0, n_lat, 8)), lat_bits[3:])
 
-    sent = call(dpre_kernel, "dpre", [like((hidden + (height + 2) // height * width, cells), BF16)])(
-        after(scalars, keep_one), pre1, cot, h0_near, back, back_got
-    )[0]
     keep, send = call(
         functools.partial(grad_first_kernel, height, width, rows_one, n_lat, outer),
         "gradfirst",
         [like((n_lat, part, rows_one), BF16)] * 2,
         scratch=[pltpu.VMEM((2, wide_cells, channels), BF16)],
     )(scalars, sent, swap(sent, "dp", 1))
-    grad_first = finished(keep, swap(send, "dp", outer), list(range(n_lat)), lat_bits)
-
-    edge_got = swap(after(edge, send_one), "dp", outer)
+    first_got = swap(send, "dp", outer)
+    grad_first = finished(after(keep, streams), first_got, list(range(n_lat)), lat_bits)
+
+    edge_got = swap(after(edge, send), "dp", outer)
     second, second_other = call(
         functools.partial(second_kernel, height, width, chunk),
         "second",
         partial_outs,
         scratch=[pltpu.VMEM((2, 3, hidden // chunk, wide_cells, chunk), BF16)],
-    )(scalars, h1, h1_got, edge, edge_got, w_two)
+    )(after(scalars, first_got), h1, h1_got, edge, edge_got, w_two)
     encoded = (second + swap(second_other, "dp", outer).astype(F32)).astype(BF16).reshape(1, height, width, hidden)
     return encoded, grad_first, grad_second
 

time: 93.9 us -> 86.6 us (0.922)
  starting transfers between devices: 42.5 us -> 35 us
  waiting for transfers between devices: 23.2 us -> 29.4 us
  local copies, waits for them, and re-layouts: 3.7 us -> 0.14 us
  other arithmetic: 2.42 us -> 1.15 us
  Pallas kernels: 20.2 us -> 19.1 us
    ppermute x26 -> x25, starting transfers between devices: 39.5 us -> 32.1 us  [swap(): lax.ppermute(value, axis, [(i, i ^ bit) for i in range(lax.axis_size(axis...]
    ppermute x26 -> x25, waiting for transfers between devices: 23.2 us -> 29.4 us  [swap(): lax.ppermute(value, axis, [(i, i ^ bit) for i in range(lax.axis_size(axis...]
    unnamed x16 -> x15, local copies, waits for them, and re-layouts: 3.07 us -> 0.04 us
    select_n x1, other arithmetic: 1.43 us -> 0.16 us  [local(): jnp.where(lower, w_second, w_other)]
    pallas_call x17, Pallas kernels: 20.2 us -> 19.1 us  [run(): pl.pallas_call(kernel, name=name, out_shape=outs, in_specs=[SMEM] * scala...]
  transfers between devices with their start and end apart: 29 -> 28, of which waited for: 10 -> 11; matrix products, arithmetic and copies ran while one was open for 3% -> 1% of each run, Pallas kernels for 18% -> 18%
where the time goes in v3:
time: 86.6 us; the launch traced here: 86.4 us
  starting transfers between devices  35 us (40%)
  waiting for transfers between devices  29.4 us (34%)
  Pallas kernels  19.1 us (22%)
  between operations  1.62 us (2%)
  other arithmetic  1.15 us (1%)
    ppermute x25, starting transfers between devices, swap(): lax.ppermute(value, axis, [(i, i ^ bit) for i in range(lax.axis_size(axis...  32.1 us
    ppermute x25, waiting for transfers between devices, swap(): lax.ppermute(value, axis, [(i, i ^ bit) for i in range(lax.axis_size(axis...  29.4 us
    pallas_call x17, Pallas kernels, run(): pl.pallas_call(kernel, name=name, out_shape=outs, in_specs=[SMEM] * scala...  19.1 us
    ppermute x3, starting transfers between devices, with_partners(): return (swap(first, 'lat', 1), lax.ppermute(second, 'lat', pairs))  2.86 us
  transfers between devices with their start and end apart: 28, of which 11 were waited for; matrix products, arithmetic and copies ran while one was open for 1% of the time, Pallas kernels for 18%

profile of v3, /device:TPU:0, one launch (start us, length us, event | category | flops | bytes accessed | tf_op | source)
XLA Modules:
  0.0 86.4 jit_solution(8580597647063066880)
XLA Ops:
  0.6 0.5 collective-permute-start.2
  1.8 2.6 %edges.1 = (bf16[288,128]{1,0:T(8,128)(2,1)}, bf16[288,128]{1,0:T(8,128)(2,1)}, bf16[128,512]{1,0:T(8,128)(2,1)}, bf16[128,512]{1,0:T(8,128)(2,1)}) custom-call(s32[1,1]{1,0:T(1,128)} %copy.13.s_ref, f32[1024,128]{1,0:T(8,128)} %bitcast.17, f32[1,1024]{1,0:T(1,128)} %row_ref.1, f32[1,1024]{1,0:T(1,128)} %col_ref.1, s32[2,128]{1,0:T(2,128)} %bitcast.26, ...), custom_call_target="tpu_custom_call" | custom-call | flops 4107269120 | tf_op jit(solution)/shard_map/edges/pallas_call | solution.py:20
  4.5 2.6 %collective-permute-start.3 = (bf16[288,128]{1,0:T(8,128)(2,1)}, bf16[288,128]{1,0:T(8,128)(2,1)S(1)}, u32[]{:S(2)}, u32[]{:S(2)}) collective-permute-start(bf16[288,128]{1,0:T(8,128)(2,1)} %get-tuple-element.51), channel_id=1, source_target_pairs={{0,4},{4,0},{8,12},{12,8},{16,20},{20,16},{24,28},{28,24},{1,5},{5... | collective-permute-start | bytes 221192 | tf_op jit(solution)/shard_map/ppermute | solution.py:329
  7.1 1.5 %collective-permute-start.4 = (bf16[288,128]{1,0:T(8,128)(2,1)}, bf16[288,128]{1,0:T(8,128)(2,1)S(1)}, u32[]{:S(2)}, u32[]{:S(2)}) collective-permute-start(bf16[288,128]{1,0:T(8,128)(2,1)} %get-tuple-element.52), channel_id=1, source_target_pairs={{4,8},{12,16},{20,24},{8,4},{16,12},{24,20},{0,0},{28,28},{5,9},{1... | collective-permute-start | bytes 221192 | tf_op jit(solution)/shard_map/ppermute | solution.py:347
  8.6 1.5 %collective-permute-start.5 = (bf16[256,512]{1,0:T(8,128)(2,1)S(1)}, bf16[256,512]{1,0:T(8,128)(2,1)S(1)}, u32[]{:S(2)}, u32[]{:S(2)}) collective-permute-start(bf16[256,512]{1,0:T(8,128)(2,1)S(1)} %bitcast.20), channel_id=1, source_target_pairs={{0,2},{1,3},{2,0},{3,1},{4,6},{5,7},{6,4},{7,5},{8,10},{9,11},{10,... | collective-permute-start | bytes 786440 | tf_op jit(solution)/shard_map/ppermute | solution.py:329
  10.1 3.5 %collective-permute-start = (bf16[128,512]{1,0:T(8,128)(2,1)}, bf16[128,512]{1,0:T(8,128)(2,1)S(1)}, u32[]{:S(2)}, u32[]{:S(2)}) collective-permute-start(bf16[128,512]{1,0:T(8,128)(2,1)} %get-tuple-element.46), channel_id=1, source_target_pairs={{0,4},{4,0},{8,12},{12,8},{16,20},{20,16},{24,28},{28,24},{1,5},{5... | collective-permute-start | bytes 393224 | tf_op jit(solution)/shard_map/ppermute | solution.py:329
  13.6 0.3 own.1
  14.1 0.7 collective-permute-start.1
  14.8 0.6 collective-permute-start.9
  15.4 0.7 finish.1.own_ref
  16.0 1.1 %collective-permute-done = bf16[128,512]{1,0:T(8,128)(2,1)S(1)} collective-permute-done((bf16[128,512]{1,0:T(8,128)(2,1)}, bf16[128,512]{1,0:T(8,128)(2,1)S(1)}, u32[]{:S(2)}, u32[]{:S(2)}) %collective-permute-start) | collective-permute-done | bytes 131104 | tf_op jit(solution)/shard_map/ppermute | solution.py:329
  17.1 3.3 %collective-permute-start.7 = (bf16[256,128]{1,0:T(8,128)(2,1)S(1)}, bf16[256,128]{1,0:T(8,128)(2,1)S(1)}, u32[]{:S(2)}, u32[]{:S(2)}) collective-permute-start(bf16[256,128]{1,0:T(8,128)(2,1)S(1)} %finish.1.own_ref), channel_id=1, source_target_pairs={{0,4},{4,0},{8,12},{12,8},{16,20},{20,16},{24,28},{28,24},{1,5},{5... | collective-permute-start | bytes 196616 | tf_op jit(solution)/shard_map/ppermute | solution.py:329
  20.4 0.7 collective-permute-start.8
  21.1 2.2 %collective-permute-done.9 = bf16[288,512]{1,0:T(8,128)(2,1)S(1)} collective-permute-done((bf16[288,512]{1,0:T(8,128)(2,1)S(1)}, bf16[288,512]{1,0:T(8,128)(2,1)S(1)}, u32[]{:S(2)}, u32[]{:S(2)}) %collective-permute-start.9) | collective-permute-done | bytes 294944 | tf_op jit(solution)/shard_map/ppermute | solution.py:329
  23.3 1.5 %collective-permute-start.6 = (bf16[256,512]{1,0:T(8,128)(2,1)S(1)}, bf16[256,512]{1,0:T(8,128)(2,1)S(1)}, u32[]{:S(2)}, u32[]{:S(2)}) collective-permute-start(bf16[256,512]{1,0:T(8,128)(2,1)S(1)} %constant_dynamic-update-slice_fusion.side_ref), channel_id=1, source_target_pairs={{0,2},{1,3},{2,0},{3,1},{4,6},{5,7},{6,4},{7,5},{8,10},{9,11},{10,... | collective-permute-start | bytes 786440 | tf_op jit(solution)/shard_map/ppermute | solution.py:329
  25.4 5.4 %collective-permute-done.6.side_got = bf16[256,512]{1,0:T(8,128)(2,1)S(1)} collective-permute-done((bf16[256,512]{1,0:T(8,128)(2,1)S(1)}, bf16[256,512]{1,0:T(8,128)(2,1)S(1)}, u32[]{:S(2)}, u32[]{:S(2)}) %collective-permute-start.6) | collective-permute-done | bytes 262176 | tf_op jit(solution)/shard_map/ppermute | solution.py:329
  30.7 2.9 %back.1 = (f32[256,512]{1,0:T(8,128)S(1)}, bf16[256,512]{1,0:T(8,128)(2,1)S(1)}, bf16[4,256,512]{2,1,0:T(8,128)(2,1)S(1)}) custom-call(s32[7]{0:T(128)S(1)} %stack.44.s_ref, bf16[256,512]{1,0:T(8,128)(2,1)S(1)} %bitcast.21, bf16[256,512]{1,0:T(8,128)(2,1)S(1)} %collective-permute-done.5.cot_got, ...), custom_call_target="tpu_custom_call" | custom-call | flops 4600141312 | tf_op jit(solution)/shard_map/back/pallas_call | solution.py:20
  33.6 1.8 %collective-permute-start.11 = (bf16[256,512]{1,0:T(8,128)(2,1)S(1)}, bf16[256,512]{1,0:T(8,128)(2,1)S(1)}, u32[]{:S(2)}, u32[]{:S(2)}) collective-permute-start(bf16[256,512]{1,0:T(8,128)(2,1)S(1)} %get-tuple-element.59), channel_id=1, source_target_pairs={{0,2},{1,3},{2,0},{3,1},{4,6},{5,7},{6,4},{7,5},{8,10},{9,11},{10,... | collective-permute-start | bytes 786440 | tf_op jit(solution)/shard_map/ppermute | solution.py:329
  35.4 1.5 %first.1 = (f32[256,512]{1,0:T(8,128)S(1)}, bf16[256,512]{1,0:T(8,128)(2,1)S(1)}, bf16[256,512]{1,0:T(8,128)(2,1)S(1)}, bf16[128,512]{1,0:T(8,128)(2,1)S(1)}) custom-call(s32[7]{0:T(128)S(1)} %stack.44.s_ref, bf16[256,128]{1,0:T(8,128)(2,1)S(1)} %finish.1.own_ref, bf16[256,128]{1,0:T(8,128)(2,1)S(1)} %collective-permute-done.7.a_ref, ...), custom_call_target="tpu_custom_call" | custom-call | flops 24202651648 | tf_op jit(solution)/shard_map/first/pallas_call | solution.py:20
  37.0 0.3 collective-permute-start.13
  37.3 0.3 collective-permute-start.14
  37.6 3.7 %collective-permute-done.11.got_ref = bf16[256,512]{1,0:T(8,128)(2,1)S(1)} collective-permute-done((bf16[256,512]{1,0:T(8,128)(2,1)S(1)}, bf16[256,512]{1,0:T(8,128)(2,1)S(1)}, u32[]{:S(2)}, u32[]{:S(2)}) %collective-permute-start.11) | collective-permute-done | bytes 262176 | tf_op jit(solution)/shard_map/ppermute | solution.py:329
  41.3 4.7 %collective-permute-done.13.refs_1_.mid_two = bf16[256,512]{1,0:T(8,128)(2,1)S(1)} collective-permute-done((bf16[256,512]{1,0:T(8,128)(2,1)S(1)}, bf16[256,512]{1,0:T(8,128)(2,1)S(1)}, u32[]{:S(2)}, u32[]{:S(2)}) %collective-permute-start.13) | collective-permute-done | bytes 262176 | tf_op jit(solution)/shard_map/ppermute | solution.py:329
  46.0 1.8 %turn.1.turned_ref = bf16[3,512,1024]{2,1,0:T(8,128)(2,1)S(1)} custom-call(s32[7]{0:T(128)S(1)} %stack.44.s_ref, bf16[4,256,512]{2,1,0:T(8,128)(2,1)S(1)} %get-tuple-element.61.refs_0_, bf16[4,256,512]{2,1,0:T(8,128)(2,1)S(1)} %collective-permute-done.12.refs_1_), custom_call_target="tpu_custom_call" | custom-call | flops 2957233664 | tf_op jit(solution)/shard_map/turn/pallas_call | solution.py:20
  47.8 2.5 %gradsecond.1 = (bf16[4,32,1152]{2,1,0:T(8,128)(2,1)S(1)}, bf16[4,32,1152]{2,1,0:T(8,128)(2,1)S(1)}, bf16[4,32,1152]{2,1,0:T(8,128)(2,1)S(1)}, bf16[4,32,1152]{2,1,0:T(8,128)(2,1)S(1)}) custom-call(s32[7]{0:T(128)S(1)} %stack.44.s_ref, bf16[3,512,1024]{2,1,0:T(8,128)(2,1)S(1)} %turn.1.turned_ref, bf16[256,512]{1,0:T(8,128)(2,1)S(1)} %get-tuple-element.58.refs_0_.mid_one, ...), custom_call_target="tpu_custom_call" | custom-call | flops 4107269120 | tf_op jit(solution)/shard_map/gradsecond/pallas_call | solution.py:20
  50.3 0.8 dpre.1.refs_0_
  51.1 0.6 collective-permute-start.16
  51.7 2.5 %collective-permute-start.20 = (bf16[4,32,1152]{2,1,0:T(8,128)(2,1)S(1)}, bf16[4,32,1152]{2,1,0:T(8,128)(2,1)S(1)}, u32[]{:S(2)}, u32[]{:S(2)}) collective-permute-start(bf16[4,32,1152]{2,1,0:T(8,128)(2,1)S(1)} %get-tuple-element.73), channel_id=1, source_target_pairs={{0,4},{4,0},{8,12},{12,8},{16,20},{20,16},{24,28},{28,24},{1,5},{5... | collective-permute-start | bytes 884744 | tf_op jit(solution)/shard_map/ppermute | solution.py:329
  54.2 1.6 %collective-permute-start.21 = (bf16[4,32,1152]{2,1,0:T(8,128)(2,1)S(1)}, bf16[4,32,1152]{2,1,0:T(8,128)(2,1)S(1)}, u32[]{:S(2)}, u32[]{:S(2)}) collective-permute-start(bf16[4,32,1152]{2,1,0:T(8,128)(2,1)S(1)} %get-tuple-element.75), channel_id=1, source_target_pairs={{0,8},{4,12},{8,0},{12,4},{16,24},{20,28},{24,16},{28,20},{1,9},{5... | collective-permute-start | bytes 884744 | tf_op jit(solution)/shard_map/ppermute | solution.py:329
  55.8 1.5 %gradfirst.1 = (bf16[8,64,288]{2,1,0:T(8,128)(2,1)S(1)}, bf16[8,64,288]{2,1,0:T(8,128)(2,1)S(1)}) custom-call(s32[7]{0:T(128)S(1)} %stack.44.s_ref, bf16[768,256]{1,0:T(8,128)(2,1)S(1)} %dpre.1.refs_0_, bf16[768,256]{1,0:T(8,128)(2,1)S(1)} %collective-permute-done.16.refs_1_), custom_call_target="tpu_custom_call" | custom-call | flops 2464361472 | tf_op jit(solution)/shard_map/gradfirst/pallas_call | solution.py:20
  57.2 1.4 %collective-permute-start.17 = (bf16[8,64,288]{2,1,0:T(8,128)(2,1)S(1)}, bf16[8,64,288]{2,1,0:T(8,128)(2,1)S(1)}, u32[]{:S(2)}, u32[]{:S(2)}) collective-permute-start(bf16[8,64,288]{2,1,0:T(8,128)(2,1)S(1)} %get-tuple-element.66), channel_id=1, source_target_pairs={{0,2},{1,3},{2,0},{3,1},{4,6},{5,7},{6,4},{7,5},{8,10},{9,11},{10,... | collective-permute-start | bytes 884744 | tf_op jit(solution)/shard_map/ppermute | solution.py:329
  58.6 2.8 %collective-permute-done.20.refs_1_ = bf16[4,32,1152]{2,1,0:T(8,128)(2,1)S(1)} collective-permute-done((bf16[4,32,1152]{2,1,0:T(8,128)(2,1)S(1)}, bf16[4,32,1152]{2,1,0:T(8,128)(2,1)S(1)}, u32[]{:S(2)}, u32[]{:S(2)}) %collective-permute-start.20) | collective-permute-done | bytes 294944 | tf_op jit(solution)/shard_map/ppermute | solution.py:329
  61.4 1.5 %collective-permute-done.21.refs_3_ = bf16[4,32,1152]{2,1,0:T(8,128)(2,1)S(1)} collective-permute-done((bf16[4,32,1152]{2,1,0:T(8,128)(2,1)S(1)}, bf16[4,32,1152]{2,1,0:T(8,128)(2,1)S(1)}, u32[]{:S(2)}, u32[]{:S(2)}) %collective-permute-start.21) | collective-permute-done | bytes 294944 | tf_op jit(solution)/shard_map/ppermute | solution.py:329
  63.0 1.6 %collective-permute-start.25 = (bf16[2,32,1152]{2,1,0:T(8,128)(2,1)S(1)}, bf16[2,32,1152]{2,1,0:T(8,128)(2,1)S(1)}, u32[]{:S(2)}, u32[]{:S(2)}) collective-permute-start(bf16[2,32,1152]{2,1,0:T(8,128)(2,1)S(1)} %get-tuple-element.84), channel_id=1, source_target_pairs={{0,8},{4,12},{8,0},{12,4},{16,24},{20,28},{24,16},{28,20},{1,9},{5... | collective-permute-start | bytes 442376 | tf_op jit(solution)/shard_map/ppermute | solution.py:329
  64.7 0.4 collective-permute-start.26
  65.0 1.4 %collective-permute-start.18 = (bf16[256,512]{1,0:T(8,128)(2,1)S(1)}, bf16[256,512]{1,0:T(8,128)(2,1)S(1)}, u32[]{:S(2)}, u32[]{:S(2)}) collective-permute-start(bf16[256,512]{1,0:T(8,128)(2,1)S(1)} %get-tuple-element.69.edge_one), channel_id=1, source_target_pairs={{0,2},{1,3},{2,0},{3,1},{4,6},{5,7},{6,4},{7,5},{8,10},{9,11},{10,... | collective-permute-start | bytes 786440 | tf_op jit(solution)/shard_map/ppermute | solution.py:329
  66.4 2.8 %collective-permute-done.17.refs_1_ = bf16[8,64,288]{2,1,0:T(8,128)(2,1)S(1)} collective-permute-done((bf16[8,64,288]{2,1,0:T(8,128)(2,1)S(1)}, bf16[8,64,288]{2,1,0:T(8,128)(2,1)S(1)}, u32[]{:S(2)}, u32[]{:S(2)}) %collective-permute-start.17) | collective-permute-done | bytes 294944 | tf_op jit(solution)/shard_map/ppermute | solution.py:329
  69.4 1.1 %collective-permute-done.26.got_two = bf16[2,32,1152]{2,1,0:T(8,128)(2,1)S(1)} collective-permute-done((bf16[2,32,1152]{2,1,0:T(8,128)(2,1)S(1)}, bf16[2,32,1152]{2,1,0:T(8,128)(2,1)S(1)}, u32[]{:S(2)}, u32[]{:S(2)}) %collective-permute-start.26) | collective-permute-done | bytes 147488 | tf_op jit(solution)/shard_map/ppermute | solution.py:329
  70.6 1.7 %collective-permute-start.27 = (bf16[1,64,1152]{2,1,0:T(8,128)(2,1)S(1)}, bf16[1,64,1152]{2,1,0:T(8,128)(2,1)S(1)}, u32[]{:S(2)}, u32[]{:S(2)}) collective-permute-start(bf16[1,64,1152]{2,1,0:T(8,128)(2,1)S(1)} %get-tuple-element.88), channel_id=1, source_target_pairs={{0,16},{4,20},{8,24},{12,28},{16,0},{20,4},{24,8},{28,12},{1,17},{... | collective-permute-start | bytes 442376 | tf_op jit(solution)/shard_map/ppermute | solution.py:329
  72.2 2.8 %collective-permute-done.22.refs_1_ = bf16[4,64,288]{2,1,0:T(8,128)(2,1)S(1)} collective-permute-done((bf16[4,64,288]{2,1,0:T(8,128)(2,1)S(1)}, bf16[4,64,288]{2,1,0:T(8,128)(2,1)S(1)}, u32[]{:S(2)}, u32[]{:S(2)}) %collective-permute-start.22) | collective-permute-done | bytes 147488 | tf_op jit(solution)/shard_map/ppermute | solution.py:329
  75.1 0.5 collective-permute-start.23
  75.6 2.7 %second.1 = (f32[256,512]{1,0:T(8,128)S(1)}, bf16[256,512]{1,0:T(8,128)(2,1)S(1)}) custom-call(s32[7]{0:T(128)S(1)} %stack.44.s_ref, bf16[256,512]{1,0:T(8,128)(2,1)S(1)} %get-tuple-element.58.refs_0_.mid_one, bf16[256,512]{1,0:T(8,128)(2,1)S(1)} %collective-permute-done.13.refs_1_.mid_two, bf16[256,512]{1,0:T(8,128)(2,1)S(1)} %get-tuple-element.69.edge_one, ...), custom_call_target="tpu_custom_call" | custom-call | flops 4435850752 | tf_op jit(solution)/shard_map/second/pallas_call | solution.py:20
  78.3 1.4 %collective-permute-start.19 = (bf16[256,512]{1,0:T(8,128)(2,1)S(1)}, bf16[256,512]{1,0:T(8,128)(2,1)S(1)}, u32[]{:S(2)}, u32[]{:S(2)}) collective-permute-start(bf16[256,512]{1,0:T(8,128)(2,1)S(1)} %get-tuple-element.71), channel_id=1, source_target_pairs={{0,2},{1,3},{2,0},{3,1},{4,6},{5,7},{6,4},{7,5},{8,10},{9,11},{10,... | collective-permute-start | bytes 786440 | tf_op jit(solution)/shard_map/ppermute | solution.py:329
  79.8 3.1 %collective-permute-start.24 = (bf16[1,64,288]{2,1,0:T(8,128)(2,1)S(1)}, bf16[1,64,288]{2,1,0:T(8,128)(2,1)S(1)}, u32[]{:S(2)}, u32[]{:S(2)}) collective-permute-start(bf16[1,64,288]{2,1,0:T(8,128)(2,1)S(1)} %get-tuple-element.82), channel_id=1, source_target_pairs={{0,16},{4,20},{8,24},{12,28},{16,0},{20,4},{24,8},{28,12},{1,17},{... | collective-permute-start | bytes 110600 | tf_op jit(solution)/shard_map/ppermute | solution.py:329
  82.9 0.7 last.3
  83.6 1.3 %collective-permute-done.24.got_ref = bf16[1,64,288]{2,1,0:T(8,128)(2,1)S(1)} collective-permute-done((bf16[1,64,288]{2,1,0:T(8,128)(2,1)S(1)}, bf16[1,64,288]{2,1,0:T(8,128)(2,1)S(1)}, u32[]{:S(2)}, u32[]{:S(2)}) %collective-permute-start.24) | collective-permute-done | bytes 36896 | tf_op jit(solution)/shard_map/ppermute | solution.py:329
  85.0 0.7 last.2
  85.6 0.8 add_convert_fusion
  (46 shorter events, 1.1 us)
Async XLA Ops:
  0.6 24.3 %collective-permute-start.2 = (bf16[1152,512]{1,0:T(8,128)(2,1)}, bf16[1152,512]{1,0:T(8,128)(2,1)S(1)}, u32[]{:S(2)}, u32[]{:S(2)}) collective-permute-start(bf16[1152,512]{1,0:T(8,128)(2,1)} %param.17), channel_id=1, source_target_pairs={{0,1},{1,0},{2,3},{3,2},{4,5},{5,4},{6,7},{7,6},{8,9},{9,8},{10,11... | collective-permute-start | bytes 3538952 | tf_op jit(solution)/shard_map/ppermute | solution.py:329
  1.8 6.8 %copy-start.1 = (bf16[1,2,128,512]{3,2,1,0:T(8,128)(2,1)S(1)}, bf16[1,2,128,512]{3,2,1,0:T(8,128)(2,1)}, u32[]{:S(2)}) copy-start(bf16[1,2,128,512]{3,2,1,0:T(8,128)(2,1)} %param.15) | copy-start | bytes 786436
  1.8 11.8 %copy-start = (f32[1,1024,128]{2,1,0:T(8,128)S(1)}, f32[1,1024,128]{2,1,0:T(8,128)}, u32[]{:S(2)}) copy-start(f32[1,1024,128]{2,1,0:T(8,128)} %param.9) | copy-start | bytes 1572868
  1.8 11.8 %copy-start.2 = (f32[1,1024]{1,0:T(1,128)S(1)}, f32[1,1024]{1,0:T(1,128)}, u32[]{:S(2)}) copy-start(f32[1,1024]{1,0:T(1,128)} %row_ref.1) | copy-start | bytes 12292
  1.8 11.8 %copy-start.3 = (f32[1,1024]{1,0:T(1,128)S(1)}, f32[1,1024]{1,0:T(1,128)}, u32[]{:S(2)}) copy-start(f32[1,1024]{1,0:T(1,128)} %col_ref.1) | copy-start | bytes 12292
  4.5 9.6 %collective-permute-start.3 = (bf16[288,128]{1,0:T(8,128)(2,1)}, bf16[288,128]{1,0:T(8,128)(2,1)S(1)}, u32[]{:S(2)}, u32[]{:S(2)}) collective-permute-start(bf16[288,128]{1,0:T(8,128)(2,1)} %get-tuple-element.51), channel_id=1, source_target_pairs={{0,4},{4,0},{8,12},{12,8},{16,20},{20,16},{24,28},{28,24},{1,5},{5... | collective-permute-start | bytes 221192 | tf_op jit(solution)/shard_map/ppermute | solution.py:329
  7.1 7.7 %collective-permute-start.4 = (bf16[288,128]{1,0:T(8,128)(2,1)}, bf16[288,128]{1,0:T(8,128)(2,1)S(1)}, u32[]{:S(2)}, u32[]{:S(2)}) collective-permute-start(bf16[288,128]{1,0:T(8,128)(2,1)} %get-tuple-element.52), channel_id=1, source_target_pairs={{4,8},{12,16},{20,24},{8,4},{16,12},{24,20},{0,0},{28,28},{5,9},{1... | collective-permute-start | bytes 221192 | tf_op jit(solution)/shard_map/ppermute | solution.py:347
  8.6 16.8 %collective-permute-start.5 = (bf16[256,512]{1,0:T(8,128)(2,1)S(1)}, bf16[256,512]{1,0:T(8,128)(2,1)S(1)}, u32[]{:S(2)}, u32[]{:S(2)}) collective-permute-start(bf16[256,512]{1,0:T(8,128)(2,1)S(1)} %bitcast.20), channel_id=1, source_target_pairs={{0,2},{1,3},{2,0},{3,1},{4,6},{5,7},{6,4},{7,5},{8,10},{9,11},{10,... | collective-permute-start | bytes 786440 | tf_op jit(solution)/shard_map/ppermute | solution.py:329
  10.1 4.0 %copy-start.6 = (bf16[128,512]{1,0:T(8,128)(2,1)S(1)}, bf16[128,512]{1,0:T(8,128)(2,1)}, u32[]{:S(2)}) copy-start(bf16[128,512]{1,0:T(8,128)(2,1)} %get-tuple-element.47) | copy-start | bytes 393220
  10.1 4.7 %copy-start.5 = (bf16[288,512]{1,0:T(8,128)(2,1)S(1)}, bf16[288,512]{1,0:T(8,128)(2,1)}, u32[]{:S(2)}) copy-start(bf16[288,512]{1,0:T(8,128)(2,1)} %param.16) | copy-start | bytes 884740
  10.1 7.0 %collective-permute-start = (bf16[128,512]{1,0:T(8,128)(2,1)}, bf16[128,512]{1,0:T(8,128)(2,1)S(1)}, u32[]{:S(2)}, u32[]{:S(2)}) collective-permute-start(bf16[128,512]{1,0:T(8,128)(2,1)} %get-tuple-element.46), channel_id=1, source_target_pairs={{0,4},{4,0},{8,12},{12,8},{16,20},{20,16},{24,28},{28,24},{1,5},{5... | collective-permute-start | bytes 393224 | tf_op jit(solution)/shard_map/ppermute | solution.py:329
  14.1 6.3 %collective-permute-start.1 = (bf16[128,512]{1,0:T(8,128)(2,1)S(1)}, bf16[128,512]{1,0:T(8,128)(2,1)S(1)}, u32[]{:S(2)}, u32[]{:S(2)}) collective-permute-start(bf16[128,512]{1,0:T(8,128)(2,1)S(1)} %copy-done.6), channel_id=1, source_target_pairs={{4,8},{12,16},{20,24},{8,4},{16,12},{24,20},{0,0},{28,28},{5,9},{1... | collective-permute-start | bytes 393224 | tf_op jit(solution)/shard_map/ppermute | solution.py:347
  14.8 8.6 %collective-permute-start.9 = (bf16[288,512]{1,0:T(8,128)(2,1)S(1)}, bf16[288,512]{1,0:T(8,128)(2,1)S(1)}, u32[]{:S(2)}, u32[]{:S(2)}) collective-permute-start(bf16[288,512]{1,0:T(8,128)(2,1)S(1)} %copy-done.5), channel_id=1, source_target_pairs={{0,2},{1,3},{2,0},{3,1},{4,6},{5,7},{6,4},{7,5},{8,10},{9,11},{10,... | collective-permute-start | bytes 884744 | tf_op jit(solution)/shard_map/ppermute | solution.py:329
  16.0 9.0 %copy-start.4 = (bf16[1152,512]{1,0:T(8,128)(2,1)S(1)}, bf16[1152,512]{1,0:T(8,128)(2,1)}, u32[]{:S(2)}) copy-start(bf16[1152,512]{1,0:T(8,128)(2,1)} %param.17) | copy-start | bytes 3538948
  17.1 18.3 %collective-permute-start.7 = (bf16[256,128]{1,0:T(8,128)(2,1)S(1)}, bf16[256,128]{1,0:T(8,128)(2,1)S(1)}, u32[]{:S(2)}, u32[]{:S(2)}) collective-permute-start(bf16[256,128]{1,0:T(8,128)(2,1)S(1)} %finish.1.own_ref), channel_id=1, source_target_pairs={{0,4},{4,0},{8,12},{12,8},{16,20},{20,16},{24,28},{28,24},{1,5},{5... | collective-permute-start | bytes 196616 | tf_op jit(solution)/shard_map/ppermute | solution.py:329
  20.4 15.0 %collective-permute-start.8 = (bf16[256,128]{1,0:T(8,128)(2,1)S(1)}, bf16[256,128]{1,0:T(8,128)(2,1)S(1)}, u32[]{:S(2)}, u32[]{:S(2)}) collective-permute-start(bf16[256,128]{1,0:T(8,128)(2,1)S(1)} %finish.1.own_ref), channel_id=1, source_target_pairs={{4,8},{12,16},{20,24},{8,4},{16,12},{24,20},{0,0},{28,28},{5,9},{1... | collective-permute-start | bytes 196616 | tf_op jit(solution)/shard_map/ppermute | solution.py:347
  23.3 7.4 %collective-permute-start.6 = (bf16[256,512]{1,0:T(8,128)(2,1)S(1)}, bf16[256,512]{1,0:T(8,128)(2,1)S(1)}, u32[]{:S(2)}, u32[]{:S(2)}) collective-permute-start(bf16[256,512]{1,0:T(8,128)(2,1)S(1)} %constant_dynamic-update-slice_fusion.side_ref), channel_id=1, source_target_pairs={{0,2},{1,3},{2,0},{3,1},{4,6},{5,7},{6,4},{7,5},{8,10},{9,11},{10,... | collective-permute-start | bytes 786440 | tf_op jit(solution)/shard_map/ppermute | solution.py:329
  24.9 10.5 %collective-permute-start.10 = (bf16[2,288,512]{2,1,0:T(8,128)(2,1)S(1)}, bf16[2,288,512]{2,1,0:T(8,128)(2,1)S(1)}, u32[]{:S(2)}, u32[]{:S(2)}) collective-permute-start(bf16[2,288,512]{2,1,0:T(8,128)(2,1)S(1)} %pad_maximum_fusion.1.w_near), channel_id=1, source_target_pairs={{0,1},{1,0},{2,3},{3,2},{4,5},{5,4},{6,7},{7,6},{8,9},{9,8},{10,11... | collective-permute-start | bytes 1769480 | tf_op jit(solution)/shard_map/ppermute | solution.py:329
  33.6 7.7 %collective-permute-start.11 = (bf16[256,512]{1,0:T(8,128)(2,1)S(1)}, bf16[256,512]{1,0:T(8,128)(2,1)S(1)}, u32[]{:S(2)}, u32[]{:S(2)}) collective-permute-start(bf16[256,512]{1,0:T(8,128)(2,1)S(1)} %get-tuple-element.59), channel_id=1, source_target_pairs={{0,2},{1,3},{2,0},{3,1},{4,6},{5,7},{6,4},{7,5},{8,10},{9,11},{10,... | collective-permute-start | bytes 786440 | tf_op jit(solution)/shard_map/ppermute | solution.py:329
  35.4 10.6 %collective-permute-start.12 = (bf16[4,256,512]{2,1,0:T(8,128)(2,1)S(1)}, bf16[4,256,512]{2,1,0:T(8,128)(2,1)S(1)}, u32[]{:S(2)}, u32[]{:S(2)}) collective-permute-start(bf16[4,256,512]{2,1,0:T(8,128)(2,1)S(1)} %get-tuple-element.61.refs_0_), channel_id=1, source_target_pairs={{0,1},{1,0},{2,3},{3,2},{4,5},{5,4},{6,7},{7,6},{8,9},{9,8},{10,11... | collective-permute-start | bytes 3145736 | tf_op jit(solution)/shard_map/ppermute | solution.py:329
  37.0 9.0 %collective-permute-start.13 = (bf16[256,512]{1,0:T(8,128)(2,1)S(1)}, bf16[256,512]{1,0:T(8,128)(2,1)S(1)}, u32[]{:S(2)}, u32[]{:S(2)}) collective-permute-start(bf16[256,512]{1,0:T(8,128)(2,1)S(1)} %get-tuple-element.58.refs_0_.mid_one), channel_id=1, source_target_pairs={{0,2},{1,3},{2,0},{3,1},{4,6},{5,7},{6,4},{7,5},{8,10},{9,11},{10,... | collective-permute-start | bytes 786440 | tf_op jit(solution)/shard_map/ppermute | solution.py:329
  37.3 10.5 %collective-permute-start.14 = (bf16[256,512]{1,0:T(8,128)(2,1)S(1)}, bf16[256,512]{1,0:T(8,128)(2,1)S(1)}, u32[]{:S(2)}, u32[]{:S(2)}) collective-permute-start(bf16[256,512]{1,0:T(8,128)(2,1)S(1)} %get-tuple-element.58.refs_0_.mid_one), channel_id=1, source_target_pairs={{0,1},{1,0},{2,3},{3,2},{4,5},{5,4},{6,7},{7,6},{8,9},{9,8},{10,11... | collective-permute-start | bytes 786440 | tf_op jit(solution)/shard_map/ppermute | solution.py:329
  46.0 1.8 %collective-permute-start.15 = (bf16[256,512]{1,0:T(8,128)(2,1)S(1)}, bf16[256,512]{1,0:T(8,128)(2,1)S(1)}, u32[]{:S(2)}, u32[]{:S(2)}) collective-permute-start(bf16[256,512]{1,0:T(8,128)(2,1)S(1)} %collective-permute-done.13.refs_1_.mid_two), channel_id=1, source_target_pairs={{0,1},{1,0},{2,3},{3,2},{4,5},{5,4},{6,7},{7,6},{8,9},{9,8},{10,11... | collective-permute-start | bytes 786440 | tf_op jit(solution)/shard_map/ppermute | solution.py:329
  51.1 4.6 %collective-permute-start.16 = (bf16[768,256]{1,0:T(8,128)(2,1)S(1)}, bf16[768,256]{1,0:T(8,128)(2,1)S(1)}, u32[]{:S(2)}, u32[]{:S(2)}) collective-permute-start(bf16[768,256]{1,0:T(8,128)(2,1)S(1)} %dpre.1.refs_0_), channel_id=1, source_target_pairs={{0,1},{1,0},{2,3},{3,2},{4,5},{5,4},{6,7},{7,6},{8,9},{9,8},{10,11... | collective-permute-start | bytes 1179656 | tf_op jit(solution)/shard_map/ppermute | solution.py:329
  51.7 9.7 %collective-permute-start.20 = (bf16[4,32,1152]{2,1,0:T(8,128)(2,1)S(1)}, bf16[4,32,1152]{2,1,0:T(8,128)(2,1)S(1)}, u32[]{:S(2)}, u32[]{:S(2)}) collective-permute-start(bf16[4,32,1152]{2,1,0:T(8,128)(2,1)S(1)} %get-tuple-element.73), channel_id=1, source_target_pairs={{0,4},{4,0},{8,12},{12,8},{16,20},{20,16},{24,28},{28,24},{1,5},{5... | collective-permute-start | bytes 884744 | tf_op jit(solution)/shard_map/ppermute | solution.py:329
  54.2 8.7 %collective-permute-start.21 = (bf16[4,32,1152]{2,1,0:T(8,128)(2,1)S(1)}, bf16[4,32,1152]{2,1,0:T(8,128)(2,1)S(1)}, u32[]{:S(2)}, u32[]{:S(2)}) collective-permute-start(bf16[4,32,1152]{2,1,0:T(8,128)(2,1)S(1)} %get-tuple-element.75), channel_id=1, source_target_pairs={{0,8},{4,12},{8,0},{12,4},{16,24},{20,28},{24,16},{28,20},{1,9},{5... | collective-permute-start | bytes 884744 | tf_op jit(solution)/shard_map/ppermute | solution.py:329
  57.2 12.0 %collective-permute-start.17 = (bf16[8,64,288]{2,1,0:T(8,128)(2,1)S(1)}, bf16[8,64,288]{2,1,0:T(8,128)(2,1)S(1)}, u32[]{:S(2)}, u32[]{:S(2)}) collective-permute-start(bf16[8,64,288]{2,1,0:T(8,128)(2,1)S(1)} %get-tuple-element.66), channel_id=1, source_target_pairs={{0,2},{1,3},{2,0},{3,1},{4,6},{5,7},{6,4},{7,5},{8,10},{9,11},{10,... | collective-permute-start | bytes 884744 | tf_op jit(solution)/shard_map/ppermute | solution.py:329
  63.0 6.3 %collective-permute-start.25 = (bf16[2,32,1152]{2,1,0:T(8,128)(2,1)S(1)}, bf16[2,32,1152]{2,1,0:T(8,128)(2,1)S(1)}, u32[]{:S(2)}, u32[]{:S(2)}) collective-permute-start(bf16[2,32,1152]{2,1,0:T(8,128)(2,1)S(1)} %get-tuple-element.84), channel_id=1, source_target_pairs={{0,8},{4,12},{8,0},{12,4},{16,24},{20,28},{24,16},{28,20},{1,9},{5... | collective-permute-start | bytes 442376 | tf_op jit(solution)/shard_map/ppermute | solution.py:329
  64.7 5.8 %collective-permute-start.26 = (bf16[2,32,1152]{2,1,0:T(8,128)(2,1)S(1)}, bf16[2,32,1152]{2,1,0:T(8,128)(2,1)S(1)}, u32[]{:S(2)}, u32[]{:S(2)}) collective-permute-start(bf16[2,32,1152]{2,1,0:T(8,128)(2,1)S(1)} %get-tuple-element.86), channel_id=1, source_target_pairs={{0,4},{4,0},{8,12},{12,8},{16,20},{20,16},{24,28},{28,24},{1,5},{5... | collective-permute-start | bytes 442376 | tf_op jit(solution)/shard_map/ppermute | solution.py:329
  65.0 10.5 %collective-permute-start.18 = (bf16[256,512]{1,0:T(8,128)(2,1)S(1)}, bf16[256,512]{1,0:T(8,128)(2,1)S(1)}, u32[]{:S(2)}, u32[]{:S(2)}) collective-permute-start(bf16[256,512]{1,0:T(8,128)(2,1)S(1)} %get-tuple-element.69.edge_one), channel_id=1, source_target_pairs={{0,2},{1,3},{2,0},{3,1},{4,6},{5,7},{6,4},{7,5},{8,10},{9,11},{10,... | collective-permute-start | bytes 786440 | tf_op jit(solution)/shard_map/ppermute | solution.py:329
  69.3 5.7 %collective-permute-start.22 = (bf16[4,64,288]{2,1,0:T(8,128)(2,1)S(1)}, bf16[4,64,288]{2,1,0:T(8,128)(2,1)S(1)}, u32[]{:S(2)}, u32[]{:S(2)}) collective-permute-start(bf16[4,64,288]{2,1,0:T(8,128)(2,1)S(1)} %get-tuple-element.78), channel_id=1, source_target_pairs={{0,4},{4,0},{8,12},{12,8},{16,20},{20,16},{24,28},{28,24},{1,5},{5... | collective-permute-start | bytes 442376 | tf_op jit(solution)/shard_map/ppermute | solution.py:329
  70.6 12.3 %collective-permute-start.27 = (bf16[1,64,1152]{2,1,0:T(8,128)(2,1)S(1)}, bf16[1,64,1152]{2,1,0:T(8,128)(2,1)S(1)}, u32[]{:S(2)}, u32[]{:S(2)}) collective-permute-start(bf16[1,64,1152]{2,1,0:T(8,128)(2,1)S(1)} %get-tuple-element.88), channel_id=1, source_target_pairs={{0,16},{4,20},{8,24},{12,28},{16,0},{20,4},{24,8},{28,12},{1,17},{... | collective-permute-start | bytes 442376 | tf_op jit(solution)/shard_map/ppermute | solution.py:329
  75.1 4.7 %collective-permute-start.23 = (bf16[2,64,288]{2,1,0:T(8,128)(2,1)S(1)}, bf16[2,64,288]{2,1,0:T(8,128)(2,1)S(1)}, u32[]{:S(2)}, u32[]{:S(2)}) collective-permute-start(bf16[2,64,288]{2,1,0:T(8,128)(2,1)S(1)} %get-tuple-element.80), channel_id=1, source_target_pairs={{0,8},{4,12},{8,0},{12,4},{16,24},{20,28},{24,16},{28,20},{1,9},{5... | collective-permute-start | bytes 221192 | tf_op jit(solution)/shard_map/ppermute | solution.py:329
  78.3 7.3 %collective-permute-start.19 = (bf16[256,512]{1,0:T(8,128)(2,1)S(1)}, bf16[256,512]{1,0:T(8,128)(2,1)S(1)}, u32[]{:S(2)}, u32[]{:S(2)}) collective-permute-start(bf16[256,512]{1,0:T(8,128)(2,1)S(1)} %get-tuple-element.71), channel_id=1, source_target_pairs={{0,2},{1,3},{2,0},{3,1},{4,6},{5,7},{6,4},{7,5},{8,10},{9,11},{10,... | collective-permute-start | bytes 786440 | tf_op jit(solution)/shard_map/ppermute | solution.py:329
  79.8 5.2 %collective-permute-start.24 = (bf16[1,64,288]{2,1,0:T(8,128)(2,1)S(1)}, bf16[1,64,288]{2,1,0:T(8,128)(2,1)S(1)}, u32[]{:S(2)}, u32[]{:S(2)}) collective-permute-start(bf16[1,64,288]{2,1,0:T(8,128)(2,1)S(1)} %get-tuple-element.82), channel_id=1, source_target_pairs={{0,16},{4,20},{8,24},{12,28},{16,0},{20,4},{24,8},{28,12},{1,17},{... | collective-permute-start | bytes 110600 | tf_op jit(solution)/shard_map/ppermute | solution.py:329

commit v4 on v3

--- a/solution.py
+++ b/solution.py
@@ -70,7 +70,7 @@
 
 
 def edge_kernel(height, width, s_ref, *refs):
-    far, (first_ref, second_ref, side_a, side_b), near, sems = refs[:6], refs[6:10], refs[10:16], refs[16]
+    far, (first_ref, second_ref), near, sems = refs[:6], refs[6:8], refs[8:14], refs[14]
     copies = [pltpu.make_async_copy(a, b, sems.at[n]) for n, (a, b) in enumerate(zip(far, near))]
     for copy in copies:
         copy.start()
@@ -79,8 +79,11 @@
     feat_ref, row_ref, col_ref, index_ref, mask_ref, cot_ref = near
     up = lax.rem(lax.axis_index("lat"), 2) == 0
     low, high = cot_ref[:width], cot_ref[(height - 1) * width :]
-    side_a[...] = jnp.where(up, high, low)
-    side_b[...] = jnp.where(up, low, high)
+    lanes = feat_ref.shape[1]
+    for out_ref, side in ((first_ref, jnp.where(up, high, low)), (second_ref, jnp.where(up, low, high))):
+        for q in range(side.shape[1] // lanes):
+            at = height * (width + 16) + q * width
+            out_ref[at : at + width] = side[:, q * lanes : (q + 1) * lanes]
     slots, channels = feat_ref.shape
     factor = column_factor(col_ref, width)
     entries = index_ref.shape[1]
@@ -119,7 +122,7 @@
     return first, second
 
 
-def finish_kernel(height, width, s_ref, numer_ref, denom_ref, first_ref, second_ref, out_ref):
+def finish_kernel(height, width, s_ref, numer_ref, denom_ref, first_ref, second_ref, out_ref, side_ref):
     first, second = partners(s_ref)
     cells = height * width
 
@@ -134,6 +137,11 @@
         added = jnp.broadcast_to(added, (width, width)).T[:, : numer_ref.shape[1]]
         numer = numer_ref[rows] + got(rows)
         out_ref[rows] = (numer * lax.rsqrt(1.0 + denom_ref[rows] + added)).astype(BF16)
+    lanes = numer_ref.shape[1]
+    for n, ref in enumerate((first_ref, second_ref)):
+        for q in range(side_ref.shape[1] // lanes):
+            at = height * (width + 16) + q * width
+            side_ref[n * width : (n + 1) * width, q * lanes : (q + 1) * lanes] = ref[at : at + width]
 
 
 def side_rows(s_ref, first, second):
@@ -389,26 +397,25 @@
     cot = cotangent[0].reshape(cells, hidden)
 
     feat, row, col = obs_feat[0], obs_row, obs_col
-    payload = like((height * (width + 16), channels), BF16)
+    payload = like((height * (width + 16) + width * hidden // channels, channels), BF16)
     observed = [feat, row, col, edge_index[0, 0], edge_mask[0, 0], cot]
-    side = like((width, hidden), BF16)
-    *edges, side_a, side_b = call(
+    edges = call(
         functools.partial(edge_kernel, height, width),
         "edges",
-        [payload, payload, side, side],
+        [payload, payload],
         scratch=[pltpu.VMEM(v.shape, v.dtype) for v in observed] + [pltpu.SemaphoreType.DMA((len(observed),))],
         far=len(observed),
         grant=60,
     )(counts, *observed)
     cot_got, w_got, w_other = swap(cot, "dp", outer), swap(w_first, "dp", outer), swap(w_second, "dp", 1)
-    side = jnp.concatenate(with_partners(side_a, side_b), axis=0)
     from_first, from_second = with_partners(*edges)
     numer, denom = call(functools.partial(own_kernel, height, width), "own", [like((cells, channels), F32)] * 2)(
-        after(counts, (side, w_other)), feat, row, col
-    )
-    h0 = call(functools.partial(finish_kernel, height, width), "finish", [like((cells, channels), BF16)])(
+        after(counts, w_other), feat, row, col
+    )
+    sides_out = like((2 * width, hidden), BF16)
+    h0, side = call(functools.partial(finish_kernel, height, width), "finish", [like((cells, channels), BF16), sides_out])(
         scalars, numer, denom, from_first, from_second
-    )[0]
+    )
     h0_first, h0_second = with_partners(h0, h0)
     side_got = swap(side, "dp", outer)
     lower = member % 2 == 0
@@ -433,7 +440,7 @@
         [
             like((cells, hidden), F32),
             like((cells, hidden), BF16),
-            side,
+            sides_out,
             like((width, (height + 2) * channels), BF16),
         ],
         scratch=[pltpu.VMEM((n_dp * w_first.shape[0], hidden), BF16)],

time: 86.6 us -> 85.9 us (level)
  starting transfers between devices: 35 us -> 31 us
  waiting for transfers between devices: 29.4 us -> 32.8 us
    ppermute x25 -> x24, starting transfers between devices: 32.1 us -> 28.7 us  [swap(): lax.ppermute(value, axis, [(i, i ^ bit) for i in range(lax.axis_size(axis...]
    ppermute x25 -> x24, waiting for transfers between devices: 29.4 us -> 32.8 us  [swap(): lax.ppermute(value, axis, [(i, i ^ bit) for i in range(lax.axis_size(axis...]
    ppermute x3 -> x2, starting transfers between devices: 2.86 us -> 2.23 us  [with_partners(): return (swap(first, 'lat', 1), lax.ppermute(second, 'lat', pairs))]
  transfers between devices with their start and end apart: 28 -> 26, of which waited for: 11 -> 11; matrix products, arithmetic and copies ran while one was open for 1% -> 1% of each run, Pallas kernels for 18% -> 18%
where the time goes in v4:
time: 85.9 us; the launch traced here: 85.7 us
  waiting for transfers between devices  32.8 us (38%)
  starting transfers between devices  31 us (36%)
  Pallas kernels  19.1 us (22%)
  between operations  1.55 us (2%)
  other arithmetic  1.15 us (1%)
    ppermute x24, waiting for transfers between devices, swap(): lax.ppermute(value, axis, [(i, i ^ bit) for i in range(lax.axis_size(axis...  32.8 us
    ppermute x24, starting transfers between devices, swap(): lax.ppermute(value, axis, [(i, i ^ bit) for i in range(lax.axis_size(axis...  28.7 us
    pallas_call x17, Pallas kernels, run(): pl.pallas_call(kernel, name=name, out_shape=outs, in_specs=[SMEM] * scala...  19.1 us
    ppermute x2, starting transfers between devices, with_partners(): return (swap(first, 'lat', 1), lax.ppermute(second, 'lat', pairs))  2.23 us
  transfers between devices with their start and end apart: 26, of which 11 were waited for; matrix products, arithmetic and copies ran while one was open for 1% of the time, Pallas kernels for 18%

profile of v4, /device:TPU:0, one launch (start us, length us, event | category | flops | bytes accessed | tf_op | source)
XLA Modules:
  0.0 85.7 jit_solution(9769551724331026634)
XLA Ops:
  0.6 0.5 collective-permute-start
  1.9 2.7 %edges.1 = (bf16[800,128]{1,0:T(8,128)(2,1)}, bf16[800,128]{1,0:T(8,128)(2,1)}) custom-call(s32[1,1]{1,0:T(1,128)} %copy.12.s_ref, f32[1024,128]{1,0:T(8,128)} %bitcast.17, f32[1,1024]{1,0:T(1,128)} %refs_1_.1, f32[1,1024]{1,0:T(1,128)} %refs_2_.1, s32[2,128]{1,0:T(2,128)} %bitcast.26, s32[2,128]{1,0:T(2,128)} %bitcast.27, bf16[256,512]{1,0:T(8,128)(2,1)} %bitcast.19), custom_call_target="tpu_custom_call" | custom-call | flops 4107269120 | tf_op jit(solution)/shard_map/edges/pallas_call | solution.py:20
  4.6 2.6 %collective-permute-start.1 = (bf16[800,128]{1,0:T(8,128)(2,1)}, bf16[800,128]{1,0:T(8,128)(2,1)S(1)}, u32[]{:S(2)}, u32[]{:S(2)}) collective-permute-start(bf16[800,128]{1,0:T(8,128)(2,1)} %get-tuple-element.49), channel_id=1, source_target_pairs={{0,4},{4,0},{8,12},{12,8},{16,20},{20,16},{24,28},{28,24},{1,5},{5... | collective-permute-start | bytes 614408 | tf_op jit(solution)/shard_map/ppermute | solution.py:337
  7.1 1.6 %collective-permute-start.2 = (bf16[800,128]{1,0:T(8,128)(2,1)}, bf16[800,128]{1,0:T(8,128)(2,1)S(1)}, u32[]{:S(2)}, u32[]{:S(2)}) collective-permute-start(bf16[800,128]{1,0:T(8,128)(2,1)} %get-tuple-element.50), channel_id=1, source_target_pairs={{4,8},{12,16},{20,24},{8,4},{16,12},{24,20},{0,0},{28,28},{5,9},{1... | collective-permute-start | bytes 614408 | tf_op jit(solution)/shard_map/ppermute | solution.py:355
  8.7 1.5 %collective-permute-start.7 = (bf16[288,512]{1,0:T(8,128)(2,1)S(1)}, bf16[288,512]{1,0:T(8,128)(2,1)S(1)}, u32[]{:S(2)}, u32[]{:S(2)}) collective-permute-start(bf16[288,512]{1,0:T(8,128)(2,1)S(1)} %copy-done.5), channel_id=1, source_target_pairs={{0,2},{1,3},{2,0},{3,1},{4,6},{5,7},{6,4},{7,5},{8,10},{9,11},{10,... | collective-permute-start | bytes 884744 | tf_op jit(solution)/shard_map/ppermute | solution.py:337
  10.2 0.5 collective-permute-start.3
  10.8 0.3 own.1
  11.2 5.6 %collective-permute-done.1.first_ref = bf16[800,128]{1,0:T(8,128)(2,1)S(1)} collective-permute-done((bf16[800,128]{1,0:T(8,128)(2,1)}, bf16[800,128]{1,0:T(8,128)(2,1)S(1)}, u32[]{:S(2)}, u32[]{:S(2)}) %collective-permute-start.1) | collective-permute-done | bytes 204832 | tf_op jit(solution)/shard_map/ppermute | solution.py:337
  16.8 0.7 finish.1
  17.5 2.4 %collective-permute-start.5 = (bf16[256,128]{1,0:T(8,128)(2,1)S(1)}, bf16[256,128]{1,0:T(8,128)(2,1)S(1)}, u32[]{:S(2)}, u32[]{:S(2)}) collective-permute-start(bf16[256,128]{1,0:T(8,128)(2,1)S(1)} %get-tuple-element.51.own_ref), channel_id=1, source_target_pairs={{0,4},{4,0},{8,12},{12,8},{16,20},{20,16},{24,28},{28,24},{1,5},{5... | collective-permute-start | bytes 196616 | tf_op jit(solution)/shard_map/ppermute | solution.py:337
  20.0 0.7 collective-permute-start.6
  20.6 1.6 %collective-permute-start.4 = (bf16[256,512]{1,0:T(8,128)(2,1)S(1)}, bf16[256,512]{1,0:T(8,128)(2,1)S(1)}, u32[]{:S(2)}, u32[]{:S(2)}) collective-permute-start(bf16[256,512]{1,0:T(8,128)(2,1)S(1)} %get-tuple-element.53.side_ref), channel_id=1, source_target_pairs={{0,2},{1,3},{2,0},{3,1},{4,6},{5,7},{6,4},{7,5},{8,10},{9,11},{10,... | collective-permute-start | bytes 786440 | tf_op jit(solution)/shard_map/ppermute | solution.py:337
  22.4 0.2 broadcast_select_fusion.1
  22.5 0.2 pad_maximum_fusion.w_ref
  22.7 1.5 %collective-permute-done.3.cot_got = bf16[256,512]{1,0:T(8,128)(2,1)S(1)} collective-permute-done((bf16[256,512]{1,0:T(8,128)(2,1)S(1)}, bf16[256,512]{1,0:T(8,128)(2,1)S(1)}, u32[]{:S(2)}, u32[]{:S(2)}) %collective-permute-start.3) | collective-permute-done | bytes 262176 | tf_op jit(solution)/shard_map/ppermute | solution.py:337
  24.2 4.9 %collective-permute-done.4.side_got = bf16[256,512]{1,0:T(8,128)(2,1)S(1)} collective-permute-done((bf16[256,512]{1,0:T(8,128)(2,1)S(1)}, bf16[256,512]{1,0:T(8,128)(2,1)S(1)}, u32[]{:S(2)}, u32[]{:S(2)}) %collective-permute-start.4) | collective-permute-done | bytes 262176 | tf_op jit(solution)/shard_map/ppermute | solution.py:337
  29.1 2.9 %back.1 = (f32[256,512]{1,0:T(8,128)S(1)}, bf16[256,512]{1,0:T(8,128)(2,1)S(1)}, bf16[4,256,512]{2,1,0:T(8,128)(2,1)S(1)}) custom-call(s32[7]{0:T(128)S(1)} %stack.44.s_ref, bf16[256,512]{1,0:T(8,128)(2,1)S(1)} %bitcast.21, bf16[256,512]{1,0:T(8,128)(2,1)S(1)} %collective-permute-done.3.cot_got, bf16[256,512]{1,0:T(8,128)(2,1)S(1)} %get-tuple-element.53.side_ref, ...), custom_call_target="tpu_custom_call" | custom-call | flops 4600141312 | tf_op jit(solution)/shard_map/back/pallas_call | solution.py:20
  31.9 1.6 %collective-permute-start.9 = (bf16[256,512]{1,0:T(8,128)(2,1)S(1)}, bf16[256,512]{1,0:T(8,128)(2,1)S(1)}, u32[]{:S(2)}, u32[]{:S(2)}) collective-permute-start(bf16[256,512]{1,0:T(8,128)(2,1)S(1)} %get-tuple-element.59), channel_id=1, source_target_pairs={{0,2},{1,3},{2,0},{3,1},{4,6},{5,7},{6,4},{7,5},{8,10},{9,11},{10,... | collective-permute-start | bytes 786440 | tf_op jit(solution)/shard_map/ppermute | solution.py:337
  33.5 1.5 %first.1 = (f32[256,512]{1,0:T(8,128)S(1)}, bf16[256,512]{1,0:T(8,128)(2,1)S(1)}, bf16[256,512]{1,0:T(8,128)(2,1)S(1)}, bf16[128,512]{1,0:T(8,128)(2,1)S(1)}) custom-call(s32[7]{0:T(128)S(1)} %stack.44.s_ref, bf16[256,128]{1,0:T(8,128)(2,1)S(1)} %get-tuple-element.51.own_ref, bf16[256,128]{1,0:T(8,128)(2,1)S(1)} %collective-permute-done.5.a_ref, ...), custom_call_target="tpu_custom_call" | custom-call | flops 24202651648 | tf_op jit(solution)/shard_map/first/pallas_call | solution.py:20
  35.1 0.6 collective-permute-start.11
  35.6 0.2 collective-permute-start.12
  35.8 4.8 %collective-permute-done.9.got_ref = bf16[256,512]{1,0:T(8,128)(2,1)S(1)} collective-permute-done((bf16[256,512]{1,0:T(8,128)(2,1)S(1)}, bf16[256,512]{1,0:T(8,128)(2,1)S(1)}, u32[]{:S(2)}, u32[]{:S(2)}) %collective-permute-start.9) | collective-permute-done | bytes 262176 | tf_op jit(solution)/shard_map/ppermute | solution.py:337
  40.6 4.4 %collective-permute-done.11.refs_1_.mid_two = bf16[256,512]{1,0:T(8,128)(2,1)S(1)} collective-permute-done((bf16[256,512]{1,0:T(8,128)(2,1)S(1)}, bf16[256,512]{1,0:T(8,128)(2,1)S(1)}, u32[]{:S(2)}, u32[]{:S(2)}) %collective-permute-start.11) | collective-permute-done | bytes 262176 | tf_op jit(solution)/shard_map/ppermute | solution.py:337
  45.1 1.8 %turn.1.turned_ref = bf16[3,512,1024]{2,1,0:T(8,128)(2,1)S(1)} custom-call(s32[7]{0:T(128)S(1)} %stack.44.s_ref, bf16[4,256,512]{2,1,0:T(8,128)(2,1)S(1)} %get-tuple-element.61.refs_0_, bf16[4,256,512]{2,1,0:T(8,128)(2,1)S(1)} %collective-permute-done.10.refs_1_), custom_call_target="tpu_custom_call" | custom-call | flops 2957233664 | tf_op jit(solution)/shard_map/turn/pallas_call | solution.py:20
  46.9 2.5 %gradsecond.1 = (bf16[4,32,1152]{2,1,0:T(8,128)(2,1)S(1)}, bf16[4,32,1152]{2,1,0:T(8,128)(2,1)S(1)}, bf16[4,32,1152]{2,1,0:T(8,128)(2,1)S(1)}, bf16[4,32,1152]{2,1,0:T(8,128)(2,1)S(1)}) custom-call(s32[7]{0:T(128)S(1)} %stack.44.s_ref, bf16[3,512,1024]{2,1,0:T(8,128)(2,1)S(1)} %turn.1.turned_ref, bf16[256,512]{1,0:T(8,128)(2,1)S(1)} %get-tuple-element.58.refs_0_.mid_one, ...), custom_call_target="tpu_custom_call" | custom-call | flops 4107269120 | tf_op jit(solution)/shard_map/gradsecond/pallas_call | solution.py:20
  49.4 0.8 dpre.1.refs_0_
  50.2 0.6 collective-permute-start.14
  50.8 2.3 %collective-permute-start.18 = (bf16[4,32,1152]{2,1,0:T(8,128)(2,1)S(1)}, bf16[4,32,1152]{2,1,0:T(8,128)(2,1)S(1)}, u32[]{:S(2)}, u32[]{:S(2)}) collective-permute-start(bf16[4,32,1152]{2,1,0:T(8,128)(2,1)S(1)} %get-tuple-element.73), channel_id=1, source_target_pairs={{0,4},{4,0},{8,12},{12,8},{16,20},{20,16},{24,28},{28,24},{1,5},{5... | collective-permute-start | bytes 884744 | tf_op jit(solution)/shard_map/ppermute | solution.py:337
  53.1 1.6 %collective-permute-start.19 = (bf16[4,32,1152]{2,1,0:T(8,128)(2,1)S(1)}, bf16[4,32,1152]{2,1,0:T(8,128)(2,1)S(1)}, u32[]{:S(2)}, u32[]{:S(2)}) collective-permute-start(bf16[4,32,1152]{2,1,0:T(8,128)(2,1)S(1)} %get-tuple-element.75), channel_id=1, source_target_pairs={{0,8},{4,12},{8,0},{12,4},{16,24},{20,28},{24,16},{28,20},{1,9},{5... | collective-permute-start | bytes 884744 | tf_op jit(solution)/shard_map/ppermute | solution.py:337
  54.6 1.5 %gradfirst.1 = (bf16[8,64,288]{2,1,0:T(8,128)(2,1)S(1)}, bf16[8,64,288]{2,1,0:T(8,128)(2,1)S(1)}) custom-call(s32[7]{0:T(128)S(1)} %stack.44.s_ref, bf16[768,256]{1,0:T(8,128)(2,1)S(1)} %dpre.1.refs_0_, bf16[768,256]{1,0:T(8,128)(2,1)S(1)} %collective-permute-done.14.refs_1_), custom_call_target="tpu_custom_call" | custom-call | flops 2464361472 | tf_op jit(solution)/shard_map/gradfirst/pallas_call | solution.py:20
  56.1 1.6 %collective-permute-start.15 = (bf16[8,64,288]{2,1,0:T(8,128)(2,1)S(1)}, bf16[8,64,288]{2,1,0:T(8,128)(2,1)S(1)}, u32[]{:S(2)}, u32[]{:S(2)}) collective-permute-start(bf16[8,64,288]{2,1,0:T(8,128)(2,1)S(1)} %get-tuple-element.66), channel_id=1, source_target_pairs={{0,2},{1,3},{2,0},{3,1},{4,6},{5,7},{6,4},{7,5},{8,10},{9,11},{10,... | collective-permute-start | bytes 884744 | tf_op jit(solution)/shard_map/ppermute | solution.py:337
  57.7 2.6 %collective-permute-done.18.refs_1_ = bf16[4,32,1152]{2,1,0:T(8,128)(2,1)S(1)} collective-permute-done((bf16[4,32,1152]{2,1,0:T(8,128)(2,1)S(1)}, bf16[4,32,1152]{2,1,0:T(8,128)(2,1)S(1)}, u32[]{:S(2)}, u32[]{:S(2)}) %collective-permute-start.18) | collective-permute-done | bytes 294944 | tf_op jit(solution)/shard_map/ppermute | solution.py:337
  60.3 1.5 %collective-permute-done.19.refs_3_ = bf16[4,32,1152]{2,1,0:T(8,128)(2,1)S(1)} collective-permute-done((bf16[4,32,1152]{2,1,0:T(8,128)(2,1)S(1)}, bf16[4,32,1152]{2,1,0:T(8,128)(2,1)S(1)}, u32[]{:S(2)}, u32[]{:S(2)}) %collective-permute-start.19) | collective-permute-done | bytes 294944 | tf_op jit(solution)/shard_map/ppermute | solution.py:337
  61.9 1.6 %collective-permute-start.23 = (bf16[2,32,1152]{2,1,0:T(8,128)(2,1)S(1)}, bf16[2,32,1152]{2,1,0:T(8,128)(2,1)S(1)}, u32[]{:S(2)}, u32[]{:S(2)}) collective-permute-start(bf16[2,32,1152]{2,1,0:T(8,128)(2,1)S(1)} %get-tuple-element.84), channel_id=1, source_target_pairs={{0,8},{4,12},{8,0},{12,4},{16,24},{20,28},{24,16},{28,20},{1,9},{5... | collective-permute-start | bytes 442376 | tf_op jit(solution)/shard_map/ppermute | solution.py:337
  63.6 0.4 collective-permute-start.24
  63.9 1.5 %collective-permute-start.16 = (bf16[256,512]{1,0:T(8,128)(2,1)S(1)}, bf16[256,512]{1,0:T(8,128)(2,1)S(1)}, u32[]{:S(2)}, u32[]{:S(2)}) collective-permute-start(bf16[256,512]{1,0:T(8,128)(2,1)S(1)} %get-tuple-element.69.edge_one), channel_id=1, source_target_pairs={{0,2},{1,3},{2,0},{3,1},{4,6},{5,7},{6,4},{7,5},{8,10},{9,11},{10,... | collective-permute-start | bytes 786440 | tf_op jit(solution)/shard_map/ppermute | solution.py:337
  65.4 2.6 %collective-permute-done.15.refs_1_ = bf16[8,64,288]{2,1,0:T(8,128)(2,1)S(1)} collective-permute-done((bf16[8,64,288]{2,1,0:T(8,128)(2,1)S(1)}, bf16[8,64,288]{2,1,0:T(8,128)(2,1)S(1)}, u32[]{:S(2)}, u32[]{:S(2)}) %collective-permute-start.15) | collective-permute-done | bytes 294944 | tf_op jit(solution)/shard_map/ppermute | solution.py:337
  68.2 1.1 %collective-permute-done.24.got_two = bf16[2,32,1152]{2,1,0:T(8,128)(2,1)S(1)} collective-permute-done((bf16[2,32,1152]{2,1,0:T(8,128)(2,1)S(1)}, bf16[2,32,1152]{2,1,0:T(8,128)(2,1)S(1)}, u32[]{:S(2)}, u32[]{:S(2)}) %collective-permute-start.24) | collective-permute-done | bytes 147488 | tf_op jit(solution)/shard_map/ppermute | solution.py:337
  69.4 2.1 %collective-permute-start.25 = (bf16[1,64,1152]{2,1,0:T(8,128)(2,1)S(1)}, bf16[1,64,1152]{2,1,0:T(8,128)(2,1)S(1)}, u32[]{:S(2)}, u32[]{:S(2)}) collective-permute-start(bf16[1,64,1152]{2,1,0:T(8,128)(2,1)S(1)} %get-tuple-element.88), channel_id=1, source_target_pairs={{0,16},{4,20},{8,24},{12,28},{16,0},{20,4},{24,8},{28,12},{1,17},{... | collective-permute-start | bytes 442376 | tf_op jit(solution)/shard_map/ppermute | solution.py:337
  71.5 2.4 %collective-permute-done.20.refs_1_ = bf16[4,64,288]{2,1,0:T(8,128)(2,1)S(1)} collective-permute-done((bf16[4,64,288]{2,1,0:T(8,128)(2,1)S(1)}, bf16[4,64,288]{2,1,0:T(8,128)(2,1)S(1)}, u32[]{:S(2)}, u32[]{:S(2)}) %collective-permute-start.20) | collective-permute-done | bytes 147488 | tf_op jit(solution)/shard_map/ppermute | solution.py:337
  73.9 0.5 collective-permute-start.21
  74.5 2.7 %second.1 = (f32[256,512]{1,0:T(8,128)S(1)}, bf16[256,512]{1,0:T(8,128)(2,1)S(1)}) custom-call(s32[7]{0:T(128)S(1)} %stack.44.s_ref, bf16[256,512]{1,0:T(8,128)(2,1)S(1)} %get-tuple-element.58.refs_0_.mid_one, bf16[256,512]{1,0:T(8,128)(2,1)S(1)} %collective-permute-done.11.refs_1_.mid_two, bf16[256,512]{1,0:T(8,128)(2,1)S(1)} %get-tuple-element.69.edge_one, ...), custom_call_target="tpu_custom_call" | custom-call | flops 4435850752 | tf_op jit(solution)/shard_map/second/pallas_call | solution.py:20
  77.2 1.6 %collective-permute-start.17 = (bf16[256,512]{1,0:T(8,128)(2,1)S(1)}, bf16[256,512]{1,0:T(8,128)(2,1)S(1)}, u32[]{:S(2)}, u32[]{:S(2)}) collective-permute-start(bf16[256,512]{1,0:T(8,128)(2,1)S(1)} %get-tuple-element.71), channel_id=1, source_target_pairs={{0,2},{1,3},{2,0},{3,1},{4,6},{5,7},{6,4},{7,5},{8,10},{9,11},{10,... | collective-permute-start | bytes 786440 | tf_op jit(solution)/shard_map/ppermute | solution.py:337
  78.8 3.4 %collective-permute-start.22 = (bf16[1,64,288]{2,1,0:T(8,128)(2,1)S(1)}, bf16[1,64,288]{2,1,0:T(8,128)(2,1)S(1)}, u32[]{:S(2)}, u32[]{:S(2)}) collective-permute-start(bf16[1,64,288]{2,1,0:T(8,128)(2,1)S(1)} %get-tuple-element.82), channel_id=1, source_target_pairs={{0,16},{4,20},{8,24},{12,28},{16,0},{20,4},{24,8},{28,12},{1,17},{... | collective-permute-start | bytes 110600 | tf_op jit(solution)/shard_map/ppermute | solution.py:337
  82.2 0.7 last.3
  82.9 1.3 %collective-permute-done.22.got_ref = bf16[1,64,288]{2,1,0:T(8,128)(2,1)S(1)} collective-permute-done((bf16[1,64,288]{2,1,0:T(8,128)(2,1)S(1)}, bf16[1,64,288]{2,1,0:T(8,128)(2,1)S(1)}, u32[]{:S(2)}, u32[]{:S(2)}) %collective-permute-start.22) | collective-permute-done | bytes 36896 | tf_op jit(solution)/shard_map/ppermute | solution.py:337
  84.3 0.7 last.2
  84.9 0.8 add_convert_fusion
  (38 shorter events, 0.8 us)
Async XLA Ops:
  0.6 21.6 %collective-permute-start = (bf16[1152,512]{1,0:T(8,128)(2,1)}, bf16[1152,512]{1,0:T(8,128)(2,1)S(1)}, u32[]{:S(2)}, u32[]{:S(2)}) collective-permute-start(bf16[1152,512]{1,0:T(8,128)(2,1)} %param.17), channel_id=1, source_target_pairs={{0,1},{1,0},{2,3},{3,2},{4,5},{5,4},{6,7},{7,6},{8,9},{9,8},{10,11... | collective-permute-start | bytes 3538952 | tf_op jit(solution)/shard_map/ppermute | solution.py:337
  1.8 6.9 %copy-start.5 = (bf16[288,512]{1,0:T(8,128)(2,1)S(1)}, bf16[288,512]{1,0:T(8,128)(2,1)}, u32[]{:S(2)}) copy-start(bf16[288,512]{1,0:T(8,128)(2,1)} %param.16) | copy-start | bytes 884740
  1.8 8.4 %copy-start.1 = (bf16[1,2,128,512]{3,2,1,0:T(8,128)(2,1)S(1)}, bf16[1,2,128,512]{3,2,1,0:T(8,128)(2,1)}, u32[]{:S(2)}) copy-start(bf16[1,2,128,512]{3,2,1,0:T(8,128)(2,1)} %param.15) | copy-start | bytes 786436
  1.8 9.0 %copy-start = (f32[1,1024,128]{2,1,0:T(8,128)S(1)}, f32[1,1024,128]{2,1,0:T(8,128)}, u32[]{:S(2)}) copy-start(f32[1,1024,128]{2,1,0:T(8,128)} %param.9) | copy-start | bytes 1572868
  1.8 9.0 %copy-start.2 = (f32[1,1024]{1,0:T(1,128)S(1)}, f32[1,1024]{1,0:T(1,128)}, u32[]{:S(2)}) copy-start(f32[1,1024]{1,0:T(1,128)} %refs_1_.1) | copy-start | bytes 12292
  1.8 9.0 %copy-start.3 = (f32[1,1024]{1,0:T(1,128)S(1)}, f32[1,1024]{1,0:T(1,128)}, u32[]{:S(2)}) copy-start(f32[1,1024]{1,0:T(1,128)} %refs_2_.1) | copy-start | bytes 12292
  4.6 12.3 %collective-permute-start.1 = (bf16[800,128]{1,0:T(8,128)(2,1)}, bf16[800,128]{1,0:T(8,128)(2,1)S(1)}, u32[]{:S(2)}, u32[]{:S(2)}) collective-permute-start(bf16[800,128]{1,0:T(8,128)(2,1)} %get-tuple-element.49), channel_id=1, source_target_pairs={{0,4},{4,0},{8,12},{12,8},{16,20},{20,16},{24,28},{28,24},{1,5},{5... | collective-permute-start | bytes 614408 | tf_op jit(solution)/shard_map/ppermute | solution.py:337
  7.1 9.7 %collective-permute-start.2 = (bf16[800,128]{1,0:T(8,128)(2,1)}, bf16[800,128]{1,0:T(8,128)(2,1)S(1)}, u32[]{:S(2)}, u32[]{:S(2)}) collective-permute-start(bf16[800,128]{1,0:T(8,128)(2,1)} %get-tuple-element.50), channel_id=1, source_target_pairs={{4,8},{12,16},{20,24},{8,4},{16,12},{24,20},{0,0},{28,28},{5,9},{1... | collective-permute-start | bytes 614408 | tf_op jit(solution)/shard_map/ppermute | solution.py:355
  8.7 11.9 %collective-permute-start.7 = (bf16[288,512]{1,0:T(8,128)(2,1)S(1)}, bf16[288,512]{1,0:T(8,128)(2,1)S(1)}, u32[]{:S(2)}, u32[]{:S(2)}) collective-permute-start(bf16[288,512]{1,0:T(8,128)(2,1)S(1)} %copy-done.5), channel_id=1, source_target_pairs={{0,2},{1,3},{2,0},{3,1},{4,6},{5,7},{6,4},{7,5},{8,10},{9,11},{10,... | collective-permute-start | bytes 884744 | tf_op jit(solution)/shard_map/ppermute | solution.py:337
  10.2 13.9 %collective-permute-start.3 = (bf16[256,512]{1,0:T(8,128)(2,1)S(1)}, bf16[256,512]{1,0:T(8,128)(2,1)S(1)}, u32[]{:S(2)}, u32[]{:S(2)}) collective-permute-start(bf16[256,512]{1,0:T(8,128)(2,1)S(1)} %bitcast.20), channel_id=1, source_target_pairs={{0,2},{1,3},{2,0},{3,1},{4,6},{5,7},{6,4},{7,5},{8,10},{9,11},{10,... | collective-permute-start | bytes 786440 | tf_op jit(solution)/shard_map/ppermute | solution.py:337
  17.5 4.9 %copy-start.4 = (bf16[1152,512]{1,0:T(8,128)(2,1)S(1)}, bf16[1152,512]{1,0:T(8,128)(2,1)}, u32[]{:S(2)}) copy-start(bf16[1152,512]{1,0:T(8,128)(2,1)} %param.17) | copy-start | bytes 3538948
  17.5 16.0 %collective-permute-start.5 = (bf16[256,128]{1,0:T(8,128)(2,1)S(1)}, bf16[256,128]{1,0:T(8,128)(2,1)S(1)}, u32[]{:S(2)}, u32[]{:S(2)}) collective-permute-start(bf16[256,128]{1,0:T(8,128)(2,1)S(1)} %get-tuple-element.51.own_ref), channel_id=1, source_target_pairs={{0,4},{4,0},{8,12},{12,8},{16,20},{20,16},{24,28},{28,24},{1,5},{5... | collective-permute-start | bytes 196616 | tf_op jit(solution)/shard_map/ppermute | solution.py:337
  20.0 13.6 %collective-permute-start.6 = (bf16[256,128]{1,0:T(8,128)(2,1)S(1)}, bf16[256,128]{1,0:T(8,128)(2,1)S(1)}, u32[]{:S(2)}, u32[]{:S(2)}) collective-permute-start(bf16[256,128]{1,0:T(8,128)(2,1)S(1)} %get-tuple-element.51.own_ref), channel_id=1, source_target_pairs={{4,8},{12,16},{20,24},{8,4},{16,12},{24,20},{0,0},{28,28},{5,9},{1... | collective-permute-start | bytes 196616 | tf_op jit(solution)/shard_map/ppermute | solution.py:355
  20.6 8.4 %collective-permute-start.4 = (bf16[256,512]{1,0:T(8,128)(2,1)S(1)}, bf16[256,512]{1,0:T(8,128)(2,1)S(1)}, u32[]{:S(2)}, u32[]{:S(2)}) collective-permute-start(bf16[256,512]{1,0:T(8,128)(2,1)S(1)} %get-tuple-element.53.side_ref), channel_id=1, source_target_pairs={{0,2},{1,3},{2,0},{3,1},{4,6},{5,7},{6,4},{7,5},{8,10},{9,11},{10,... | collective-permute-start | bytes 786440 | tf_op jit(solution)/shard_map/ppermute | solution.py:337
  22.3 11.3 %collective-permute-start.8 = (bf16[2,288,512]{2,1,0:T(8,128)(2,1)S(1)}, bf16[2,288,512]{2,1,0:T(8,128)(2,1)S(1)}, u32[]{:S(2)}, u32[]{:S(2)}) collective-permute-start(bf16[2,288,512]{2,1,0:T(8,128)(2,1)S(1)} %pad_maximum_fusion.1.w_near), channel_id=1, source_target_pairs={{0,1},{1,0},{2,3},{3,2},{4,5},{5,4},{6,7},{7,6},{8,9},{9,8},{10,11... | collective-permute-start | bytes 1769480 | tf_op jit(solution)/shard_map/ppermute | solution.py:337
  31.9 8.7 %collective-permute-start.9 = (bf16[256,512]{1,0:T(8,128)(2,1)S(1)}, bf16[256,512]{1,0:T(8,128)(2,1)S(1)}, u32[]{:S(2)}, u32[]{:S(2)}) collective-permute-start(bf16[256,512]{1,0:T(8,128)(2,1)S(1)} %get-tuple-element.59), channel_id=1, source_target_pairs={{0,2},{1,3},{2,0},{3,1},{4,6},{5,7},{6,4},{7,5},{8,10},{9,11},{10,... | collective-permute-start | bytes 786440 | tf_op jit(solution)/shard_map/ppermute | solution.py:337
  33.5 11.6 %collective-permute-start.10 = (bf16[4,256,512]{2,1,0:T(8,128)(2,1)S(1)}, bf16[4,256,512]{2,1,0:T(8,128)(2,1)S(1)}, u32[]{:S(2)}, u32[]{:S(2)}) collective-permute-start(bf16[4,256,512]{2,1,0:T(8,128)(2,1)S(1)} %get-tuple-element.61.refs_0_), channel_id=1, source_target_pairs={{0,1},{1,0},{2,3},{3,2},{4,5},{5,4},{6,7},{7,6},{8,9},{9,8},{10,11... | collective-permute-start | bytes 3145736 | tf_op jit(solution)/shard_map/ppermute | solution.py:337
  35.1 10.0 %collective-permute-start.11 = (bf16[256,512]{1,0:T(8,128)(2,1)S(1)}, bf16[256,512]{1,0:T(8,128)(2,1)S(1)}, u32[]{:S(2)}, u32[]{:S(2)}) collective-permute-start(bf16[256,512]{1,0:T(8,128)(2,1)S(1)} %get-tuple-element.58.refs_0_.mid_one), channel_id=1, source_target_pairs={{0,2},{1,3},{2,0},{3,1},{4,6},{5,7},{6,4},{7,5},{8,10},{9,11},{10,... | collective-permute-start | bytes 786440 | tf_op jit(solution)/shard_map/ppermute | solution.py:337
  35.6 11.3 %collective-permute-start.12 = (bf16[256,512]{1,0:T(8,128)(2,1)S(1)}, bf16[256,512]{1,0:T(8,128)(2,1)S(1)}, u32[]{:S(2)}, u32[]{:S(2)}) collective-permute-start(bf16[256,512]{1,0:T(8,128)(2,1)S(1)} %get-tuple-element.58.refs_0_.mid_one), channel_id=1, source_target_pairs={{0,1},{1,0},{2,3},{3,2},{4,5},{5,4},{6,7},{7,6},{8,9},{9,8},{10,11... | collective-permute-start | bytes 786440 | tf_op jit(solution)/shard_map/ppermute | solution.py:337
  45.1 1.8 %collective-permute-start.13 = (bf16[256,512]{1,0:T(8,128)(2,1)S(1)}, bf16[256,512]{1,0:T(8,128)(2,1)S(1)}, u32[]{:S(2)}, u32[]{:S(2)}) collective-permute-start(bf16[256,512]{1,0:T(8,128)(2,1)S(1)} %collective-permute-done.11.refs_1_.mid_two), channel_id=1, source_target_pairs={{0,1},{1,0},{2,3},{3,2},{4,5},{5,4},{6,7},{7,6},{8,9},{9,8},{10,11... | collective-permute-start | bytes 786440 | tf_op jit(solution)/shard_map/ppermute | solution.py:337
  50.2 4.4 %collective-permute-start.14 = (bf16[768,256]{1,0:T(8,128)(2,1)S(1)}, bf16[768,256]{1,0:T(8,128)(2,1)S(1)}, u32[]{:S(2)}, u32[]{:S(2)}) collective-permute-start(bf16[768,256]{1,0:T(8,128)(2,1)S(1)} %dpre.1.refs_0_), channel_id=1, source_target_pairs={{0,1},{1,0},{2,3},{3,2},{4,5},{5,4},{6,7},{7,6},{8,9},{9,8},{10,11... | collective-permute-start | bytes 1179656 | tf_op jit(solution)/shard_map/ppermute | solution.py:337
  50.8 9.5 %collective-permute-start.18 = (bf16[4,32,1152]{2,1,0:T(8,128)(2,1)S(1)}, bf16[4,32,1152]{2,1,0:T(8,128)(2,1)S(1)}, u32[]{:S(2)}, u32[]{:S(2)}) collective-permute-start(bf16[4,32,1152]{2,1,0:T(8,128)(2,1)S(1)} %get-tuple-element.73), channel_id=1, source_target_pairs={{0,4},{4,0},{8,12},{12,8},{16,20},{20,16},{24,28},{28,24},{1,5},{5... | collective-permute-start | bytes 884744 | tf_op jit(solution)/shard_map/ppermute | solution.py:337
  53.1 8.7 %collective-permute-start.19 = (bf16[4,32,1152]{2,1,0:T(8,128)(2,1)S(1)}, bf16[4,32,1152]{2,1,0:T(8,128)(2,1)S(1)}, u32[]{:S(2)}, u32[]{:S(2)}) collective-permute-start(bf16[4,32,1152]{2,1,0:T(8,128)(2,1)S(1)} %get-tuple-element.75), channel_id=1, source_target_pairs={{0,8},{4,12},{8,0},{12,4},{16,24},{20,28},{24,16},{28,20},{1,9},{5... | collective-permute-start | bytes 884744 | tf_op jit(solution)/shard_map/ppermute | solution.py:337
  56.1 12.0 %collective-permute-start.15 = (bf16[8,64,288]{2,1,0:T(8,128)(2,1)S(1)}, bf16[8,64,288]{2,1,0:T(8,128)(2,1)S(1)}, u32[]{:S(2)}, u32[]{:S(2)}) collective-permute-start(bf16[8,64,288]{2,1,0:T(8,128)(2,1)S(1)} %get-tuple-element.66), channel_id=1, source_target_pairs={{0,2},{1,3},{2,0},{3,1},{4,6},{5,7},{6,4},{7,5},{8,10},{9,11},{10,... | collective-permute-start | bytes 884744 | tf_op jit(solution)/shard_map/ppermute | solution.py:337
  61.9 6.3 %collective-permute-start.23 = (bf16[2,32,1152]{2,1,0:T(8,128)(2,1)S(1)}, bf16[2,32,1152]{2,1,0:T(8,128)(2,1)S(1)}, u32[]{:S(2)}, u32[]{:S(2)}) collective-permute-start(bf16[2,32,1152]{2,1,0:T(8,128)(2,1)S(1)} %get-tuple-element.84), channel_id=1, source_target_pairs={{0,8},{4,12},{8,0},{12,4},{16,24},{20,28},{24,16},{28,20},{1,9},{5... | collective-permute-start | bytes 442376 | tf_op jit(solution)/shard_map/ppermute | solution.py:337
  63.6 5.8 %collective-permute-start.24 = (bf16[2,32,1152]{2,1,0:T(8,128)(2,1)S(1)}, bf16[2,32,1152]{2,1,0:T(8,128)(2,1)S(1)}, u32[]{:S(2)}, u32[]{:S(2)}) collective-permute-start(bf16[2,32,1152]{2,1,0:T(8,128)(2,1)S(1)} %get-tuple-element.86), channel_id=1, source_target_pairs={{0,4},{4,0},{8,12},{12,8},{16,20},{20,16},{24,28},{28,24},{1,5},{5... | collective-permute-start | bytes 442376 | tf_op jit(solution)/shard_map/ppermute | solution.py:337
  63.9 10.5 %collective-permute-start.16 = (bf16[256,512]{1,0:T(8,128)(2,1)S(1)}, bf16[256,512]{1,0:T(8,128)(2,1)S(1)}, u32[]{:S(2)}, u32[]{:S(2)}) collective-permute-start(bf16[256,512]{1,0:T(8,128)(2,1)S(1)} %get-tuple-element.69.edge_one), channel_id=1, source_target_pairs={{0,2},{1,3},{2,0},{3,1},{4,6},{5,7},{6,4},{7,5},{8,10},{9,11},{10,... | collective-permute-start | bytes 786440 | tf_op jit(solution)/shard_map/ppermute | solution.py:337
  68.2 5.7 %collective-permute-start.20 = (bf16[4,64,288]{2,1,0:T(8,128)(2,1)S(1)}, bf16[4,64,288]{2,1,0:T(8,128)(2,1)S(1)}, u32[]{:S(2)}, u32[]{:S(2)}) collective-permute-start(bf16[4,64,288]{2,1,0:T(8,128)(2,1)S(1)} %get-tuple-element.78), channel_id=1, source_target_pairs={{0,4},{4,0},{8,12},{12,8},{16,20},{20,16},{24,28},{28,24},{1,5},{5... | collective-permute-start | bytes 442376 | tf_op jit(solution)/shard_map/ppermute | solution.py:337
  69.4 12.8 %collective-permute-start.25 = (bf16[1,64,1152]{2,1,0:T(8,128)(2,1)S(1)}, bf16[1,64,1152]{2,1,0:T(8,128)(2,1)S(1)}, u32[]{:S(2)}, u32[]{:S(2)}) collective-permute-start(bf16[1,64,1152]{2,1,0:T(8,128)(2,1)S(1)} %get-tuple-element.88), channel_id=1, source_target_pairs={{0,16},{4,20},{8,24},{12,28},{16,0},{20,4},{24,8},{28,12},{1,17},{... | collective-permute-start | bytes 442376 | tf_op jit(solution)/shard_map/ppermute | solution.py:337
  73.9 4.8 %collective-permute-start.21 = (bf16[2,64,288]{2,1,0:T(8,128)(2,1)S(1)}, bf16[2,64,288]{2,1,0:T(8,128)(2,1)S(1)}, u32[]{:S(2)}, u32[]{:S(2)}) collective-permute-start(bf16[2,64,288]{2,1,0:T(8,128)(2,1)S(1)} %get-tuple-element.80), channel_id=1, source_target_pairs={{0,8},{4,12},{8,0},{12,4},{16,24},{20,28},{24,16},{28,20},{1,9},{5... | collective-permute-start | bytes 221192 | tf_op jit(solution)/shard_map/ppermute | solution.py:337
  77.2 7.7 %collective-permute-start.17 = (bf16[256,512]{1,0:T(8,128)(2,1)S(1)}, bf16[256,512]{1,0:T(8,128)(2,1)S(1)}, u32[]{:S(2)}, u32[]{:S(2)}) collective-permute-start(bf16[256,512]{1,0:T(8,128)(2,1)S(1)} %get-tuple-element.71), channel_id=1, source_target_pairs={{0,2},{1,3},{2,0},{3,1},{4,6},{5,7},{6,4},{7,5},{8,10},{9,11},{10,... | collective-permute-start | bytes 786440 | tf_op jit(solution)/shard_map/ppermute | solution.py:337
  78.8 5.4 %collective-permute-start.22 = (bf16[1,64,288]{2,1,0:T(8,128)(2,1)S(1)}, bf16[1,64,288]{2,1,0:T(8,128)(2,1)S(1)}, u32[]{:S(2)}, u32[]{:S(2)}) collective-permute-start(bf16[1,64,288]{2,1,0:T(8,128)(2,1)S(1)} %get-tuple-element.82), channel_id=1, source_target_pairs={{0,16},{4,20},{8,24},{12,28},{16,0},{20,4},{24,8},{28,12},{1,17},{... | collective-permute-start | bytes 110600 | tf_op jit(solution)/shard_map/ppermute | solution.py:337

commit v5 on v4

--- a/solution.py
+++ b/solution.py
@@ -74,30 +74,34 @@
     copies = [pltpu.make_async_copy(a, b, sems.at[n]) for n, (a, b) in enumerate(zip(far, near))]
     for copy in copies:
         copy.start()
-    for copy in copies:
+    for copy in copies[1:5]:
         copy.wait()
     feat_ref, row_ref, col_ref, index_ref, mask_ref, cot_ref = near
     up = lax.rem(lax.axis_index("lat"), 2) == 0
+    slots, channels = feat_ref.shape
+    factor = column_factor(col_ref, width)
+    entries = index_ref.shape[1]
+    slot = lax.broadcasted_iota(jnp.int32, (slots, entries), 0)
+    live = slot < s_ref[0, 0]
+    counted = []
+    for side in range(2):
+        named = jnp.where((slot == index_ref[side : side + 1]) & live, mask_ref[side : side + 1], 0)
+        times = jnp.sum(named.astype(F32), axis=1, keepdims=True)
+        offset = height if side == 1 else -height
+        counted.append((times, cell_weights(factor, row_ref, [float(offset + i) for i in range(height)])))
+    copies[0].wait()
+    copies[5].wait()
+    feat = feat_ref[...]
+    totals = []
+    for times, weights in counted:
+        values = jnp.concatenate([feat * times, jnp.broadcast_to(times, feat.shape)], axis=1)
+        totals.append(dot(weights, values.astype(BF16)))
     low, high = cot_ref[:width], cot_ref[(height - 1) * width :]
     lanes = feat_ref.shape[1]
     for out_ref, side in ((first_ref, jnp.where(up, high, low)), (second_ref, jnp.where(up, low, high))):
         for q in range(side.shape[1] // lanes):
             at = height * (width + 16) + q * width
             out_ref[at : at + width] = side[:, q * lanes : (q + 1) * lanes]
-    slots, channels = feat_ref.shape
-    factor = column_factor(col_ref, width)
-    entries = index_ref.shape[1]
-    slot = lax.broadcasted_iota(jnp.int32, (slots, entries), 0)
-    live = slot < s_ref[0, 0]
-    feat = feat_ref[...]
-    totals = []
-    for side in range(2):
-        named = jnp.where((slot == index_ref[side : side + 1]) & live, mask_ref[side : side + 1], 0)
-        times = jnp.sum(named.astype(F32), axis=1, keepdims=True)
-        values = jnp.concatenate([feat * times, jnp.broadcast_to(times, feat.shape)], axis=1)
-        offset = height if side == 1 else -height
-        weights = cell_weights(factor, row_ref, [float(offset + i) for i in range(height)])
-        totals.append(dot(weights, values.astype(BF16)))
     for out_ref, one, other in ((first_ref, 1, 0), (second_ref, 0, 1)):
         total = jnp.where(up, totals[one], totals[other])
         out_ref[: height * width] = total[:, :channels].astype(BF16)

time: 85.9 us -> 86 us (level)
  transfers between devices with their start and end apart: 26 -> 26, of which waited for: 11 -> 11; matrix products, arithmetic and copies ran while one was open for 1% -> 1% of each run, Pallas kernels for 18% -> 19%
where the time goes in v5:
time: 86 us; the launch traced here: 85.8 us
  waiting for transfers between devices  32.8 us (38%)
  starting transfers between devices  31 us (36%)
  Pallas kernels  19.2 us (22%)
  between operations  1.55 us (2%)
  other arithmetic  1.15 us (1%)
    ppermute x24, waiting for transfers between devices, swap(): lax.ppermute(value, axis, [(i, i ^ bit) for i in range(lax.axis_size(axis...  32.8 us
    ppermute x24, starting transfers between devices, swap(): lax.ppermute(value, axis, [(i, i ^ bit) for i in range(lax.axis_size(axis...  28.7 us
    pallas_call x17, Pallas kernels, run(): pl.pallas_call(kernel, name=name, out_shape=outs, in_specs=[SMEM] * scala...  19.2 us
    ppermute x2, starting transfers between devices, with_partners(): return (swap(first, 'lat', 1), lax.ppermute(second, 'lat', pairs))  2.23 us
  transfers between devices with their start and end apart: 26, of which 11 were waited for; matrix products, arithmetic and copies ran while one was open for 1% of the time, Pallas kernels for 19%

profile of v5, /device:TPU:0, one launch (start us, length us, event | category | flops | bytes accessed | tf_op | source)
XLA Modules:
  0.0 85.8 jit_solution(10994923007926524260)
XLA Ops:
  0.6 0.5 collective-permute-start
  1.9 2.8 %edges.1 = (bf16[800,128]{1,0:T(8,128)(2,1)}, bf16[800,128]{1,0:T(8,128)(2,1)}) custom-call(s32[1,1]{1,0:T(1,128)} %copy.12.s_ref, f32[1024,128]{1,0:T(8,128)} %bitcast.17, f32[1,1024]{1,0:T(1,128)} %refs_1_.1, f32[1,1024]{1,0:T(1,128)} %refs_2_.1, s32[2,128]{1,0:T(2,128)} %bitcast.26, s32[2,128]{1,0:T(2,128)} %bitcast.27, bf16[256,512]{1,0:T(8,128)(2,1)} %bitcast.19), custom_call_target="tpu_custom_call" | custom-call | flops 4107269120 | tf_op jit(solution)/shard_map/edges/pallas_call | solution.py:20
  4.7 2.6 %collective-permute-start.1 = (bf16[800,128]{1,0:T(8,128)(2,1)}, bf16[800,128]{1,0:T(8,128)(2,1)S(1)}, u32[]{:S(2)}, u32[]{:S(2)}) collective-permute-start(bf16[800,128]{1,0:T(8,128)(2,1)} %get-tuple-element.49), channel_id=1, source_target_pairs={{0,4},{4,0},{8,12},{12,8},{16,20},{20,16},{24,28},{28,24},{1,5},{5... | collective-permute-start | bytes 614408 | tf_op jit(solution)/shard_map/ppermute | solution.py:341
  7.2 1.6 %collective-permute-start.2 = (bf16[800,128]{1,0:T(8,128)(2,1)}, bf16[800,128]{1,0:T(8,128)(2,1)S(1)}, u32[]{:S(2)}, u32[]{:S(2)}) collective-permute-start(bf16[800,128]{1,0:T(8,128)(2,1)} %get-tuple-element.50), channel_id=1, source_target_pairs={{4,8},{12,16},{20,24},{8,4},{16,12},{24,20},{0,0},{28,28},{5,9},{1... | collective-permute-start | bytes 614408 | tf_op jit(solution)/shard_map/ppermute | solution.py:359
  8.8 1.5 %collective-permute-start.7 = (bf16[288,512]{1,0:T(8,128)(2,1)S(1)}, bf16[288,512]{1,0:T(8,128)(2,1)S(1)}, u32[]{:S(2)}, u32[]{:S(2)}) collective-permute-start(bf16[288,512]{1,0:T(8,128)(2,1)S(1)} %copy-done.5), channel_id=1, source_target_pairs={{0,2},{1,3},{2,0},{3,1},{4,6},{5,7},{6,4},{7,5},{8,10},{9,11},{10,... | collective-permute-start | bytes 884744 | tf_op jit(solution)/shard_map/ppermute | solution.py:341
  10.3 0.5 collective-permute-start.3
  10.9 0.3 own.1
  11.3 5.7 %collective-permute-done.1.first_ref = bf16[800,128]{1,0:T(8,128)(2,1)S(1)} collective-permute-done((bf16[800,128]{1,0:T(8,128)(2,1)}, bf16[800,128]{1,0:T(8,128)(2,1)S(1)}, u32[]{:S(2)}, u32[]{:S(2)}) %collective-permute-start.1) | collective-permute-done | bytes 204832 | tf_op jit(solution)/shard_map/ppermute | solution.py:341
  16.9 0.7 finish.1
  17.6 2.4 %collective-permute-start.5 = (bf16[256,128]{1,0:T(8,128)(2,1)S(1)}, bf16[256,128]{1,0:T(8,128)(2,1)S(1)}, u32[]{:S(2)}, u32[]{:S(2)}) collective-permute-start(bf16[256,128]{1,0:T(8,128)(2,1)S(1)} %get-tuple-element.51.own_ref), channel_id=1, source_target_pairs={{0,4},{4,0},{8,12},{12,8},{16,20},{20,16},{24,28},{28,24},{1,5},{5... | collective-permute-start | bytes 196616 | tf_op jit(solution)/shard_map/ppermute | solution.py:341
  20.1 0.7 collective-permute-start.6
  20.7 1.6 %collective-permute-start.4 = (bf16[256,512]{1,0:T(8,128)(2,1)S(1)}, bf16[256,512]{1,0:T(8,128)(2,1)S(1)}, u32[]{:S(2)}, u32[]{:S(2)}) collective-permute-start(bf16[256,512]{1,0:T(8,128)(2,1)S(1)} %get-tuple-element.53.side_ref), channel_id=1, source_target_pairs={{0,2},{1,3},{2,0},{3,1},{4,6},{5,7},{6,4},{7,5},{8,10},{9,11},{10,... | collective-permute-start | bytes 786440 | tf_op jit(solution)/shard_map/ppermute | solution.py:341
  22.5 0.2 broadcast_select_fusion.1
  22.6 0.2 pad_maximum_fusion.w_ref
  22.8 1.5 %collective-permute-done.3.cot_got = bf16[256,512]{1,0:T(8,128)(2,1)S(1)} collective-permute-done((bf16[256,512]{1,0:T(8,128)(2,1)S(1)}, bf16[256,512]{1,0:T(8,128)(2,1)S(1)}, u32[]{:S(2)}, u32[]{:S(2)}) %collective-permute-start.3) | collective-permute-done | bytes 262176 | tf_op jit(solution)/shard_map/ppermute | solution.py:341
  24.3 4.9 %collective-permute-done.4.side_got = bf16[256,512]{1,0:T(8,128)(2,1)S(1)} collective-permute-done((bf16[256,512]{1,0:T(8,128)(2,1)S(1)}, bf16[256,512]{1,0:T(8,128)(2,1)S(1)}, u32[]{:S(2)}, u32[]{:S(2)}) %collective-permute-start.4) | collective-permute-done | bytes 262176 | tf_op jit(solution)/shard_map/ppermute | solution.py:341
  29.2 2.9 %back.1 = (f32[256,512]{1,0:T(8,128)S(1)}, bf16[256,512]{1,0:T(8,128)(2,1)S(1)}, bf16[4,256,512]{2,1,0:T(8,128)(2,1)S(1)}) custom-call(s32[7]{0:T(128)S(1)} %stack.44.s_ref, bf16[256,512]{1,0:T(8,128)(2,1)S(1)} %bitcast.21, bf16[256,512]{1,0:T(8,128)(2,1)S(1)} %collective-permute-done.3.cot_got, bf16[256,512]{1,0:T(8,128)(2,1)S(1)} %get-tuple-element.53.side_ref, ...), custom_call_target="tpu_custom_call" | custom-call | flops 4600141312 | tf_op jit(solution)/shard_map/back/pallas_call | solution.py:20
  32.1 1.6 %collective-permute-start.9 = (bf16[256,512]{1,0:T(8,128)(2,1)S(1)}, bf16[256,512]{1,0:T(8,128)(2,1)S(1)}, u32[]{:S(2)}, u32[]{:S(2)}) collective-permute-start(bf16[256,512]{1,0:T(8,128)(2,1)S(1)} %get-tuple-element.59), channel_id=1, source_target_pairs={{0,2},{1,3},{2,0},{3,1},{4,6},{5,7},{6,4},{7,5},{8,10},{9,11},{10,... | collective-permute-start | bytes 786440 | tf_op jit(solution)/shard_map/ppermute | solution.py:341
  33.7 1.5 %first.1 = (f32[256,512]{1,0:T(8,128)S(1)}, bf16[256,512]{1,0:T(8,128)(2,1)S(1)}, bf16[256,512]{1,0:T(8,128)(2,1)S(1)}, bf16[128,512]{1,0:T(8,128)(2,1)S(1)}) custom-call(s32[7]{0:T(128)S(1)} %stack.44.s_ref, bf16[256,128]{1,0:T(8,128)(2,1)S(1)} %get-tuple-element.51.own_ref, bf16[256,128]{1,0:T(8,128)(2,1)S(1)} %collective-permute-done.5.a_ref, ...), custom_call_target="tpu_custom_call" | custom-call | flops 24202651648 | tf_op jit(solution)/shard_map/first/pallas_call | solution.py:20
  35.2 0.6 collective-permute-start.11
  35.7 0.2 collective-permute-start.12
  36.0 4.8 %collective-permute-done.9.got_ref = bf16[256,512]{1,0:T(8,128)(2,1)S(1)} collective-permute-done((bf16[256,512]{1,0:T(8,128)(2,1)S(1)}, bf16[256,512]{1,0:T(8,128)(2,1)S(1)}, u32[]{:S(2)}, u32[]{:S(2)}) %collective-permute-start.9) | collective-permute-done | bytes 262176 | tf_op jit(solution)/shard_map/ppermute | solution.py:341
  40.8 4.4 %collective-permute-done.11.refs_1_.mid_two = bf16[256,512]{1,0:T(8,128)(2,1)S(1)} collective-permute-done((bf16[256,512]{1,0:T(8,128)(2,1)S(1)}, bf16[256,512]{1,0:T(8,128)(2,1)S(1)}, u32[]{:S(2)}, u32[]{:S(2)}) %collective-permute-start.11) | collective-permute-done | bytes 262176 | tf_op jit(solution)/shard_map/ppermute | solution.py:341
  45.2 1.8 %turn.1.turned_ref = bf16[3,512,1024]{2,1,0:T(8,128)(2,1)S(1)} custom-call(s32[7]{0:T(128)S(1)} %stack.44.s_ref, bf16[4,256,512]{2,1,0:T(8,128)(2,1)S(1)} %get-tuple-element.61.refs_0_, bf16[4,256,512]{2,1,0:T(8,128)(2,1)S(1)} %collective-permute-done.10.refs_1_), custom_call_target="tpu_custom_call" | custom-call | flops 2957233664 | tf_op jit(solution)/shard_map/turn/pallas_call | solution.py:20
  47.0 2.5 %gradsecond.1 = (bf16[4,32,1152]{2,1,0:T(8,128)(2,1)S(1)}, bf16[4,32,1152]{2,1,0:T(8,128)(2,1)S(1)}, bf16[4,32,1152]{2,1,0:T(8,128)(2,1)S(1)}, bf16[4,32,1152]{2,1,0:T(8,128)(2,1)S(1)}) custom-call(s32[7]{0:T(128)S(1)} %stack.44.s_ref, bf16[3,512,1024]{2,1,0:T(8,128)(2,1)S(1)} %turn.1.turned_ref, bf16[256,512]{1,0:T(8,128)(2,1)S(1)} %get-tuple-element.58.refs_0_.mid_one, ...), custom_call_target="tpu_custom_call" | custom-call | flops 4107269120 | tf_op jit(solution)/shard_map/gradsecond/pallas_call | solution.py:20
  49.5 0.8 dpre.1.refs_0_
  50.3 0.6 collective-permute-start.14
  50.9 2.3 %collective-permute-start.18 = (bf16[4,32,1152]{2,1,0:T(8,128)(2,1)S(1)}, bf16[4,32,1152]{2,1,0:T(8,128)(2,1)S(1)}, u32[]{:S(2)}, u32[]{:S(2)}) collective-permute-start(bf16[4,32,1152]{2,1,0:T(8,128)(2,1)S(1)} %get-tuple-element.73), channel_id=1, source_target_pairs={{0,4},{4,0},{8,12},{12,8},{16,20},{20,16},{24,28},{28,24},{1,5},{5... | collective-permute-start | bytes 884744 | tf_op jit(solution)/shard_map/ppermute | solution.py:341
  53.2 1.6 %collective-permute-start.19 = (bf16[4,32,1152]{2,1,0:T(8,128)(2,1)S(1)}, bf16[4,32,1152]{2,1,0:T(8,128)(2,1)S(1)}, u32[]{:S(2)}, u32[]{:S(2)}) collective-permute-start(bf16[4,32,1152]{2,1,0:T(8,128)(2,1)S(1)} %get-tuple-element.75), channel_id=1, source_target_pairs={{0,8},{4,12},{8,0},{12,4},{16,24},{20,28},{24,16},{28,20},{1,9},{5... | collective-permute-start | bytes 884744 | tf_op jit(solution)/shard_map/ppermute | solution.py:341
  54.8 1.5 %gradfirst.1 = (bf16[8,64,288]{2,1,0:T(8,128)(2,1)S(1)}, bf16[8,64,288]{2,1,0:T(8,128)(2,1)S(1)}) custom-call(s32[7]{0:T(128)S(1)} %stack.44.s_ref, bf16[768,256]{1,0:T(8,128)(2,1)S(1)} %dpre.1.refs_0_, bf16[768,256]{1,0:T(8,128)(2,1)S(1)} %collective-permute-done.14.refs_1_), custom_call_target="tpu_custom_call" | custom-call | flops 2464361472 | tf_op jit(solution)/shard_map/gradfirst/pallas_call | solution.py:20
  56.2 1.6 %collective-permute-start.15 = (bf16[8,64,288]{2,1,0:T(8,128)(2,1)S(1)}, bf16[8,64,288]{2,1,0:T(8,128)(2,1)S(1)}, u32[]{:S(2)}, u32[]{:S(2)}) collective-permute-start(bf16[8,64,288]{2,1,0:T(8,128)(2,1)S(1)} %get-tuple-element.66), channel_id=1, source_target_pairs={{0,2},{1,3},{2,0},{3,1},{4,6},{5,7},{6,4},{7,5},{8,10},{9,11},{10,... | collective-permute-start | bytes 884744 | tf_op jit(solution)/shard_map/ppermute | solution.py:341
  57.8 2.6 %collective-permute-done.18.refs_1_ = bf16[4,32,1152]{2,1,0:T(8,128)(2,1)S(1)} collective-permute-done((bf16[4,32,1152]{2,1,0:T(8,128)(2,1)S(1)}, bf16[4,32,1152]{2,1,0:T(8,128)(2,1)S(1)}, u32[]{:S(2)}, u32[]{:S(2)}) %collective-permute-start.18) | collective-permute-done | bytes 294944 | tf_op jit(solution)/shard_map/ppermute | solution.py:341
  60.4 1.5 %collective-permute-done.19.refs_3_ = bf16[4,32,1152]{2,1,0:T(8,128)(2,1)S(1)} collective-permute-done((bf16[4,32,1152]{2,1,0:T(8,128)(2,1)S(1)}, bf16[4,32,1152]{2,1,0:T(8,128)(2,1)S(1)}, u32[]{:S(2)}, u32[]{:S(2)}) %collective-permute-start.19) | collective-permute-done | bytes 294944 | tf_op jit(solution)/shard_map/ppermute | solution.py:341
  62.0 1.6 %collective-permute-start.23 = (bf16[2,32,1152]{2,1,0:T(8,128)(2,1)S(1)}, bf16[2,32,1152]{2,1,0:T(8,128)(2,1)S(1)}, u32[]{:S(2)}, u32[]{:S(2)}) collective-permute-start(bf16[2,32,1152]{2,1,0:T(8,128)(2,1)S(1)} %get-tuple-element.84), channel_id=1, source_target_pairs={{0,8},{4,12},{8,0},{12,4},{16,24},{20,28},{24,16},{28,20},{1,9},{5... | collective-permute-start | bytes 442376 | tf_op jit(solution)/shard_map/ppermute | solution.py:341
  63.7 0.4 collective-permute-start.24
  64.0 1.5 %collective-permute-start.16 = (bf16[256,512]{1,0:T(8,128)(2,1)S(1)}, bf16[256,512]{1,0:T(8,128)(2,1)S(1)}, u32[]{:S(2)}, u32[]{:S(2)}) collective-permute-start(bf16[256,512]{1,0:T(8,128)(2,1)S(1)} %get-tuple-element.69.edge_one), channel_id=1, source_target_pairs={{0,2},{1,3},{2,0},{3,1},{4,6},{5,7},{6,4},{7,5},{8,10},{9,11},{10,... | collective-permute-start | bytes 786440 | tf_op jit(solution)/shard_map/ppermute | solution.py:341
  65.6 2.6 %collective-permute-done.15.refs_1_ = bf16[8,64,288]{2,1,0:T(8,128)(2,1)S(1)} collective-permute-done((bf16[8,64,288]{2,1,0:T(8,128)(2,1)S(1)}, bf16[8,64,288]{2,1,0:T(8,128)(2,1)S(1)}, u32[]{:S(2)}, u32[]{:S(2)}) %collective-permute-start.15) | collective-permute-done | bytes 294944 | tf_op jit(solution)/shard_map/ppermute | solution.py:341
  68.4 1.1 %collective-permute-done.24.got_two = bf16[2,32,1152]{2,1,0:T(8,128)(2,1)S(1)} collective-permute-done((bf16[2,32,1152]{2,1,0:T(8,128)(2,1)S(1)}, bf16[2,32,1152]{2,1,0:T(8,128)(2,1)S(1)}, u32[]{:S(2)}, u32[]{:S(2)}) %collective-permute-start.24) | collective-permute-done | bytes 147488 | tf_op jit(solution)/shard_map/ppermute | solution.py:341
  69.6 2.1 %collective-permute-start.25 = (bf16[1,64,1152]{2,1,0:T(8,128)(2,1)S(1)}, bf16[1,64,1152]{2,1,0:T(8,128)(2,1)S(1)}, u32[]{:S(2)}, u32[]{:S(2)}) collective-permute-start(bf16[1,64,1152]{2,1,0:T(8,128)(2,1)S(1)} %get-tuple-element.88), channel_id=1, source_target_pairs={{0,16},{4,20},{8,24},{12,28},{16,0},{20,4},{24,8},{28,12},{1,17},{... | collective-permute-start | bytes 442376 | tf_op jit(solution)/shard_map/ppermute | solution.py:341
  71.6 2.4 %collective-permute-done.20.refs_1_ = bf16[4,64,288]{2,1,0:T(8,128)(2,1)S(1)} collective-permute-done((bf16[4,64,288]{2,1,0:T(8,128)(2,1)S(1)}, bf16[4,64,288]{2,1,0:T(8,128)(2,1)S(1)}, u32[]{:S(2)}, u32[]{:S(2)}) %collective-permute-start.20) | collective-permute-done | bytes 147488 | tf_op jit(solution)/shard_map/ppermute | solution.py:341
  74.1 0.5 collective-permute-start.21
  74.6 2.7 %second.1 = (f32[256,512]{1,0:T(8,128)S(1)}, bf16[256,512]{1,0:T(8,128)(2,1)S(1)}) custom-call(s32[7]{0:T(128)S(1)} %stack.44.s_ref, bf16[256,512]{1,0:T(8,128)(2,1)S(1)} %get-tuple-element.58.refs_0_.mid_one, bf16[256,512]{1,0:T(8,128)(2,1)S(1)} %collective-permute-done.11.refs_1_.mid_two, bf16[256,512]{1,0:T(8,128)(2,1)S(1)} %get-tuple-element.69.edge_one, ...), custom_call_target="tpu_custom_call" | custom-call | flops 4435850752 | tf_op jit(solution)/shard_map/second/pallas_call | solution.py:20
  77.3 1.6 %collective-permute-start.17 = (bf16[256,512]{1,0:T(8,128)(2,1)S(1)}, bf16[256,512]{1,0:T(8,128)(2,1)S(1)}, u32[]{:S(2)}, u32[]{:S(2)}) collective-permute-start(bf16[256,512]{1,0:T(8,128)(2,1)S(1)} %get-tuple-element.71), channel_id=1, source_target_pairs={{0,2},{1,3},{2,0},{3,1},{4,6},{5,7},{6,4},{7,5},{8,10},{9,11},{10,... | collective-permute-start | bytes 786440 | tf_op jit(solution)/shard_map/ppermute | solution.py:341
  78.9 3.4 %collective-permute-start.22 = (bf16[1,64,288]{2,1,0:T(8,128)(2,1)S(1)}, bf16[1,64,288]{2,1,0:T(8,128)(2,1)S(1)}, u32[]{:S(2)}, u32[]{:S(2)}) collective-permute-start(bf16[1,64,288]{2,1,0:T(8,128)(2,1)S(1)} %get-tuple-element.82), channel_id=1, source_target_pairs={{0,16},{4,20},{8,24},{12,28},{16,0},{20,4},{24,8},{28,12},{1,17},{... | collective-permute-start | bytes 110600 | tf_op jit(solution)/shard_map/ppermute | solution.py:341
  82.3 0.7 last.3
  83.1 1.3 %collective-permute-done.22.got_ref = bf16[1,64,288]{2,1,0:T(8,128)(2,1)S(1)} collective-permute-done((bf16[1,64,288]{2,1,0:T(8,128)(2,1)S(1)}, bf16[1,64,288]{2,1,0:T(8,128)(2,1)S(1)}, u32[]{:S(2)}, u32[]{:S(2)}) %collective-permute-start.22) | collective-permute-done | bytes 36896 | tf_op jit(solution)/shard_map/ppermute | solution.py:341
  84.4 0.7 last.2
  85.0 0.8 add_convert_fusion
  (38 shorter events, 0.8 us)
Async XLA Ops:
  0.6 21.8 %collective-permute-start = (bf16[1152,512]{1,0:T(8,128)(2,1)}, bf16[1152,512]{1,0:T(8,128)(2,1)S(1)}, u32[]{:S(2)}, u32[]{:S(2)}) collective-permute-start(bf16[1152,512]{1,0:T(8,128)(2,1)} %param.17), channel_id=1, source_target_pairs={{0,1},{1,0},{2,3},{3,2},{4,5},{5,4},{6,7},{7,6},{8,9},{9,8},{10,11... | collective-permute-start | bytes 3538952 | tf_op jit(solution)/shard_map/ppermute | solution.py:341
  1.8 7.0 %copy-start.5 = (bf16[288,512]{1,0:T(8,128)(2,1)S(1)}, bf16[288,512]{1,0:T(8,128)(2,1)}, u32[]{:S(2)}) copy-start(bf16[288,512]{1,0:T(8,128)(2,1)} %param.16) | copy-start | bytes 884740
  1.8 8.5 %copy-start.1 = (bf16[1,2,128,512]{3,2,1,0:T(8,128)(2,1)S(1)}, bf16[1,2,128,512]{3,2,1,0:T(8,128)(2,1)}, u32[]{:S(2)}) copy-start(bf16[1,2,128,512]{3,2,1,0:T(8,128)(2,1)} %param.15) | copy-start | bytes 786436
  1.8 9.1 %copy-start = (f32[1,1024,128]{2,1,0:T(8,128)S(1)}, f32[1,1024,128]{2,1,0:T(8,128)}, u32[]{:S(2)}) copy-start(f32[1,1024,128]{2,1,0:T(8,128)} %param.9) | copy-start | bytes 1572868
  1.8 9.1 %copy-start.2 = (f32[1,1024]{1,0:T(1,128)S(1)}, f32[1,1024]{1,0:T(1,128)}, u32[]{:S(2)}) copy-start(f32[1,1024]{1,0:T(1,128)} %refs_1_.1) | copy-start | bytes 12292
  1.8 9.1 %copy-start.3 = (f32[1,1024]{1,0:T(1,128)S(1)}, f32[1,1024]{1,0:T(1,128)}, u32[]{:S(2)}) copy-start(f32[1,1024]{1,0:T(1,128)} %refs_2_.1) | copy-start | bytes 12292
  4.7 12.3 %collective-permute-start.1 = (bf16[800,128]{1,0:T(8,128)(2,1)}, bf16[800,128]{1,0:T(8,128)(2,1)S(1)}, u32[]{:S(2)}, u32[]{:S(2)}) collective-permute-start(bf16[800,128]{1,0:T(8,128)(2,1)} %get-tuple-element.49), channel_id=1, source_target_pairs={{0,4},{4,0},{8,12},{12,8},{16,20},{20,16},{24,28},{28,24},{1,5},{5... | collective-permute-start | bytes 614408 | tf_op jit(solution)/shard_map/ppermute | solution.py:341
  7.2 9.7 %collective-permute-start.2 = (bf16[800,128]{1,0:T(8,128)(2,1)}, bf16[800,128]{1,0:T(8,128)(2,1)S(1)}, u32[]{:S(2)}, u32[]{:S(2)}) collective-permute-start(bf16[800,128]{1,0:T(8,128)(2,1)} %get-tuple-element.50), channel_id=1, source_target_pairs={{4,8},{12,16},{20,24},{8,4},{16,12},{24,20},{0,0},{28,28},{5,9},{1... | collective-permute-start | bytes 614408 | tf_op jit(solution)/shard_map/ppermute | solution.py:359
  8.8 11.9 %collective-permute-start.7 = (bf16[288,512]{1,0:T(8,128)(2,1)S(1)}, bf16[288,512]{1,0:T(8,128)(2,1)S(1)}, u32[]{:S(2)}, u32[]{:S(2)}) collective-permute-start(bf16[288,512]{1,0:T(8,128)(2,1)S(1)} %copy-done.5), channel_id=1, source_target_pairs={{0,2},{1,3},{2,0},{3,1},{4,6},{5,7},{6,4},{7,5},{8,10},{9,11},{10,... | collective-permute-start | bytes 884744 | tf_op jit(solution)/shard_map/ppermute | solution.py:341
  10.3 13.9 %collective-permute-start.3 = (bf16[256,512]{1,0:T(8,128)(2,1)S(1)}, bf16[256,512]{1,0:T(8,128)(2,1)S(1)}, u32[]{:S(2)}, u32[]{:S(2)}) collective-permute-start(bf16[256,512]{1,0:T(8,128)(2,1)S(1)} %bitcast.20), channel_id=1, source_target_pairs={{0,2},{1,3},{2,0},{3,1},{4,6},{5,7},{6,4},{7,5},{8,10},{9,11},{10,... | collective-permute-start | bytes 786440 | tf_op jit(solution)/shard_map/ppermute | solution.py:341
  17.6 4.9 %copy-start.4 = (bf16[1152,512]{1,0:T(8,128)(2,1)S(1)}, bf16[1152,512]{1,0:T(8,128)(2,1)}, u32[]{:S(2)}) copy-start(bf16[1152,512]{1,0:T(8,128)(2,1)} %param.17) | copy-start | bytes 3538948
  17.6 16.0 %collective-permute-start.5 = (bf16[256,128]{1,0:T(8,128)(2,1)S(1)}, bf16[256,128]{1,0:T(8,128)(2,1)S(1)}, u32[]{:S(2)}, u32[]{:S(2)}) collective-permute-start(bf16[256,128]{1,0:T(8,128)(2,1)S(1)} %get-tuple-element.51.own_ref), channel_id=1, source_target_pairs={{0,4},{4,0},{8,12},{12,8},{16,20},{20,16},{24,28},{28,24},{1,5},{5... | collective-permute-start | bytes 196616 | tf_op jit(solution)/shard_map/ppermute | solution.py:341
  20.1 13.6 %collective-permute-start.6 = (bf16[256,128]{1,0:T(8,128)(2,1)S(1)}, bf16[256,128]{1,0:T(8,128)(2,1)S(1)}, u32[]{:S(2)}, u32[]{:S(2)}) collective-permute-start(bf16[256,128]{1,0:T(8,128)(2,1)S(1)} %get-tuple-element.51.own_ref), channel_id=1, source_target_pairs={{4,8},{12,16},{20,24},{8,4},{16,12},{24,20},{0,0},{28,28},{5,9},{1... | collective-permute-start | bytes 196616 | tf_op jit(solution)/shard_map/ppermute | solution.py:359
  20.7 8.4 %collective-permute-start.4 = (bf16[256,512]{1,0:T(8,128)(2,1)S(1)}, bf16[256,512]{1,0:T(8,128)(2,1)S(1)}, u32[]{:S(2)}, u32[]{:S(2)}) collective-permute-start(bf16[256,512]{1,0:T(8,128)(2,1)S(1)} %get-tuple-element.53.side_ref), channel_id=1, source_target_pairs={{0,2},{1,3},{2,0},{3,1},{4,6},{5,7},{6,4},{7,5},{8,10},{9,11},{10,... | collective-permute-start | bytes 786440 | tf_op jit(solution)/shard_map/ppermute | solution.py:341
  22.4 11.3 %collective-permute-start.8 = (bf16[2,288,512]{2,1,0:T(8,128)(2,1)S(1)}, bf16[2,288,512]{2,1,0:T(8,128)(2,1)S(1)}, u32[]{:S(2)}, u32[]{:S(2)}) collective-permute-start(bf16[2,288,512]{2,1,0:T(8,128)(2,1)S(1)} %pad_maximum_fusion.1.w_near), channel_id=1, source_target_pairs={{0,1},{1,0},{2,3},{3,2},{4,5},{5,4},{6,7},{7,6},{8,9},{9,8},{10,11... | collective-permute-start | bytes 1769480 | tf_op jit(solution)/shard_map/ppermute | solution.py:341
  32.1 8.7 %collective-permute-start.9 = (bf16[256,512]{1,0:T(8,128)(2,1)S(1)}, bf16[256,512]{1,0:T(8,128)(2,1)S(1)}, u32[]{:S(2)}, u32[]{:S(2)}) collective-permute-start(bf16[256,512]{1,0:T(8,128)(2,1)S(1)} %get-tuple-element.59), channel_id=1, source_target_pairs={{0,2},{1,3},{2,0},{3,1},{4,6},{5,7},{6,4},{7,5},{8,10},{9,11},{10,... | collective-permute-start | bytes 786440 | tf_op jit(solution)/shard_map/ppermute | solution.py:341
  33.6 11.6 %collective-permute-start.10 = (bf16[4,256,512]{2,1,0:T(8,128)(2,1)S(1)}, bf16[4,256,512]{2,1,0:T(8,128)(2,1)S(1)}, u32[]{:S(2)}, u32[]{:S(2)}) collective-permute-start(bf16[4,256,512]{2,1,0:T(8,128)(2,1)S(1)} %get-tuple-element.61.refs_0_), channel_id=1, source_target_pairs={{0,1},{1,0},{2,3},{3,2},{4,5},{5,4},{6,7},{7,6},{8,9},{9,8},{10,11... | collective-permute-start | bytes 3145736 | tf_op jit(solution)/shard_map/ppermute | solution.py:341
  35.2 10.0 %collective-permute-start.11 = (bf16[256,512]{1,0:T(8,128)(2,1)S(1)}, bf16[256,512]{1,0:T(8,128)(2,1)S(1)}, u32[]{:S(2)}, u32[]{:S(2)}) collective-permute-start(bf16[256,512]{1,0:T(8,128)(2,1)S(1)} %get-tuple-element.58.refs_0_.mid_one), channel_id=1, source_target_pairs={{0,2},{1,3},{2,0},{3,1},{4,6},{5,7},{6,4},{7,5},{8,10},{9,11},{10,... | collective-permute-start | bytes 786440 | tf_op jit(solution)/shard_map/ppermute | solution.py:341
  35.7 11.3 %collective-permute-start.12 = (bf16[256,512]{1,0:T(8,128)(2,1)S(1)}, bf16[256,512]{1,0:T(8,128)(2,1)S(1)}, u32[]{:S(2)}, u32[]{:S(2)}) collective-permute-start(bf16[256,512]{1,0:T(8,128)(2,1)S(1)} %get-tuple-element.58.refs_0_.mid_one), channel_id=1, source_target_pairs={{0,1},{1,0},{2,3},{3,2},{4,5},{5,4},{6,7},{7,6},{8,9},{9,8},{10,11... | collective-permute-start | bytes 786440 | tf_op jit(solution)/shard_map/ppermute | solution.py:341
  45.2 1.8 %collective-permute-start.13 = (bf16[256,512]{1,0:T(8,128)(2,1)S(1)}, bf16[256,512]{1,0:T(8,128)(2,1)S(1)}, u32[]{:S(2)}, u32[]{:S(2)}) collective-permute-start(bf16[256,512]{1,0:T(8,128)(2,1)S(1)} %collective-permute-done.11.refs_1_.mid_two), channel_id=1, source_target_pairs={{0,1},{1,0},{2,3},{3,2},{4,5},{5,4},{6,7},{7,6},{8,9},{9,8},{10,11... | collective-permute-start | bytes 786440 | tf_op jit(solution)/shard_map/ppermute | solution.py:341
  50.3 4.4 %collective-permute-start.14 = (bf16[768,256]{1,0:T(8,128)(2,1)S(1)}, bf16[768,256]{1,0:T(8,128)(2,1)S(1)}, u32[]{:S(2)}, u32[]{:S(2)}) collective-permute-start(bf16[768,256]{1,0:T(8,128)(2,1)S(1)} %dpre.1.refs_0_), channel_id=1, source_target_pairs={{0,1},{1,0},{2,3},{3,2},{4,5},{5,4},{6,7},{7,6},{8,9},{9,8},{10,11... | collective-permute-start | bytes 1179656 | tf_op jit(solution)/shard_map/ppermute | solution.py:341
  50.9 9.5 %collective-permute-start.18 = (bf16[4,32,1152]{2,1,0:T(8,128)(2,1)S(1)}, bf16[4,32,1152]{2,1,0:T(8,128)(2,1)S(1)}, u32[]{:S(2)}, u32[]{:S(2)}) collective-permute-start(bf16[4,32,1152]{2,1,0:T(8,128)(2,1)S(1)} %get-tuple-element.73), channel_id=1, source_target_pairs={{0,4},{4,0},{8,12},{12,8},{16,20},{20,16},{24,28},{28,24},{1,5},{5... | collective-permute-start | bytes 884744 | tf_op jit(solution)/shard_map/ppermute | solution.py:341
  53.2 8.7 %collective-permute-start.19 = (bf16[4,32,1152]{2,1,0:T(8,128)(2,1)S(1)}, bf16[4,32,1152]{2,1,0:T(8,128)(2,1)S(1)}, u32[]{:S(2)}, u32[]{:S(2)}) collective-permute-start(bf16[4,32,1152]{2,1,0:T(8,128)(2,1)S(1)} %get-tuple-element.75), channel_id=1, source_target_pairs={{0,8},{4,12},{8,0},{12,4},{16,24},{20,28},{24,16},{28,20},{1,9},{5... | collective-permute-start | bytes 884744 | tf_op jit(solution)/shard_map/ppermute | solution.py:341
  56.2 12.0 %collective-permute-start.15 = (bf16[8,64,288]{2,1,0:T(8,128)(2,1)S(1)}, bf16[8,64,288]{2,1,0:T(8,128)(2,1)S(1)}, u32[]{:S(2)}, u32[]{:S(2)}) collective-permute-start(bf16[8,64,288]{2,1,0:T(8,128)(2,1)S(1)} %get-tuple-element.66), channel_id=1, source_target_pairs={{0,2},{1,3},{2,0},{3,1},{4,6},{5,7},{6,4},{7,5},{8,10},{9,11},{10,... | collective-permute-start | bytes 884744 | tf_op jit(solution)/shard_map/ppermute | solution.py:341
  62.0 6.3 %collective-permute-start.23 = (bf16[2,32,1152]{2,1,0:T(8,128)(2,1)S(1)}, bf16[2,32,1152]{2,1,0:T(8,128)(2,1)S(1)}, u32[]{:S(2)}, u32[]{:S(2)}) collective-permute-start(bf16[2,32,1152]{2,1,0:T(8,128)(2,1)S(1)} %get-tuple-element.84), channel_id=1, source_target_pairs={{0,8},{4,12},{8,0},{12,4},{16,24},{20,28},{24,16},{28,20},{1,9},{5... | collective-permute-start | bytes 442376 | tf_op jit(solution)/shard_map/ppermute | solution.py:341
  63.7 5.8 %collective-permute-start.24 = (bf16[2,32,1152]{2,1,0:T(8,128)(2,1)S(1)}, bf16[2,32,1152]{2,1,0:T(8,128)(2,1)S(1)}, u32[]{:S(2)}, u32[]{:S(2)}) collective-permute-start(bf16[2,32,1152]{2,1,0:T(8,128)(2,1)S(1)} %get-tuple-element.86), channel_id=1, source_target_pairs={{0,4},{4,0},{8,12},{12,8},{16,20},{20,16},{24,28},{28,24},{1,5},{5... | collective-permute-start | bytes 442376 | tf_op jit(solution)/shard_map/ppermute | solution.py:341
  64.0 10.5 %collective-permute-start.16 = (bf16[256,512]{1,0:T(8,128)(2,1)S(1)}, bf16[256,512]{1,0:T(8,128)(2,1)S(1)}, u32[]{:S(2)}, u32[]{:S(2)}) collective-permute-start(bf16[256,512]{1,0:T(8,128)(2,1)S(1)} %get-tuple-element.69.edge_one), channel_id=1, source_target_pairs={{0,2},{1,3},{2,0},{3,1},{4,6},{5,7},{6,4},{7,5},{8,10},{9,11},{10,... | collective-permute-start | bytes 786440 | tf_op jit(solution)/shard_map/ppermute | solution.py:341
  68.3 5.7 %collective-permute-start.20 = (bf16[4,64,288]{2,1,0:T(8,128)(2,1)S(1)}, bf16[4,64,288]{2,1,0:T(8,128)(2,1)S(1)}, u32[]{:S(2)}, u32[]{:S(2)}) collective-permute-start(bf16[4,64,288]{2,1,0:T(8,128)(2,1)S(1)} %get-tuple-element.78), channel_id=1, source_target_pairs={{0,4},{4,0},{8,12},{12,8},{16,20},{20,16},{24,28},{28,24},{1,5},{5... | collective-permute-start | bytes 442376 | tf_op jit(solution)/shard_map/ppermute | solution.py:341
  69.6 12.8 %collective-permute-start.25 = (bf16[1,64,1152]{2,1,0:T(8,128)(2,1)S(1)}, bf16[1,64,1152]{2,1,0:T(8,128)(2,1)S(1)}, u32[]{:S(2)}, u32[]{:S(2)}) collective-permute-start(bf16[1,64,1152]{2,1,0:T(8,128)(2,1)S(1)} %get-tuple-element.88), channel_id=1, source_target_pairs={{0,16},{4,20},{8,24},{12,28},{16,0},{20,4},{24,8},{28,12},{1,17},{... | collective-permute-start | bytes 442376 | tf_op jit(solution)/shard_map/ppermute | solution.py:341
  74.1 4.8 %collective-permute-start.21 = (bf16[2,64,288]{2,1,0:T(8,128)(2,1)S(1)}, bf16[2,64,288]{2,1,0:T(8,128)(2,1)S(1)}, u32[]{:S(2)}, u32[]{:S(2)}) collective-permute-start(bf16[2,64,288]{2,1,0:T(8,128)(2,1)S(1)} %get-tuple-element.80), channel_id=1, source_target_pairs={{0,8},{4,12},{8,0},{12,4},{16,24},{20,28},{24,16},{28,20},{1,9},{5... | collective-permute-start | bytes 221192 | tf_op jit(solution)/shard_map/ppermute | solution.py:341
  77.3 7.7 %collective-permute-start.17 = (bf16[256,512]{1,0:T(8,128)(2,1)S(1)}, bf16[256,512]{1,0:T(8,128)(2,1)S(1)}, u32[]{:S(2)}, u32[]{:S(2)}) collective-permute-start(bf16[256,512]{1,0:T(8,128)(2,1)S(1)} %get-tuple-element.71), channel_id=1, source_target_pairs={{0,2},{1,3},{2,0},{3,1},{4,6},{5,7},{6,4},{7,5},{8,10},{9,11},{10,... | collective-permute-start | bytes 786440 | tf_op jit(solution)/shard_map/ppermute | solution.py:341
  78.9 5.4 %collective-permute-start.22 = (bf16[1,64,288]{2,1,0:T(8,128)(2,1)S(1)}, bf16[1,64,288]{2,1,0:T(8,128)(2,1)S(1)}, u32[]{:S(2)}, u32[]{:S(2)}) collective-permute-start(bf16[1,64,288]{2,1,0:T(8,128)(2,1)S(1)} %get-tuple-element.82), channel_id=1, source_target_pairs={{0,16},{4,20},{8,24},{12,28},{16,0},{20,4},{24,8},{28,12},{1,17},{... | collective-permute-start | bytes 110600 | tf_op jit(solution)/shard_map/ppermute | solution.py:341
